TPU v7x, 32 devices: a whole 2x2x4 slice. The times are simulated.
32 devices in a mesh: samp: 16 (over z, x, core), blk: 2 (over y).
Axes of the slice: x: 2, y: 2, z: 4, core: 2. Of those that a mesh axis runs over, the one named last changes fastest.
Arguments:
- genotypes: bfloat16 [16384, 1000], P('samp', 'blk'), may hold values from 0 to 2, as said below
- traits: float32 [16384, 8], P('samp'), may hold values from -3000 to 3000
- observed: int32 [16384, 8], P('samp'), may hold values from 0 to 1, as said below
- fold_index: int32 [16384], P('samp'), may hold values from 0 to 4, never falling along the last dimension, each value on 1 to 6553 neighbouring positions
Outputs:
- stack_gram: float32 [8, 5, 10, 10], P('blk')
- stack_cross: float32 [8, 5, 10], P('blk')
Inputs may be any that keep to these rules, and one draw needn't show every extreme that they name: `genotypes`: genotype dosages, whole numbers. `observed`: each trait is measured in at least one sample.
All inputs are finite; a program needn't handle non-finite values.
Results may differ from a plain program's by a relative error of at most 0.0003.
Values sent between devices are 32-bit elements; how exact they have to be, the bound alone decides.
No kernel may reach another device: no remote copies, remote signals or barrier semaphores. Data moves between devices by JAX's collectives and lax.ppermute only.
A program may use at most 64 MiB of HBM per device.

v0:
```python
import jax
import jax.numpy as jnp
from jax import lax
from jax.sharding import PartitionSpec as P

BLOCK = 500
TRAITS = 8
FOLDS = 5


HERITABILITY = (0.01, 0.25, 0.5, 0.75, 0.99)
PRECISE = lax.Precision.HIGHEST


def solve_one(lower_factor, right_side):
    return jax.scipy.linalg.cho_solve((lower_factor, True), right_side)


def body(genotypes, traits, observed, fold_index):
    local_rows, local_cols = genotypes.shape
    local_blocks = local_cols // BLOCK
    sample_devices = lax.axis_size("samp")
    block_devices = lax.axis_size("blk")
    samples = local_rows * sample_devices
    markers = local_cols * block_devices
    penalty_count = len(HERITABILITY)
    present = observed.astype(jnp.float32)
    masked = present * traits
    dosage_bf = genotypes.reshape(local_rows, local_blocks, BLOCK)
    dosage = dosage_bf.astype(jnp.float32)
    gram_local = jnp.einsum(
        "sbi,sbj->bij", dosage_bf, dosage_bf, preferred_element_type=jnp.float32
    )
    sums_local = jnp.sum(dosage, 0)
    trait_local = jnp.einsum("sbj,sp->bjp", dosage, masked, precision=PRECISE)
    present_local = jnp.einsum("sbj,sp->bjp", dosage, present, precision=PRECISE)
    counts_local = jnp.sum(present, 0)
    first_local = jnp.sum(masked, 0)
    second_local = jnp.sum(masked * traits, 0)
    gram_total, column_sums, dosage_trait, dosage_present, counts, trait_sums, trait_squares = (
        lax.psum(
            (
                gram_local,
                sums_local,
                trait_local,
                present_local,
                counts_local,
                first_local,
                second_local,
            ),
            "samp",
        )
    )
    mean_trait = trait_sums / counts
    trait_scale = jnp.sqrt(trait_squares / counts - mean_trait * mean_trait + 1e-05)
    scaled = present * (traits - mean_trait) / trait_scale
    mean_dosage = column_sums / samples
    dosage_scale = jnp.sqrt(
        jnp.diagonal(gram_total, axis1=1, axis2=2) / samples - mean_dosage * mean_dosage + 1e-05
    )
    covariance = (gram_total - column_sums[:, :, None] * column_sums[:, None, :] / samples) / (
        dosage_scale[:, :, None] * dosage_scale[:, None, :]
    )
    right_side = (
        (dosage_trait - dosage_present * mean_trait) / trait_scale / dosage_scale[:, :, None]
    )
    identity = jnp.eye(BLOCK, dtype=jnp.float32)
    fit_count = local_blocks * penalty_count
    position = lax.axis_index("samp")
    assigned = jnp.minimum(
        (position * fit_count + sample_devices - 1) // sample_devices, fit_count - 1
    )
    owning = assigned * sample_devices // fit_count == position
    fit_block = assigned // penalty_count
    fit_penalty = assigned % penalty_count
    penalty_table = jnp.array(
        [markers * (1.0 - fraction) / fraction for fraction in HERITABILITY], dtype=jnp.float32
    )
    penalty = jnp.sum(jnp.where(jnp.arange(penalty_count) == fit_penalty, penalty_table, 0.0))
    chosen_cov = lax.dynamic_index_in_dim(covariance, fit_block, 0, keepdims=False)
    chosen_side = lax.dynamic_index_in_dim(right_side, fit_block, 0, keepdims=False)
    lower_factor = jnp.linalg.cholesky(chosen_cov + penalty * identity)
    solution = solve_one(lower_factor, chosen_side)
    selector = jnp.logical_and(jnp.arange(fit_count) == assigned, owning).astype(jnp.float32)
    contribution = selector[:, None, None] * solution[None]
    coefficients = lax.psum(contribution, "samp").reshape(
        local_blocks, penalty_count, BLOCK, TRAITS
    )
    centred = (dosage - mean_dosage) / dosage_scale
    predicted = jnp.einsum("sbj,brjp->pbrs", centred, coefficients, precision=PRECISE)
    energy = jnp.einsum(
        "brjp,bjk,brkp->pbr", coefficients, covariance, coefficients, precision=PRECISE
    )
    standard = predicted / jnp.sqrt(energy / samples + 1e-06)[:, :, :, None]
    regrouped = lax.all_to_all(standard, "blk", split_axis=0, concat_axis=1, tiled=True)
    trait_share = TRAITS // block_devices
    stacked = regrouped.reshape(trait_share, -1, local_rows)
    first_trait = lax.axis_index("blk") * trait_share
    scaled_share = lax.dynamic_slice_in_dim(scaled, first_trait, trait_share, 1)
    present_share = lax.dynamic_slice_in_dim(present, first_trait, trait_share, 1)
    fold_hits = (fold_index[None, :] == jnp.arange(FOLDS, dtype=jnp.int32)[:, None]).astype(
        jnp.float32
    )
    weighting = fold_hits[:, None, :] * present_share.T[None]
    weighted = weighting[:, :, None, :] * stacked[None]
    gram_part = jnp.einsum("kpls,pms->pklm", weighted, stacked, precision=PRECISE)
    cross_part = jnp.einsum("kpls,sp->pkl", weighted, scaled_share, precision=PRECISE)
    gram_sum, cross_sum = lax.psum((gram_part, cross_part), "samp")
    factor = FOLDS / samples
    return (gram_sum * factor, cross_sum * factor)


def solution(mesh):
    in_specs = (P("samp", "blk"), P("samp", None), P("samp", None), P("samp"))
    out_specs = (P("blk", None, None, None), P("blk", None, None))
    return jax.shard_map(body, mesh=mesh, in_specs=in_specs, out_specs=out_specs, check_vma=False)
```

profile of v0, /device:TPU:0, one launch (start us, length us, event | category | flops | bytes accessed | tf_op | source)
XLA Modules:
  0.0 444.1 jit_solution(3742338975323997107)
XLA Ops:
  7.2 3.3 convolution_bitcast_fusion
  14.5 64.0 %all-reduce.4 = (f32[1,500]{1,0:T(1,128)S(1)}, f32[1,500,8]{1,2,0:T(8,128)S(1)}, f32[1,500,8]{1,2,0:T(8,128)}, f32[8]{0:T(128)S(1)}, f32[8]{0:T(128)S(1)}, /*index=5*/f32[8]{0:T(128)S(1)}) all-reduce(f32[1,500]{1,0:T(1,128)S(1)} %bitcast.155, ...), channel_id=1, replica_groups=mesh['samp'=16,'blk'=2] {'samp'}, use_global_device_ids=true, to_apply=%region_2.0 | all-reduce | flops 8524 | bytes 68192 | tf_op jit(solution)/shard_map/psum | solution.py:41
  81.0 25.8 %all-reduce.8.cloned.1.call-done = f32[1,500,500]{2,1,0:T(8,128)} async-done(((f32[1,500,500]{2,1,0:T(8,128)}), f32[1,500,500]{2,1,0:T(8,128)}) %all-reduce.8.cloned.1.call-update) | async-done | bytes 1000016 | tf_op jit(solution)/shard_map/psum | solution.py:41
  106.8 10.1 %gather_fusion = f32[500]{0:T(512)S(1)} fusion(f32[500,500]{1,0:T(8,128)} %bitcast.142, s32[500]{0:T(512)S(1)} %bitcast.141), kind=kCustom, calls=%fused_computation | custom fusion | bytes 8000 | tf_op jit(solution)/shard_map/jit(diagonal)/gather | solution.py:59
  117.5 1.9 bitcast_add_fusion.1
  119.4 1.5 copy.21
  123.0 11.7 %cholesky.104 = f32[128,128]{1,0:T(8,128)S(1)} custom-call(f32[128,128]{1,0:T(8,128)S(1)} %cholesky.269), custom_call_target="Cholesky" | custom-call | tf_op jit(solution)/shard_map/jit(cholesky)/cholesky | solution.py:82
  134.9 9.8 %custom-call.34 = f32[1,128,128]{1,2,0:T(8,128)S(1)} custom-call(f32[1,128,128]{2,1,0:T(8,128)S(1)} %get-tuple-element.48), custom_call_target="InvertDiagBlocksLowerTriangular" | custom-call | tf_op jit(solution)/shard_map/jit(cholesky)/cholesky | solution.py:82
  144.7 1.4 constant_dynamic-update-slice_fusion.3
  146.1 1.4 convolution_subtract_fusion
  148.1 12.5 %cholesky.217 = f32[128,128]{1,0:T(8,128)S(1)} custom-call(f32[128,128]{1,0:T(8,128)} %cholesky.273), custom_call_target="Cholesky" | custom-call | tf_op jit(solution)/shard_map/jit(cholesky)/cholesky | solution.py:82
  160.7 1.2 select_reduce_fusion.1
  161.9 10.8 %custom-call.35 = f32[1,128,128]{1,2,0:T(8,128)S(1)} custom-call(f32[1,128,128]{2,1,0:T(8,128)} %get-tuple-element.45), custom_call_target="InvertDiagBlocksLowerTriangular" | custom-call | tf_op jit(solution)/shard_map/jit(cholesky)/cholesky | solution.py:82
  173.1 1.3 convolution_subtract_fusion.1
  174.4 11.7 %cholesky.238 = f32[128,128]{1,0:T(8,128)S(1)} custom-call(f32[128,128]{1,0:T(8,128)S(1)} %cholesky.278), custom_call_target="Cholesky" | custom-call | tf_op jit(solution)/shard_map/jit(cholesky)/cholesky | solution.py:82
  186.9 9.8 %custom-call.36 = f32[1,128,128]{1,2,0:T(8,128)S(1)} custom-call(f32[1,128,128]{2,1,0:T(8,128)S(1)} %get-tuple-element.42), custom_call_target="InvertDiagBlocksLowerTriangular" | custom-call | tf_op jit(solution)/shard_map/jit(cholesky)/cholesky | solution.py:82
  197.0 1.2 convolution_subtract_fusion.2
  198.2 10.8 %cholesky.258 = f32[116,116]{1,0:T(8,128)S(1)} custom-call(f32[116,116]{1,0:T(8,128)S(1)} %convolution_subtract_fusion.2), custom_call_target="Cholesky" | custom-call | tf_op jit(solution)/shard_map/jit(cholesky)/cholesky | solution.py:82
  209.7 1.3 compare_reduce_fusion.2
  214.7 9.1 %while.1 = (s32[]{:T(128)}, f32[500,500]{1,0:T(8,128)}, s32[3,2]{0,1:T(2,128)S(1)}, f32[3,128,128]{2,1,0:T(8,128)S(1)}, s32[]{:T(128)}) while((s32[]{:T(128)}, f32[500,500]{1,0:T(8,128)}, s32[3,2]{0,1:T(2,128)S(1)}, f32[3,128,128]{2,1,0:T(8,128)S(1)}, s32[]{:T(128)}) %tuple.48), condition=%wide.while_cond, body=%wide.while_body.sunk | while | flops 2 | bytes 131181 | solution.py:16
  215.4 2.3 bitcast_dynamic-update-slice_fusion.2
  218.4 2.3 bitcast_dynamic-update-slice_fusion.2
  221.4 2.3 bitcast_dynamic-update-slice_fusion.2
  224.7 40.1 %custom-call.37 = f32[4,128,128]{1,2,0:T(8,128)S(1)} custom-call(f32[4,128,128]{2,1,0:T(8,128)} %pad_maximum_fusion), custom_call_target="InvertDiagBlocksLowerTriangular" | custom-call | tf_op jit(solution)/shard_map/jit(_cho_solve)/triangular_solve | solution.py:16
  271.2 85.2 %all-reduce.10.cloned.1.call-done = f32[5,500,8]{1,2,0:T(8,128)} async-done(((f32[5,500,8]{1,2,0:T(8,128)}), f32[5,500,8]{1,2,0:T(8,128)}) %all-reduce.10.cloned.1.call-update) | async-done | bytes 80016 | tf_op jit(solution)/shard_map/psum | solution.py:86
  356.4 2.2 fusion.12
  358.5 1.6 fusion.13
  360.9 3.4 all-to-all-start
  364.4 4.9 %all-to-all-done = f32[8,1,5,1024]{3,1,2,0:T(1,128)S(1)} async-done(((f32[8,1,5,1024]{3,1,2,0:T(1,128)}), f32[8,1,5,1024]{3,1,2,0:T(1,128)S(1)}, u32[]{:S(2)}, u32[]{:S(2)}) %all-to-all-start) | async-done | bytes 163872 | tf_op jit(solution)/shard_map/all_to_all | solution.py:95
  369.5 4.0 fusion.4
  373.5 1.3 fusion.6
  374.8 60.6 %all-reduce.3 = (f32[4,5,10,10]{3,2,1,0:T(8,128)S(1)}, f32[4,5,10]{2,0,1:T(4,128)S(1)}) all-reduce(f32[4,5,10,10]{3,2,1,0:T(8,128)S(1)} %fusion.6, f32[4,5,10]{2,0,1:T(4,128)S(1)} %bitcast.154), channel_id=1, replica_groups=mesh['samp'=16,'blk'=2] {'samp'}, use_global_device_ids=true, to_apply=%region_21.22 | all-reduce | flops 2200 | bytes 17600 | tf_op jit(solution)/shard_map/psum | solution.py:108
  (104 shorter events, 24.4 us)
Async XLA Ops:
  7.2 99.6 %all-reduce.8.cloned.1.call-start = ((), (), s32[]{:S(2)}) async-start(), calls=%async_computation.1 | async-start | bytes 2064384 | tf_op jit(solution)/shard_map/psum | solution.py:41
  7.2 3.4 copy-start.5
  10.5 1.2 copy-start.1
  10.5 2.1 copy-start.6
  10.5 345.8 %all-reduce.10.cloned.1.call-start = ((), (), s32[]{:S(2)}) async-start(), calls=%async_computation.2 | async-start | bytes 163840 | tf_op jit(solution)/shard_map/psum | solution.py:86
  12.8 67.6 %copy-start.15 = (f32[5]{0:T(128)S(1)}, f32[5]{0:T(128)}, u32[]{:S(2)}) copy-start(f32[5]{0:T(128)} %constant.247.clone) | copy-start | bytes 64
  12.8 68.2 %copy-start.8 = (s32[1024]{0:T(1024)S(1)}, s32[1024]{0:T(1024)}, u32[]{:S(2)}) copy-start(s32[1024]{0:T(1024)} %param.8) | copy-start | bytes 12292
  106.8 10.7 %copy-start = (f32[1,500,500]{2,1,0:T(8,128)S(1)}, f32[1,500,500]{2,1,0:T(8,128)}, u32[]{:S(2)}) copy-start(f32[1,500,500]{2,1,0:T(8,128)} %all-reduce.8.cloned.1.call-done) | copy-start | bytes 3000004
  122.0 1.0 copy-start.4
  213.6 0.6 copy-start.14
  213.6 1.1 copy-start.7
  213.7 1.0 copy-start.2
  223.8 44.5 %copy-start.3 = (f32[500,500]{1,0:T(8,128)S(1)}, f32[500,500]{1,0:T(8,128)}, u32[]{:S(2)}) copy-start(f32[500,500]{1,0:T(8,128)} %get-tuple-element.106) | copy-start | bytes 3000004
  223.9 46.4 %copy-start.10 = (f32[5]{0:T(128)S(1)}, f32[5]{0:T(128)}, u32[]{:S(2)}) copy-start(f32[5]{0:T(128)} %and_convert_fusion) | copy-start | bytes 64
  223.9 47.2 %copy-start.11 = (f32[4]{0:T(128)S(1)}, f32[4]{0:T(128)}, u32[]{:S(2)}) copy-start(f32[4]{0:T(128)} %dynamic-slice.3) | copy-start | bytes 52
  223.9 47.2 %copy-start.12 = (f32[4]{0:T(128)S(1)}, f32[4]{0:T(128)}, u32[]{:S(2)}) copy-start(f32[4]{0:T(128)} %dynamic-slice.4) | copy-start | bytes 52
  271.2 87.4 %copy-start.9 = (f32[1,500]{1,0:T(1,128)S(1)}, f32[1,500]{1,0:T(1,128)}, u32[]{:S(2)}) copy-start(f32[1,500]{1,0:T(1,128)} %get-tuple-element.53) | copy-start | bytes 6004
  356.4 2.2 copy-start.13
  360.9 8.4 %all-to-all-start = ((f32[8,1,5,1024]{3,1,2,0:T(1,128)}), f32[8,1,5,1024]{3,1,2,0:T(1,128)S(1)}, u32[]{:S(2)}, u32[]{:S(2)}) async-start(f32[8,1,5,1024]{3,1,2,0:T(1,128)} %copy.22), calls=%async_computation | async-start | bytes 327680 | tf_op jit(solution)/shard_map/all_to_all | solution.py:95
Sparse Core Ops, SparseCore 0:
  11.5 95.2 all-reduce.7
  271.2 85.1 all-reduce.9
where the time goes:
time: 449 us; the launch traced here: 444 us
  other arithmetic  130 us (29%)
  blocking collectives  125 us (28%)
  waiting for transfers between devices  116 us (26%)
  local copies, waits for them, and re-layouts  27.4 us (6%)
  matrix products  24.7 us (6%)
  between operations  17.4 us (4%)
    psum x1, waiting for transfers between devices, body(): lax.psum(contribution, 'samp')  85.2 us
    another operation x14, other arithmetic, body(): lower_factor = jnp.linalg.cholesky(chosen_cov + penalty * identity)  81.3 us
    psum x1, blocking collectives, body(): lax.psum((gram_local, sums_local, trait_local, present_local, counts_loca...  64 us
    psum x1, blocking collectives, body(): gram_sum, cross_sum = lax.psum((gram_part, cross_part), 'samp')  60.6 us
    another operation x8, other arithmetic, solve_one(): return jax.scipy.linalg.cho_solve((lower_factor, True), right_side)  41.6 us
    psum x1, waiting for transfers between devices, body(): lax.psum((gram_local, sums_local, trait_local, present_local, counts_loca...  25.8 us
    gather x1, local copies, waits for them, and re-layouts, body(): jnp.diagonal(gram_total, axis1=1, axis2=2) / samples  10.1 us
    another operation x9, local copies, waits for them, and re-layouts  9.01 us
  transfers between devices with their start and end apart: 3, of which 3 were waited for; matrix products, arithmetic and copies ran while one was open for 1% of the time, Pallas kernels for 0%

commit v1 on v0

v1 whole, which is shorter than its diff:
```python
import functools
import jax
import jax.numpy as jnp
from jax import lax
from jax.experimental import pallas as pl
from jax.experimental.pallas import tpu as pltpu
from jax.sharding import PartitionSpec as P

TRAITS = 8
FOLDS = 5
HERITABILITY = (0.01, 0.25, 0.5, 0.75, 0.99)
TILE = 128
STEP = 8
SIDE = 32
SLOTS = 6
HALF = SLOTS // 2
VMEM_BYTES = 32 * 1024 * 1024

NN = (((1,), (0,)), ((), ()))
NT = (((1,), (1,)), ((), ()))
TN = (((0,), (0,)), ((), ()))


def dot(a, b, dims=NN):
    return lax.dot_general(
        a, b, dims, precision=lax.Precision.HIGHEST, preferred_element_type=jnp.float32
    )


def dot_bf16(a, b, dims=NN):
    return lax.dot_general(a, b, dims, preferred_element_type=jnp.float32)


def split_three(value):
    high = value.astype(jnp.bfloat16)
    left = value - high.astype(jnp.float32)
    middle = left.astype(jnp.bfloat16)
    low = (left - middle.astype(jnp.float32)).astype(jnp.bfloat16)
    return high, middle, low


def iota(shape, dim):
    return lax.broadcasted_iota(jnp.int32, shape, dim)


def block_rows(tiles):
    place, row = {}, 0
    for i in range(tiles):
        for j in range(i, tiles):
            place[i, j] = row
            row += TILE
    return place, row


def call(kernel, out_shape, in_specs, scratch, name):
    vmem = pl.BlockSpec(memory_space=pltpu.VMEM)
    smem = pl.BlockSpec(memory_space=pltpu.SMEM)
    return pl.pallas_call(
        kernel,
        out_shape=out_shape,
        in_specs=[smem if spec == "smem" else vmem if spec == "vmem" else spec for spec in in_specs],
        out_specs=jax.tree.map(lambda _: vmem, out_shape),
        scratch_shapes=scratch,
        compiler_params=pltpu.CompilerParams(vmem_limit_bytes=VMEM_BYTES),
        name=name,
    )


def gram_kernel(markers, dosage, traits, observed, packed, padded):
    width, rows = padded.shape
    tiles = width // TILE
    place, side = block_rows(tiles)
    edge = markers // 16 * 16
    padded[0:edge, :] = dosage[0:edge, :]
    tail = dosage[edge:edge + 16, :].astype(jnp.float32)
    tail = jnp.where(iota(tail.shape, 0) + edge < markers, tail, 0.0)
    padded[edge:edge + 16, :] = tail.astype(jnp.bfloat16)
    if edge + 16 < width:
        padded[edge + 16:, :] = jnp.zeros((width - edge - 16, rows), jnp.bfloat16)
    values = traits[...]
    present = observed[...].astype(jnp.float32)
    masked = present * values
    high, middle, low = (part.astype(jnp.float32) for part in split_three(masked))
    ones = jnp.ones(present.shape, jnp.float32)
    extra = jnp.concatenate([high, middle, low, present, ones, ones], 0).astype(jnp.bfloat16)
    products = dot_bf16(extra, padded[...], NT)
    sums = [jnp.sum(v, axis=1, keepdims=True) for v in (present, masked, masked * values)]
    lane = iota((TRAITS, TILE), 1)
    stats = jnp.where(
        lane == 0, sums[0], jnp.where(lane == 1, sums[1], jnp.where(lane == 2, sums[2], 0.0))
    )
    for i in range(tiles):
        here = dot_bf16(padded[i * TILE:(i + 1) * TILE, :], padded[i * TILE:, :], NT)
        for j in range(i, tiles):
            packed[place[i, j]:place[i, j] + TILE, :] = here[:, (j - i) * TILE:(j - i + 1) * TILE]
        cols = slice(i * TILE, (i + 1) * TILE)
        row = side + SIDE * i
        packed[row:row + 8, :] = products[0:8, cols] + products[8:16, cols] + products[16:24, cols]
        packed[row + 8:row + 16, :] = products[24:32, cols]
        packed[row + 16:row + 24, :] = products[32:40, cols]
        packed[row + 24:row + 32, :] = stats


def eliminate(work, old, fits):
    shape = (fits, STEP, TILE)
    row, lane = iota(shape, 1), iota(shape, 2)
    count = TILE // STEP
    for t in range(count):
        base = t * STEP
        panel = work[:, base:base + STEP, :]
        cols = [
            jnp.broadcast_to(panel[:, :, base + m:base + m + 1], shape) for m in range(STEP)
        ]
        inside = jnp.logical_and(lane >= base, lane < base + STEP)
        panel = jnp.where(inside, jnp.where(lane - base == row, 1.0, 0.0), panel)
        old[:, base:base + STEP, :] = jnp.where(lane < base + STEP, panel, 0.0)
        scale = None
        for j in range(STEP):
            inverse = jnp.broadcast_to(1.0 / cols[j][:, j:j + 1, :], shape)
            here = row == j
            gain = jnp.where(here, 0.0, cols[j] * inverse)
            scale = inverse if scale is None else jnp.where(here, inverse, scale)
            for m in range(j + 1, STEP):
                cols[m] = cols[m] - gain * cols[m][:, j:j + 1, :]
            panel = panel - gain * panel[:, j:j + 1, :]
        panel = panel * scale
        work[:, base:base + STEP, :] = panel
        rows = [jnp.broadcast_to(panel[:, q:q + 1, :], shape) for q in range(STEP)]
        for g in range(t + 1, count):
            other = work[:, g * STEP:(g + 1) * STEP, :]
            total = jnp.where(inside, 0.0, other)
            for q in range(STEP):
                total = total - jnp.broadcast_to(
                    other[:, :, base + q:base + q + 1], shape
                ) * rows[q]
            work[:, g * STEP:(g + 1) * STEP, :] = total


def fit_kernel(samples, markers, penalty, packed, out, stats, centre, grid, wide, work, old, rhs):
    fits = work.shape[0]
    tiles = rhs.shape[-1] // TILE
    place, side = block_rows(tiles)

    def part(tile, which):
        row = side + SIDE * tile + 8 * which
        return packed[row:row + 8, :]

    sums = part(0, 3)
    counts, first, second = sums[:, 0:1], sums[:, 1:2], sums[:, 2:3]
    mean = first / counts
    spread = jnp.sqrt(second / counts - mean * mean + 1e-05)
    lane = iota((TRAITS, TILE), 1)
    stats[...] = jnp.where(lane == 0, mean, jnp.where(lane == 1, spread, 0.0))
    eye = iota((TILE, TILE), 0) == iota((TILE, TILE), 1)
    lower = iota((TILE, TILE), 1) // STEP <= iota((TILE, TILE), 0) // STEP
    line = iota((1, TILE), 1)
    share = 1.0 / samples
    totals = [part(i, 2)[0:1, :] for i in range(tiles)]
    columns = [jnp.transpose(jnp.broadcast_to(t, (TILE, TILE))) for t in totals]
    squares = []
    for i in range(tiles):
        mine = slice(i * TILE, (i + 1) * TILE)
        block = packed[place[i, i]:place[i, i] + TILE, :]
        diagonal = jnp.sum(jnp.where(eye, block, 0.0), axis=0, keepdims=True)
        middle = totals[i] * share
        centre[:, mine] = jnp.broadcast_to(middle, (8, TILE))
        squares.append(diagonal * share - middle * middle + 1e-05)
        for j in range(i, tiles):
            block = packed[place[i, j]:place[i, j] + TILE, :]
            grid[i, :, j * TILE:(j + 1) * TILE] = block - columns[i] * totals[j] * share
        side_i = (part(i, 0) - part(i, 1) * mean) / spread
        for f in range(fits):
            rhs[f, :, mine] = side_i

    def ridge(i, f):
        value = jnp.where(line + i * TILE < markers, penalty[f] * squares[i], 1.0)
        return jnp.where(eye, value, 0.0)

    for k in range(tiles):
        lo, hi = k * TILE, (k + 1) * TILE
        for f in range(fits):
            work[f] = grid[0, :, lo:hi] + ridge(0, f) if k == 0 else wide[f, k, :, lo:hi]
        eliminate(work, old, fits)
        for f in range(fits):
            inverse = dot(old[f], jnp.where(lower, work[f], 0.0), TN)
            mine = rhs[f, :, lo:hi]
            rhs[f, :, lo:hi] = dot(mine, inverse)
            if hi == tiles * TILE:
                continue
            above = grid[0, :, hi:] if k == 0 else wide[f, k, :, hi:]
            weights = dot(inverse, above)
            rhs[f, :, hi:] = rhs[f, :, hi:] - dot(mine, weights)
            for i in range(k + 1, tiles):
                begin = i * TILE
                before = grid[i, :, begin:] if k == 0 else wide[f, i, :, begin:]
                column = above[:, begin - hi:begin - hi + TILE]
                wide[f, i, :, begin:] = before - dot(column, weights[:, begin - hi:], TN)
                if k == 0:
                    wide[f, i, :, begin:begin + TILE] = wide[f, i, :, begin:begin + TILE] + ridge(i, f)
            wide[f, k, :, hi:] = weights
    for f in range(fits):
        for k in reversed(range(tiles)):
            lo, hi = k * TILE, (k + 1) * TILE
            value = rhs[f, :, lo:hi]
            if hi < tiles * TILE:
                value = value - dot(out[f, :, hi:], wide[f, k, :, hi:], NT)
            out[f, :, lo:hi] = value


def predict_kernel(pairs, place, mine, other, centre, padded, out):
    odd = place[0] == 1
    rows = []
    for f in range(HALF):
        rows.append(jnp.where(odd, other[f], mine[f]))
    for f in range(HALF):
        rows.append(jnp.where(odd, mine[f], other[f]))
    if pairs:
        upper = iota(rows[0].shape, 0) < TRAITS // 2
        second = place[1] == 1
        halves = [[], []]
        for s in range(0, SLOTS, 2):
            a, b = rows[s], rows[s + 1]
            turned_a, turned_b = (pltpu.roll(v, TRAITS // 2, 0) for v in (a, b))
            low, high = jnp.where(upper, a, turned_b), jnp.where(upper, turned_a, b)
            halves[0].append(jnp.where(second, high, low))
            halves[1].append(jnp.where(second, low, high))
        rows = halves[0] + halves[1]
    weights = jnp.concatenate(rows, 0)
    count = weights.shape[0]
    shift = jnp.sum(weights * centre[0:1, :], axis=1, keepdims=True)
    parts = [part.astype(jnp.float32) for part in split_three(weights)]
    product = dot_bf16(jnp.concatenate(parts, 0).astype(jnp.bfloat16), padded[...])
    total = product[0:count] + product[count:2 * count] + product[2 * count:3 * count] - shift
    if pairs:
        out[0] = total[:count // 2]
        out[1] = total[count // 2:]
    else:
        out[...] = total


def stack_kernel(pairs, per_share, place, mine, other, stats, traits, observed, folds, out):
    first = place[1] * per_share
    if pairs:
        second = place[1] == 1
        levels = jnp.concatenate(
            [jnp.where(second, other[...], mine[...]), jnp.where(second, mine[...], other[...])], 0
        )
    else:
        levels = mine[...]
    count, samples = levels.shape
    present = observed[...].astype(jnp.float32)
    scaled = present * (traits[...] - stats[:, 0:1]) / stats[:, 1:2]
    pick = iota((count, TRAITS), 1) == first + iota((count, TRAITS), 0) % per_share
    spread = dot_bf16(
        jnp.where(pick, 1.0, 0.0).astype(jnp.bfloat16), present.astype(jnp.bfloat16)
    )
    kept = levels * spread
    left = [kept * jnp.where(folds[...] == k, 1.0, 0.0) for k in range(FOLDS)] + [levels]
    left = jnp.concatenate(left, 0)
    right = jnp.concatenate([levels, scaled], 0)
    full = dot(right, left, NT)
    row, col = iota(full.shape, 0), iota(full.shape, 1)
    trait = jnp.where(row < count, row % per_share, row - count - first)
    full = jnp.where(trait == col % per_share, full, 0.0)
    shape = (out.shape[0], full.shape[0])
    level, source = iota(shape, 0), iota(shape, 1)
    group = jnp.where(source < count, source // per_share, count // per_share)
    out[...] = dot(jnp.where(level == group, 1.0, 0.0), full)


def scale_kernel(per_share, samples, total, out):
    height, width = total.shape
    count = width // (FOLDS + 1)
    value = total[...]
    level, column = iota((height, count), 0), iota((height, count), 1)
    energy = jnp.where(level == column // per_share, value[:, FOLDS * count:], 0.0)
    shape = (count, width)
    source, target = iota(shape, 0), iota(shape, 1)
    by_row = dot(energy, jnp.where(source % per_share == target % per_share, 1.0, 0.0))
    every = jnp.broadcast_to(jnp.sum(energy, axis=0, keepdims=True), (8, count))
    by_column = dot(every, jnp.where(source == target % count, 1.0, 0.0))[0:1, :]
    root_row = jnp.where(
        iota((height, width), 0) < count // per_share, jnp.sqrt(by_row / samples + 1e-06), 1.0
    )
    root_column = jnp.sqrt(by_column / samples + 1e-06)
    out[...] = value / root_row / root_column * (FOLDS / samples)


def swap(value, axis, mask):
    size = lax.axis_size(axis)
    return lax.ppermute(value, axis, [(i, i ^ mask) for i in range(size)])


def masks_of(axis):
    size, mask, found = lax.axis_size(axis), 1, []
    while mask < size:
        found.append(mask)
        mask *= 2
    return found


def sum_over(value, axis, halvings):
    masks = masks_of(axis)
    position = lax.axis_index(axis)
    for mask in masks[:halvings]:
        half = value.shape[0] // 2
        low, high = value[:half], value[half:]
        up = (position & mask) != 0
        value = jnp.where(up, high, low) + swap(jnp.where(up, low, high), axis, mask)
    for mask in masks[halvings:]:
        value = value + swap(value, axis, mask)
    for mask in reversed(masks[:halvings]):
        up = (position & mask) != 0
        other = swap(value, axis, mask)
        value = jnp.concatenate([jnp.where(up, other, value), jnp.where(up, value, other)], 0)
    return value


def body(genotypes, traits, observed, fold_index):
    local_rows, markers = genotypes.shape
    sample_devices = lax.axis_size("samp")
    block_devices = lax.axis_size("blk")
    samples = local_rows * sample_devices
    all_markers = markers * block_devices
    width = -(-markers // TILE) * TILE
    tiles = width // TILE
    per_share = TRAITS // block_devices
    pairs = block_devices == 2
    f32 = functools.partial(jax.ShapeDtypeStruct, dtype=jnp.float32)
    position, block = lax.axis_index("samp"), lax.axis_index("blk")
    odd = position % 2
    place = jnp.stack([odd, block]).astype(jnp.int32)
    traits, observed = traits.T, observed.T
    _, side = block_rows(tiles)

    whole = lambda shape: pl.BlockSpec(shape, lambda _: (0, 0))
    packed, padded = pl.pallas_call(
        functools.partial(gram_kernel, markers),
        grid=(1,),
        out_shape=[
            f32((side + SIDE * tiles, TILE)),
            jax.ShapeDtypeStruct((width, local_rows), jnp.bfloat16),
        ],
        in_specs=[whole((width, local_rows)), whole(traits.shape), whole(observed.shape)],
        out_specs=[whole((side + SIDE * tiles, TILE)), whole((width, local_rows))],
        compiler_params=pltpu.CompilerParams(vmem_limit_bytes=VMEM_BYTES),
        name="local_gram",
    )(genotypes.T, traits, observed)
    packed = sum_over(packed, "samp", 2)

    penalties = [all_markers * (1.0 - h) / h for h in HERITABILITY]
    penalties = penalties + [penalties[-1]] * (SLOTS - len(penalties))
    penalty = jnp.where(
        odd == 1,
        jnp.array(penalties[HALF:], jnp.float32),
        jnp.array(penalties[:HALF], jnp.float32),
    )
    weights, stats, centre = call(
        functools.partial(fit_kernel, samples, markers),
        [f32((HALF, TRAITS, width)), f32((TRAITS, TILE)), f32((8, width))],
        ["smem", "vmem"],
        [
            pltpu.VMEM((tiles, TILE, width), jnp.float32),
            pltpu.VMEM((HALF, tiles, TILE, width), jnp.float32),
            pltpu.VMEM((HALF, TILE, TILE), jnp.float32),
            pltpu.VMEM((HALF, TILE, TILE), jnp.float32),
            pltpu.VMEM((HALF, TRAITS, width), jnp.float32),
        ],
        "ridge_fits",
    )(penalty, packed)
    other = swap(weights, "samp", 1)

    count = SLOTS * TRAITS
    shape = (2, count // 2, local_rows) if pairs else (count, local_rows)
    predicted = call(
        functools.partial(predict_kernel, pairs),
        f32(shape),
        ["smem", "vmem", "vmem", "vmem", "vmem"],
        [],
        "predictions",
    )(place, weights, other, centre, padded)
    if pairs:
        mine, theirs = predicted[0], swap(predicted[1], "blk", 1)
    else:
        shares = predicted.reshape(SLOTS, block_devices, per_share, local_rows)
        shares = lax.all_to_all(shares, "blk", split_axis=1, concat_axis=0, tiled=True)
        mine = theirs = shares.reshape(count, local_rows)

    levels = count // per_share
    height = -(-(levels + 1) // 8) * 8
    products = call(
        functools.partial(stack_kernel, pairs, per_share),
        f32((height, (FOLDS + 1) * count)),
        ["smem"] + ["vmem"] * 6,
        [],
        "stacking",
    )(place, mine, theirs, stats, traits, observed, fold_index[None, :])
    products = sum_over(products, "samp", 0)
    result = call(
        functools.partial(scale_kernel, per_share, samples),
        f32((height, (FOLDS + 1) * count)),
        ["vmem"],
        [],
        "standardize",
    )(products)

    fits = len(HERITABILITY)
    result = result[:, :FOLDS * count].reshape(height, FOLDS, block_devices, SLOTS, per_share)
    result = result[:, :, :, :fits, :].reshape(height, FOLDS, block_devices * fits, per_share)
    gram = result[:levels].reshape((block_devices, SLOTS) + result.shape[1:])[:, :fits]
    gram = gram.reshape((block_devices * fits,) + result.shape[1:])
    return gram.transpose(3, 1, 2, 0), result[levels].transpose(2, 0, 1)


def solution(mesh):
    in_specs = (P("samp", "blk"), P("samp", None), P("samp", None), P("samp"))
    out_specs = (P("blk", None, None, None), P("blk", None, None))
    return jax.shard_map(body, mesh=mesh, in_specs=in_specs, out_specs=out_specs, check_vma=False)
```

time: 449 us -> 100 us (0.22); the launches traced: 444 us -> 99.9 us
  other arithmetic: 130 us -> 0.43 us
  blocking collectives: 125 us -> 0 us
  waiting for transfers between devices: 116 us -> 39.9 us
  Pallas kernels: 0 us -> 39.8 us
  matrix products: 24.7 us -> 0 us
  local copies, waits for them, and re-layouts: 27.4 us -> 6.09 us
  between operations: 17.4 us -> 0.85 us
  starting transfers between devices: 3.51 us -> 12.8 us
    psum x2 -> x0, blocking collectives: 125 us -> none  [the longest x1 64 us: body(): lax.psum((gram_local, sums_local, trait_local, present_local, counts_loca...]
    another operation x22 -> x1, other arithmetic: 123 us -> 0.07 us  [body(): place = jnp.stack([odd, block]).astype(jnp.int32)]
    psum x2 -> x0, waiting for transfers between devices: 111 us -> none  [the longest x1 85.2 us: body(): lax.psum(contribution, 'samp')]
    ppermute x0 -> x12, waiting for transfers between devices: none -> 39.9 us  [swap(): return lax.ppermute(value, axis, [(i, i ^ mask) for i in range(size)])]
    pallas_call x0 -> x5, Pallas kernels: none -> 39.8 us  [the longest x1 35.3 us: body(): call(functools.partial(fit_kernel, samples, markers), [f32((HALF, TRAITS,...]
    ppermute x0 -> x12, starting transfers between devices: none -> 12.8 us  [swap(): return lax.ppermute(value, axis, [(i, i ^ mask) for i in range(size)])]
    dot_general x6 -> x0, matrix products: 12 us -> none  [the longest x1 4.01 us: body(): jnp.einsum('kpls,sp->pkl', weighted, scaled_share, precision=PRECISE)]
    another operation x20 -> x0, matrix products: 10.5 us -> none  [the longest x6 5.86 us: body(): lower_factor = jnp.linalg.cholesky(chosen_cov + penalty * identity)]
  transfers between devices with their start and end apart: 3 -> 12, of which waited for: 3 -> 12; matrix products, arithmetic and copies ran while one was open for 1% -> 0% of each run, Pallas kernels for 0% -> 0%
where the time goes in v1:
time: 100 us; the launch traced here: 99.9 us
  waiting for transfers between devices  39.9 us (40%)
  Pallas kernels  39.8 us (40%)
  starting transfers between devices  12.8 us (13%)
  local copies, waits for them, and re-layouts  6.09 us (6%)
    ppermute x12, waiting for transfers between devices, swap(): return lax.ppermute(value, axis, [(i, i ^ mask) for i in range(size)])  39.9 us
    pallas_call x1, Pallas kernels, body(): call(functools.partial(fit_kernel, samples, markers), [f32((HALF, TRAITS,...  35.3 us
    ppermute x12, starting transfers between devices, swap(): return lax.ppermute(value, axis, [(i, i ^ mask) for i in range(size)])  12.8 us
    unnamed x17, local copies, waits for them, and re-layouts  4.28 us
    pallas_call x1, Pallas kernels, body(): call(functools.partial(stack_kernel, pairs, per_share), f32((height, (FOL...  2.05 us
  transfers between devices with their start and end apart: 12, of which 12 were waited for; matrix products, arithmetic and copies ran while one was open for 0% of the time, Pallas kernels for 0%

profile of v1, /device:TPU:0, one launch (start us, length us, event | category | flops | bytes accessed | tf_op | source)
XLA Modules:
  0.0 99.9 jit_solution(9685062267880423899)
XLA Ops:
  0.6 1.2 %copy-done = bf16[1024,500]{0,1:T(8,128)(2,1)S(1)} copy-done((bf16[1024,500]{0,1:T(8,128)(2,1)S(1)}, bf16[1024,500]{0,1:T(8,128)(2,1)}, u32[]{:S(2)}) %copy-start) | copy-done | bytes 1024024
  1.9 0.8 copy-done.1
  2.6 0.8 copy-done.3
  3.4 1.3 %local_gram.1 = (f32[1408,128]{1,0:T(8,128)S(1)}, bf16[512,1024]{1,0:T(8,128)(2,1)S(1)}) custom-call(bf16[500,1024]{1,0:T(8,128)(2,1)S(1)} %bitcast.20, f32[8,1024]{1,0:T(8,128)S(1)} %bitcast.21, s32[8,1024]{1,0:T(8,128)S(1)} %bitcast.23), custom_call_target="tpu_custom_call" | custom-call | tf_op jit(solution)/shard_map/local_gram/pallas_call | solution.py:337
  4.7 0.5 collective-permute-start
  5.2 1.3 %collective-permute-done = f32[704,128]{1,0:T(8,128)S(1)} collective-permute-done((f32[704,128]{1,0:T(8,128)S(1)}, f32[704,128]{1,0:T(8,128)S(1)}, u32[]{:S(2)}, u32[]{:S(2)}) %collective-permute-start) | collective-permute-done | bytes 360480 | tf_op jit(solution)/shard_map/ppermute | solution.py:291
  6.6 2.9 %collective-permute-start.1 = (f32[352,128]{1,0:T(8,128)S(1)}, f32[352,128]{1,0:T(8,128)S(1)}, u32[]{:S(2)}, u32[]{:S(2)}) collective-permute-start(f32[352,128]{1,0:T(8,128)S(1)} %slice_select_fusion.1), channel_id=1, source_target_pairs={{0,4},{2,6},{4,0},{6,2},{8,12},{10,14},{12,8},{14,10},{16,20},{18,... | collective-permute-start | bytes 540680 | tf_op jit(solution)/shard_map/ppermute | solution.py:291
  9.5 4.9 %collective-permute-done.1 = f32[352,128]{1,0:T(8,128)S(1)} collective-permute-done((f32[352,128]{1,0:T(8,128)S(1)}, f32[352,128]{1,0:T(8,128)S(1)}, u32[]{:S(2)}, u32[]{:S(2)}) %collective-permute-start.1) | collective-permute-done | bytes 180256 | tf_op jit(solution)/shard_map/ppermute | solution.py:291
  14.4 1.9 %collective-permute-start.2 = (f32[352,128]{1,0:T(8,128)S(1)}, f32[352,128]{1,0:T(8,128)S(1)}, u32[]{:S(2)}, u32[]{:S(2)}) collective-permute-start(f32[352,128]{1,0:T(8,128)S(1)} %select_add_fusion.1), channel_id=1, source_target_pairs={{0,8},{2,10},{4,12},{6,14},{8,0},{10,2},{12,4},{14,6},{16,24},{18,... | collective-permute-start | bytes 540680 | tf_op jit(solution)/shard_map/ppermute | solution.py:291
  16.3 4.3 %collective-permute-done.2 = f32[352,128]{1,0:T(8,128)S(1)} collective-permute-done((f32[352,128]{1,0:T(8,128)S(1)}, f32[352,128]{1,0:T(8,128)S(1)}, u32[]{:S(2)}, u32[]{:S(2)}) %collective-permute-start.2) | collective-permute-done | bytes 180256 | tf_op jit(solution)/shard_map/ppermute | solution.py:291
  20.6 2.6 %collective-permute-start.3 = (f32[352,128]{1,0:T(8,128)S(1)}, f32[352,128]{1,0:T(8,128)S(1)}, u32[]{:S(2)}, u32[]{:S(2)}) collective-permute-start(f32[352,128]{1,0:T(8,128)S(1)} %add.31), channel_id=1, source_target_pairs={{0,16},{2,18},{4,20},{6,22},{8,24},{10,26},{12,28},{14,30},{16,0},... | collective-permute-start | bytes 540680 | tf_op jit(solution)/shard_map/ppermute | solution.py:291
  23.2 7.4 %collective-permute-done.3 = f32[352,128]{1,0:T(8,128)S(1)} collective-permute-done((f32[352,128]{1,0:T(8,128)S(1)}, f32[352,128]{1,0:T(8,128)S(1)}, u32[]{:S(2)}, u32[]{:S(2)}) %collective-permute-start.3) | collective-permute-done | bytes 180256 | tf_op jit(solution)/shard_map/ppermute | solution.py:291
  30.6 1.1 %collective-permute-start.4 = (f32[352,128]{1,0:T(8,128)S(1)}, f32[352,128]{1,0:T(8,128)S(1)}, u32[]{:S(2)}, u32[]{:S(2)}) collective-permute-start(f32[352,128]{1,0:T(8,128)S(1)} %add.32), channel_id=1, source_target_pairs={{0,4},{2,6},{4,0},{6,2},{8,12},{10,14},{12,8},{14,10},{16,20},{18,... | collective-permute-start | bytes 540680 | tf_op jit(solution)/shard_map/ppermute | solution.py:291
  31.8 4.7 %collective-permute-done.4 = f32[352,128]{1,0:T(8,128)S(1)} collective-permute-done((f32[352,128]{1,0:T(8,128)S(1)}, f32[352,128]{1,0:T(8,128)S(1)}, u32[]{:S(2)}, u32[]{:S(2)}) %collective-permute-start.4) | collective-permute-done | bytes 180256 | tf_op jit(solution)/shard_map/ppermute | solution.py:291
  36.7 0.6 copy-done.6
  37.3 1.0 collective-permute-done.5
  38.4 35.3 %ridge_fits.1 = (f32[3,8,512]{2,1,0:T(8,128)S(1)}, f32[8,128]{1,0:T(8,128)S(1)}, f32[8,512]{1,0:T(8,128)S(1)}) custom-call(f32[3]{0:T(128)S(1)} %broadcast_select_fusion.4.penalty, f32[1408,128]{1,0:T(8,128)S(1)} %pad_maximum_fusion.packed), custom_call_target="tpu_custom_call" | custom-call | tf_op jit(solution)/shard_map/ridge_fits/pallas_call | solution.py:358
  74.0 1.0 %collective-permute-done.6.other = f32[3,8,512]{2,1,0:T(8,128)S(1)} collective-permute-done((f32[3,8,512]{2,1,0:T(8,128)S(1)}, f32[3,8,512]{2,1,0:T(8,128)S(1)}, u32[]{:S(2)}, u32[]{:S(2)}) %collective-permute-start.6) | collective-permute-done | bytes 49184 | tf_op jit(solution)/shard_map/ppermute | solution.py:291
  75.0 0.9 predictions.1
  76.0 0.9 collective-permute-start.7
  76.8 4.1 %collective-permute-done.7.other = f32[24,1024]{1,0:T(8,128)S(1)} collective-permute-done((f32[24,1024]{1,0:T(8,128)S(1)}, f32[24,1024]{1,0:T(8,128)S(1)}, u32[]{:S(2)}, u32[]{:S(2)}) %collective-permute-start.7) | collective-permute-done | bytes 98336 | tf_op jit(solution)/shard_map/ppermute | solution.py:291
  80.9 2.1 %stacking.1 = f32[16,288]{1,0:T(8,128)S(1)} custom-call(s32[2]{0:T(128)S(1)} %pad_add_fusion.place, f32[24,1024]{1,0:T(8,128)S(1)} %get-tuple-element.21.mine, f32[24,1024]{1,0:T(8,128)S(1)} %collective-permute-done.7.other, f32[8,128]{1,0:T(8,128)S(1)} %get-tuple-element.11.stats, f32[8,1024]{1,0:T(8,128)S(1)} %bitcast.22, s32[8,1024]{1,0:T(8,128)S(1)} %bitcast.24, ...), custom_call_target="tpu_custom_call" | custom-call | tf_op jit(solution)/shard_map/stacking/pallas_call | solution.py:391
  83.0 1.2 %collective-permute-done.8 = f32[16,288]{1,0:T(8,128)S(1)} collective-permute-done((f32[16,288]{1,0:T(8,128)S(1)}, f32[16,288]{1,0:T(8,128)S(1)}, u32[]{:S(2)}, u32[]{:S(2)}) %collective-permute-start.8) | collective-permute-done | bytes 18464 | tf_op jit(solution)/shard_map/ppermute | solution.py:291
  84.2 0.8 collective-permute-start.9
  85.0 3.0 %collective-permute-done.9 = f32[16,288]{1,0:T(8,128)S(1)} collective-permute-done((f32[16,288]{1,0:T(8,128)S(1)}, f32[16,288]{1,0:T(8,128)S(1)}, u32[]{:S(2)}, u32[]{:S(2)}) %collective-permute-start.9) | collective-permute-done | bytes 18464 | tf_op jit(solution)/shard_map/ppermute | solution.py:291
  88.3 3.6 %collective-permute-done.10 = f32[16,288]{1,0:T(8,128)S(1)} collective-permute-done((f32[16,288]{1,0:T(8,128)S(1)}, f32[16,288]{1,0:T(8,128)S(1)}, u32[]{:S(2)}, u32[]{:S(2)}) %collective-permute-start.10) | collective-permute-done | bytes 18464 | tf_op jit(solution)/shard_map/ppermute | solution.py:291
  91.9 1.6 %collective-permute-start.11 = (f32[16,288]{1,0:T(8,128)S(1)}, f32[16,288]{1,0:T(8,128)S(1)}, u32[]{:S(2)}, u32[]{:S(2)}) collective-permute-start(f32[16,288]{1,0:T(8,128)S(1)} %add.35), channel_id=1, source_target_pairs={{0,16},{2,18},{4,20},{6,22},{8,24},{10,26},{12,28},{14,30},{16,0},... | collective-permute-start | bytes 55304 | tf_op jit(solution)/shard_map/ppermute | solution.py:291
  93.5 3.4 %collective-permute-done.11 = f32[16,288]{1,0:T(8,128)S(1)} collective-permute-done((f32[16,288]{1,0:T(8,128)S(1)}, f32[16,288]{1,0:T(8,128)S(1)}, u32[]{:S(2)}, u32[]{:S(2)}) %collective-permute-start.11) | collective-permute-done | bytes 18464 | tf_op jit(solution)/shard_map/ppermute | solution.py:291
  97.6 0.4 copy.15
  98.0 0.9 copy.17
  98.8 0.4 copy.16
  99.2 0.7 squeeze.11
  (39 shorter events, 1.7 us)
Async XLA Ops:
  0.6 1.2 %copy-start = (bf16[1024,500]{0,1:T(8,128)(2,1)S(1)}, bf16[1024,500]{0,1:T(8,128)(2,1)}, u32[]{:S(2)}) copy-start(bf16[1024,500]{0,1:T(8,128)(2,1)} %param.6) | copy-start | bytes 3072004
  1.9 0.8 copy-start.1
  2.6 0.8 copy-start.3
  4.7 1.8 %collective-permute-start = (f32[704,128]{1,0:T(8,128)S(1)}, f32[704,128]{1,0:T(8,128)S(1)}, u32[]{:S(2)}, u32[]{:S(2)}) collective-permute-start(f32[704,128]{1,0:T(8,128)S(1)} %slice_select_fusion), channel_id=1, source_target_pairs={{0,2},{2,0},{4,6},{6,4},{8,10},{10,8},{12,14},{14,12},{16,18},{18,... | collective-permute-start | bytes 1081352 | tf_op jit(solution)/shard_map/ppermute | solution.py:291
  6.6 7.8 %collective-permute-start.1 = (f32[352,128]{1,0:T(8,128)S(1)}, f32[352,128]{1,0:T(8,128)S(1)}, u32[]{:S(2)}, u32[]{:S(2)}) collective-permute-start(f32[352,128]{1,0:T(8,128)S(1)} %slice_select_fusion.1), channel_id=1, source_target_pairs={{0,4},{2,6},{4,0},{6,2},{8,12},{10,14},{12,8},{14,10},{16,20},{18,... | collective-permute-start | bytes 540680 | tf_op jit(solution)/shard_map/ppermute | solution.py:291
  14.4 6.1 %collective-permute-start.2 = (f32[352,128]{1,0:T(8,128)S(1)}, f32[352,128]{1,0:T(8,128)S(1)}, u32[]{:S(2)}, u32[]{:S(2)}) collective-permute-start(f32[352,128]{1,0:T(8,128)S(1)} %select_add_fusion.1), channel_id=1, source_target_pairs={{0,8},{2,10},{4,12},{6,14},{8,0},{10,2},{12,4},{14,6},{16,24},{18,... | collective-permute-start | bytes 540680 | tf_op jit(solution)/shard_map/ppermute | solution.py:291
  20.6 10.0 %collective-permute-start.3 = (f32[352,128]{1,0:T(8,128)S(1)}, f32[352,128]{1,0:T(8,128)S(1)}, u32[]{:S(2)}, u32[]{:S(2)}) collective-permute-start(f32[352,128]{1,0:T(8,128)S(1)} %add.31), channel_id=1, source_target_pairs={{0,16},{2,18},{4,20},{6,22},{8,24},{10,26},{12,28},{14,30},{16,0},... | collective-permute-start | bytes 540680 | tf_op jit(solution)/shard_map/ppermute | solution.py:291
  30.6 5.9 %collective-permute-start.4 = (f32[352,128]{1,0:T(8,128)S(1)}, f32[352,128]{1,0:T(8,128)S(1)}, u32[]{:S(2)}, u32[]{:S(2)}) collective-permute-start(f32[352,128]{1,0:T(8,128)S(1)} %add.32), channel_id=1, source_target_pairs={{0,4},{2,6},{4,0},{6,2},{8,12},{10,14},{12,8},{14,10},{16,20},{18,... | collective-permute-start | bytes 540680 | tf_op jit(solution)/shard_map/ppermute | solution.py:291
  36.6 1.7 %collective-permute-start.5 = (f32[704,128]{1,0:T(8,128)S(1)}, f32[704,128]{1,0:T(8,128)S(1)}, u32[]{:S(2)}, u32[]{:S(2)}) collective-permute-start(f32[704,128]{1,0:T(8,128)S(1)} %pad_maximum_fusion.1), channel_id=1, source_target_pairs={{0,2},{2,0},{4,6},{6,4},{8,10},{10,8},{12,14},{14,12},{16,18},{18,... | collective-permute-start | bytes 1081352 | tf_op jit(solution)/shard_map/ppermute | solution.py:291
  36.7 0.7 copy-start.6
  36.7 0.7 copy-start.7
  73.8 1.3 %collective-permute-start.6 = (f32[3,8,512]{2,1,0:T(8,128)S(1)}, f32[3,8,512]{2,1,0:T(8,128)S(1)}, u32[]{:S(2)}, u32[]{:S(2)}) collective-permute-start(f32[3,8,512]{2,1,0:T(8,128)S(1)} %get-tuple-element.8.mine), channel_id=1, source_target_pairs={{0,2},{2,0},{4,6},{6,4},{8,10},{10,8},{12,14},{14,12},{16,18},{18,... | collective-permute-start | bytes 147464 | tf_op jit(solution)/shard_map/ppermute | solution.py:291
  75.9 5.0 %copy-start.2 = (f32[1024,8]{0,1:T(8,128)S(1)}, f32[1024,8]{0,1:T(8,128)}, u32[]{:S(2)}) copy-start(f32[1024,8]{0,1:T(8,128)} %param.7) | copy-start | bytes 98308
  75.9 5.0 %copy-start.4 = (s32[1024,8]{0,1:T(8,128)S(1)}, s32[1024,8]{0,1:T(8,128)}, u32[]{:S(2)}) copy-start(s32[1024,8]{0,1:T(8,128)} %param.8) | copy-start | bytes 98308
  75.9 5.0 %copy-start.5 = (s32[1024]{0:T(1024)S(1)}, s32[1024]{0:T(1024)}, u32[]{:S(2)}) copy-start(s32[1024]{0:T(1024)} %param.9) | copy-start | bytes 12292
  76.0 4.9 %collective-permute-start.7 = (f32[24,1024]{1,0:T(8,128)S(1)}, f32[24,1024]{1,0:T(8,128)S(1)}, u32[]{:S(2)}, u32[]{:S(2)}) collective-permute-start(f32[24,1024]{1,0:T(8,128)S(1)} %get-tuple-element.20), channel_id=1, source_target_pairs={{0,1},{1,0},{2,3},{3,2},{4,5},{5,4},{6,7},{7,6},{8,9},{9,8},{10,11... | collective-permute-start | bytes 294920 | tf_op jit(solution)/shard_map/ppermute | solution.py:291
  83.0 1.3 %collective-permute-start.8 = (f32[16,288]{1,0:T(8,128)S(1)}, f32[16,288]{1,0:T(8,128)S(1)}, u32[]{:S(2)}, u32[]{:S(2)}) collective-permute-start(f32[16,288]{1,0:T(8,128)S(1)} %stacking.1), channel_id=1, source_target_pairs={{0,2},{2,0},{4,6},{6,4},{8,10},{10,8},{12,14},{14,12},{16,18},{18,... | collective-permute-start | bytes 55304 | tf_op jit(solution)/shard_map/ppermute | solution.py:291
  84.2 3.8 %collective-permute-start.9 = (f32[16,288]{1,0:T(8,128)S(1)}, f32[16,288]{1,0:T(8,128)S(1)}, u32[]{:S(2)}, u32[]{:S(2)}) collective-permute-start(f32[16,288]{1,0:T(8,128)S(1)} %add.33), channel_id=1, source_target_pairs={{0,4},{2,6},{4,0},{6,2},{8,12},{10,14},{12,8},{14,10},{16,20},{18,... | collective-permute-start | bytes 55304 | tf_op jit(solution)/shard_map/ppermute | solution.py:291
  88.1 3.8 %collective-permute-start.10 = (f32[16,288]{1,0:T(8,128)S(1)}, f32[16,288]{1,0:T(8,128)S(1)}, u32[]{:S(2)}, u32[]{:S(2)}) collective-permute-start(f32[16,288]{1,0:T(8,128)S(1)} %add.34), channel_id=1, source_target_pairs={{0,8},{2,10},{4,12},{6,14},{8,0},{10,2},{12,4},{14,6},{16,24},{18,... | collective-permute-start | bytes 55304 | tf_op jit(solution)/shard_map/ppermute | solution.py:291
  91.9 5.0 %collective-permute-start.11 = (f32[16,288]{1,0:T(8,128)S(1)}, f32[16,288]{1,0:T(8,128)S(1)}, u32[]{:S(2)}, u32[]{:S(2)}) collective-permute-start(f32[16,288]{1,0:T(8,128)S(1)} %add.35), channel_id=1, source_target_pairs={{0,16},{2,18},{4,20},{6,22},{8,24},{10,26},{12,28},{14,30},{16,0},... | collective-permute-start | bytes 55304 | tf_op jit(solution)/shard_map/ppermute | solution.py:291

commit v2 on v1

--- a/solution.py
+++ b/solution.py
@@ -11,7 +11,9 @@
 HERITABILITY = (0.01, 0.25, 0.5, 0.75, 0.99)
 TILE = 128
 STEP = 8
-SIDE = 32
+SIDE = 24
+SUB = 32
+FITS = len(HERITABILITY)
 SLOTS = 6
 HALF = SLOTS // 2
 VMEM_BYTES = 32 * 1024 * 1024
@@ -43,12 +45,31 @@
     return lax.broadcasted_iota(jnp.int32, shape, dim)
 
 
+def dot_six(a, b, dims=NN):
+    if dims == TN:
+        a, dims = jnp.transpose(a), NN
+    (along_a,), (along_b,) = dims[0]
+    high_a, middle_a, low_a = split_three(a)
+    high_b, middle_b, low_b = split_three(b)
+
+    def part(x, y):
+        return dot_bf16(jnp.concatenate(x, along_a), jnp.concatenate(y, along_b), dims)
+
+    small = part([low_a, middle_a], [high_b, middle_b])
+    return (small + part([middle_a, high_a], [high_b, middle_b])) + part(
+        [high_a, high_a], [low_b, high_b]
+    )
+
+
 def block_rows(tiles):
     place, row = {}, 0
     for i in range(tiles):
-        for j in range(i, tiles):
+        for j in range(i + 1, tiles):
             place[i, j] = row
             row += TILE
+    for i in range(0, tiles, 2):
+        place[i, i] = place[i + 1, i + 1] = row
+        row += TILE
     return place, row
 
 
@@ -58,7 +79,7 @@
     return pl.pallas_call(
         kernel,
         out_shape=out_shape,
-        in_specs=[smem if spec == "smem" else vmem if spec == "vmem" else spec for spec in in_specs],
+        in_specs=[smem if spec == "smem" else vmem for spec in in_specs],
         out_specs=jax.tree.map(lambda _: vmem, out_shape),
         scratch_shapes=scratch,
         compiler_params=pltpu.CompilerParams(vmem_limit_bytes=VMEM_BYTES),
@@ -85,26 +106,34 @@
     extra = jnp.concatenate([high, middle, low, present, ones, ones], 0).astype(jnp.bfloat16)
     products = dot_bf16(extra, padded[...], NT)
     sums = [jnp.sum(v, axis=1, keepdims=True) for v in (present, masked, masked * values)]
-    lane = iota((TRAITS, TILE), 1)
-    stats = jnp.where(
-        lane == 0, sums[0], jnp.where(lane == 1, sums[1], jnp.where(lane == 2, sums[2], 0.0))
-    )
+    lane, line = iota((TRAITS, TILE), 1), iota((TRAITS, TILE), 0)
+    upper = iota((TILE, TILE), 0) <= iota((TILE, TILE), 1)
+    eye = iota((TILE, TILE), 0) == iota((TILE, TILE), 1)
+    even = None
     for i in range(tiles):
         here = dot_bf16(padded[i * TILE:(i + 1) * TILE, :], padded[i * TILE:, :], NT)
-        for j in range(i, tiles):
+        for j in range(i + 1, tiles):
             packed[place[i, j]:place[i, j] + TILE, :] = here[:, (j - i) * TILE:(j - i + 1) * TILE]
+        block = here[:, :TILE]
+        if i % 2:
+            packed[place[i, i]:place[i, i] + TILE, :] = jnp.where(upper, even, block)
+        even = block
+        diagonal = jnp.sum(jnp.where(eye, block, 0.0), axis=0, keepdims=True)
         cols = slice(i * TILE, (i + 1) * TILE)
         row = side + SIDE * i
-        packed[row:row + 8, :] = products[0:8, cols] + products[8:16, cols] + products[16:24, cols]
+        total = products[0:8, cols] + products[8:16, cols] + products[16:24, cols]
+        if i == tiles - 1:
+            for n, value in enumerate(sums):
+                total = jnp.where(lane == TILE - 1 - n, value, total)
+        packed[row:row + 8, :] = total
         packed[row + 8:row + 16, :] = products[24:32, cols]
-        packed[row + 16:row + 24, :] = products[32:40, cols]
-        packed[row + 24:row + 32, :] = stats
+        packed[row + 16:row + 24, :] = jnp.where(line == 0, products[32:40, cols], diagonal)
 
 
 def eliminate(work, old, fits):
     shape = (fits, STEP, TILE)
     row, lane = iota(shape, 1), iota(shape, 2)
-    count = TILE // STEP
+    count, per = TILE // STEP, SUB // STEP
     for t in range(count):
         base = t * STEP
         panel = work[:, base:base + STEP, :]
@@ -113,7 +142,7 @@
         ]
         inside = jnp.logical_and(lane >= base, lane < base + STEP)
         panel = jnp.where(inside, jnp.where(lane - base == row, 1.0, 0.0), panel)
-        old[:, base:base + STEP, :] = jnp.where(lane < base + STEP, panel, 0.0)
+        old[:, base:base + STEP, :] = panel
         scale = None
         for j in range(STEP):
             inverse = jnp.broadcast_to(1.0 / cols[j][:, j:j + 1, :], shape)
@@ -126,7 +155,8 @@
         panel = panel * scale
         work[:, base:base + STEP, :] = panel
         rows = [jnp.broadcast_to(panel[:, q:q + 1, :], shape) for q in range(STEP)]
-        for g in range(t + 1, count):
+        stop = (t // per + 1) * per
+        for g in range(t + 1, stop):
             other = work[:, g * STEP:(g + 1) * STEP, :]
             total = jnp.where(inside, 0.0, other)
             for q in range(STEP):
@@ -134,41 +164,69 @@
                     other[:, :, base + q:base + q + 1], shape
                 ) * rows[q]
             work[:, g * STEP:(g + 1) * STEP, :] = total
+        if t + 1 == stop and stop < count:
+            first, last = (t + 1 - per) * STEP, stop * STEP
+            line, column = iota((SUB, TILE), 0) + first, iota((SUB, TILE), 1)
+            keep = jnp.logical_or(column >= last, column // STEP <= line // STEP)
+            column = iota((TILE - last, TILE), 1)
+            done = jnp.logical_and(column >= first, column < last)
+            for f in range(fits):
+                left = split_three(old[f, first:last, :])
+                right = split_three(jnp.where(keep, work[f, first:last, :], 0.0))
+                product = dot_bf16(
+                    jnp.concatenate([left[i] for i in (0, 0, 0, 1, 1, 2)], 0),
+                    jnp.concatenate([right[i] for i in (0, 1, 2, 0, 1, 0)], 0),
+                    TN,
+                )
+                rest = work[f, last:, :]
+                work[f, last:, :] = jnp.where(done, 0.0, rest) - product[last:, :]
+    lower = iota(old.shape, 2) // STEP <= iota(old.shape, 1) // STEP
+    old[...] = jnp.where(lower, old[...], 0.0)
+    work[...] = jnp.where(lower, work[...], 0.0)
 
 
 def fit_kernel(samples, markers, penalty, packed, out, stats, centre, grid, wide, work, old, rhs):
     fits = work.shape[0]
     tiles = rhs.shape[-1] // TILE
+    end = tiles * TILE
     place, side = block_rows(tiles)
 
     def part(tile, which):
         row = side + SIDE * tile + 8 * which
         return packed[row:row + 8, :]
 
-    sums = part(0, 3)
-    counts, first, second = sums[:, 0:1], sums[:, 1:2], sums[:, 2:3]
+    sums = part(tiles - 1, 0)
+    counts, first, second = (sums[:, TILE - 1 - n:TILE - n] for n in range(3))
     mean = first / counts
     spread = jnp.sqrt(second / counts - mean * mean + 1e-05)
     lane = iota((TRAITS, TILE), 1)
     stats[...] = jnp.where(lane == 0, mean, jnp.where(lane == 1, spread, 0.0))
-    eye = iota((TILE, TILE), 0) == iota((TILE, TILE), 1)
-    lower = iota((TILE, TILE), 1) // STEP <= iota((TILE, TILE), 0) // STEP
+    row, col = iota((TILE, TILE), 0), iota((TILE, TILE), 1)
+    eye, upper = row == col, row <= col
     line = iota((1, TILE), 1)
     share = 1.0 / samples
     totals = [part(i, 2)[0:1, :] for i in range(tiles)]
-    columns = [jnp.transpose(jnp.broadcast_to(t, (TILE, TILE))) for t in totals]
     squares = []
     for i in range(tiles):
         mine = slice(i * TILE, (i + 1) * TILE)
-        block = packed[place[i, i]:place[i, i] + TILE, :]
-        diagonal = jnp.sum(jnp.where(eye, block, 0.0), axis=0, keepdims=True)
+        column = jnp.transpose(jnp.broadcast_to(totals[i], (TILE, TILE)))
+        diagonal = part(i, 2)[1:2, :]
         middle = totals[i] * share
         centre[:, mine] = jnp.broadcast_to(middle, (8, TILE))
         squares.append(diagonal * share - middle * middle + 1e-05)
         for j in range(i, tiles):
             block = packed[place[i, j]:place[i, j] + TILE, :]
-            grid[i, :, j * TILE:(j + 1) * TILE] = block - columns[i] * totals[j] * share
+            if i == j:
+                turned = jnp.transpose(block)
+                if i % 2:
+                    block = jnp.where(upper, turned, block)
+                    block = jnp.where(eye, diagonal, block)
+                else:
+                    block = jnp.where(upper, block, turned)
+            grid[i, :, j * TILE:(j + 1) * TILE] = block - column * totals[j] * share
         side_i = (part(i, 0) - part(i, 1) * mean) / spread
+        if i == tiles - 1:
+            side_i = jnp.where(lane + i * TILE < markers, side_i, 0.0)
         for f in range(fits):
             rhs[f, :, mine] = side_i
 
@@ -176,33 +234,43 @@
         value = jnp.where(line + i * TILE < markers, penalty[f] * squares[i], 1.0)
         return jnp.where(eye, value, 0.0)
 
+    for f in range(fits):
+        work[f] = grid[0, :, 0:TILE] + ridge(0, f)
     for k in range(tiles):
         lo, hi = k * TILE, (k + 1) * TILE
+        eliminate(work, old, fits)
+        lefts, rights = [old[f] for f in range(fits)], [work[f] for f in range(fits)]
+        both = None
+        if hi < end:
+            above = [grid[0, :, hi:] if k == 0 else wide[f, k, :, hi:] for f in range(fits)]
+            both = [
+                dot_six(jnp.concatenate([lefts[f], rights[f]], 0), above[f]) for f in range(fits)
+            ]
+        for i in range(k + 1, tiles):
+            for f in range(fits):
+                begin = i * TILE
+                left, weights = both[f][:TILE, begin - hi:begin - hi + TILE], both[f][TILE:, begin - hi:]
+                before = grid[i, :, begin:] if k == 0 else wide[f, i, :, begin:]
+                after = before - dot_six(left, weights, TN)
+                block = after[:, :TILE] + ridge(i, f) if k == 0 else after[:, :TILE]
+                if i == k + 1:
+                    work[f] = block
+                else:
+                    wide[f, i, :, begin:begin + TILE] = block
+                if i + 1 < tiles:
+                    wide[f, i, :, begin + TILE:] = after[:, TILE:]
         for f in range(fits):
-            work[f] = grid[0, :, lo:hi] + ridge(0, f) if k == 0 else wide[f, k, :, lo:hi]
-        eliminate(work, old, fits)
+            turned = dot(rhs[f, :, lo:hi], lefts[f], NT)
+            rhs[f, :, lo:hi] = dot(turned, rights[f])
+            if hi < end:
+                weights = both[f][TILE:]
+                rhs[f, :, hi:] = rhs[f, :, hi:] - dot(turned, weights)
+                wide[f, k, :, hi:] = dot_six(lefts[f], weights, TN)
+    for k in reversed(range(tiles)):
         for f in range(fits):
-            inverse = dot(old[f], jnp.where(lower, work[f], 0.0), TN)
-            mine = rhs[f, :, lo:hi]
-            rhs[f, :, lo:hi] = dot(mine, inverse)
-            if hi == tiles * TILE:
-                continue
-            above = grid[0, :, hi:] if k == 0 else wide[f, k, :, hi:]
-            weights = dot(inverse, above)
-            rhs[f, :, hi:] = rhs[f, :, hi:] - dot(mine, weights)
-            for i in range(k + 1, tiles):
-                begin = i * TILE
-                before = grid[i, :, begin:] if k == 0 else wide[f, i, :, begin:]
-                column = above[:, begin - hi:begin - hi + TILE]
-                wide[f, i, :, begin:] = before - dot(column, weights[:, begin - hi:], TN)
-                if k == 0:
-                    wide[f, i, :, begin:begin + TILE] = wide[f, i, :, begin:begin + TILE] + ridge(i, f)
-            wide[f, k, :, hi:] = weights
-    for f in range(fits):
-        for k in reversed(range(tiles)):
             lo, hi = k * TILE, (k + 1) * TILE
             value = rhs[f, :, lo:hi]
-            if hi < tiles * TILE:
+            if hi < end:
                 value = value - dot(out[f, :, hi:], wide[f, k, :, hi:], NT)
             out[f, :, lo:hi] = value
 
@@ -248,6 +316,7 @@
     else:
         levels = mine[...]
     count, samples = levels.shape
+    height, width = out.shape
     present = observed[...].astype(jnp.float32)
     scaled = present * (traits[...] - stats[:, 0:1]) / stats[:, 1:2]
     pick = iota((count, TRAITS), 1) == first + iota((count, TRAITS), 0) % per_share
@@ -255,35 +324,59 @@
         jnp.where(pick, 1.0, 0.0).astype(jnp.bfloat16), present.astype(jnp.bfloat16)
     )
     kept = levels * spread
-    left = [kept * jnp.where(folds[...] == k, 1.0, 0.0) for k in range(FOLDS)] + [levels]
+    left = [kept * jnp.where(folds[...] == k, 1.0, 0.0) for k in range(FOLDS)]
+    left = left + [jnp.zeros((width - FOLDS * count, samples), jnp.float32)]
     left = jnp.concatenate(left, 0)
     right = jnp.concatenate([levels, scaled], 0)
     full = dot(right, left, NT)
     row, col = iota(full.shape, 0), iota(full.shape, 1)
     trait = jnp.where(row < count, row % per_share, row - count - first)
     full = jnp.where(trait == col % per_share, full, 0.0)
-    shape = (out.shape[0], full.shape[0])
+    shape = (height, full.shape[0])
     level, source = iota(shape, 0), iota(shape, 1)
-    group = jnp.where(source < count, source // per_share, count // per_share)
+    slot = source // per_share
+    group = jnp.where(slot % SLOTS < FITS, slot // SLOTS * FITS + slot % SLOTS, height)
+    group = jnp.where(source < count, group, count // per_share // SLOTS * FITS)
     out[...] = dot(jnp.where(level == group, 1.0, 0.0), full)
-
-
-def scale_kernel(per_share, samples, total, out):
+    energy = dot(jnp.ones((8, samples), jnp.float32), levels * levels, NT)
+    last = count // per_share // SLOTS * FITS + 1
+    out[last:last + 1, 0:count] = energy[0:1, :]
+
+
+def scale_kernel(per_share, blocks, samples, total, gram, cross):
     height, width = total.shape
-    count = width // (FOLDS + 1)
+    count = blocks * SLOTS * per_share
+    levels = blocks * FITS
     value = total[...]
-    level, column = iota((height, count), 0), iota((height, count), 1)
-    energy = jnp.where(level == column // per_share, value[:, FOLDS * count:], 0.0)
+    energy = jnp.broadcast_to(value[levels + 1:levels + 2, 0:count], (height, count))
+    level, column = iota((height, count), 0), iota((height, count), 1) // per_share
+    group = jnp.where(column % SLOTS < FITS, column // SLOTS * FITS + column % SLOTS, height)
     shape = (count, width)
     source, target = iota(shape, 0), iota(shape, 1)
-    by_row = dot(energy, jnp.where(source % per_share == target % per_share, 1.0, 0.0))
-    every = jnp.broadcast_to(jnp.sum(energy, axis=0, keepdims=True), (8, count))
-    by_column = dot(every, jnp.where(source == target % count, 1.0, 0.0))[0:1, :]
+    by_row = dot(
+        jnp.where(level == group, energy, 0.0),
+        jnp.where(source % per_share == target % per_share, 1.0, 0.0),
+    )
+    by_column = dot(energy, jnp.where(source == target % count, 1.0, 0.0))
     root_row = jnp.where(
-        iota((height, width), 0) < count // per_share, jnp.sqrt(by_row / samples + 1e-06), 1.0
+        iota((height, width), 0) < levels, jnp.sqrt(by_row / samples + 1e-06), 1.0
     )
     root_column = jnp.sqrt(by_column / samples + 1e-06)
-    out[...] = value / root_row / root_column * (FOLDS / samples)
+    value = value / root_row / root_column * (FOLDS / samples)
+    turned = jnp.transpose(value)
+    shape = (FOLDS * 8, width)
+    line, column = iota(shape, 0), iota(shape, 1)
+    chosen = jnp.logical_and(line // 8 == column // count, line % 8 == column % per_share)
+    products = jnp.where(chosen, jnp.broadcast_to(value[levels:levels + 1, :], shape), 0.0)
+    shape = (width, TILE)
+    slot, target = iota(shape, 0) % count // per_share, iota(shape, 1)
+    group = jnp.where(slot % SLOTS < FITS, slot // SLOTS * FITS + slot % SLOTS, -1)
+    products = dot(products, jnp.where(group == target, 1.0, 0.0))
+    for k in range(FOLDS):
+        cross[k] = products[8 * k:8 * k + per_share, 0:levels]
+        for l in range(levels):
+            row = k * count + (l // FITS * SLOTS + l % FITS) * per_share
+            gram[k, l] = turned[row:row + per_share, 0:levels]
 
 
 def swap(value, axis, mask):
@@ -386,30 +479,25 @@
         shares = lax.all_to_all(shares, "blk", split_axis=1, concat_axis=0, tiled=True)
         mine = theirs = shares.reshape(count, local_rows)
 
-    levels = count // per_share
-    height = -(-(levels + 1) // 8) * 8
+    levels = block_devices * FITS
+    height = -(-(levels + 2) // 8) * 8
+    lanes = -(-FOLDS * count // TILE) * TILE
     products = call(
         functools.partial(stack_kernel, pairs, per_share),
-        f32((height, (FOLDS + 1) * count)),
+        f32((height, lanes)),
         ["smem"] + ["vmem"] * 6,
         [],
         "stacking",
     )(place, mine, theirs, stats, traits, observed, fold_index[None, :])
     products = sum_over(products, "samp", 0)
-    result = call(
-        functools.partial(scale_kernel, per_share, samples),
-        f32((height, (FOLDS + 1) * count)),
+    gram, cross = call(
+        functools.partial(scale_kernel, per_share, block_devices, samples),
+        [f32((FOLDS, levels, per_share, levels)), f32((FOLDS, per_share, levels))],
         ["vmem"],
         [],
         "standardize",
     )(products)
-
-    fits = len(HERITABILITY)
-    result = result[:, :FOLDS * count].reshape(height, FOLDS, block_devices, SLOTS, per_share)
-    result = result[:, :, :, :fits, :].reshape(height, FOLDS, block_devices * fits, per_share)
-    gram = result[:levels].reshape((block_devices, SLOTS) + result.shape[1:])[:, :fits]
-    gram = gram.reshape((block_devices * fits,) + result.shape[1:])
-    return gram.transpose(3, 1, 2, 0), result[levels].transpose(2, 0, 1)
+    return gram.transpose(2, 0, 1, 3), cross.transpose(1, 0, 2)
 
 
 def solution(mesh):

time: 100 us -> 84.4 us (0.84)
  Pallas kernels: 39.8 us -> 31.2 us
  waiting for transfers between devices: 39.9 us -> 35.2 us
  local copies, waits for them, and re-layouts: 6.09 us -> 3.42 us
    pallas_call x1, Pallas kernels: 35.3 us -> 25.6 us  [body(): call(functools.partial(fit_kernel, samples, markers), [f32((HALF, TRAITS,...]
    ppermute x12, waiting for transfers between devices: 39.9 us -> 35.2 us  [swap(): return lax.ppermute(value, axis, [(i, i ^ mask) for i in range(size)])]
    pallas_call x2, Pallas kernels: 2.34 us -> 3.43 us  [the longest x1 2.24 us: body(): call(functools.partial(stack_kernel, pairs, per_share), f32((height, lane...]
    unnamed x17 -> x16, local copies, waits for them, and re-layouts: 4.28 us -> 3.4 us
where the time goes in v2:
time: 84.4 us; the launch traced here: 84.1 us
  waiting for transfers between devices  35.2 us (42%)
  Pallas kernels  31.2 us (37%)
  starting transfers between devices  13 us (15%)
  local copies, waits for them, and re-layouts  3.42 us (4%)
    ppermute x12, waiting for transfers between devices, swap(): return lax.ppermute(value, axis, [(i, i ^ mask) for i in range(size)])  35.2 us
    pallas_call x1, Pallas kernels, body(): call(functools.partial(fit_kernel, samples, markers), [f32((HALF, TRAITS,...  25.6 us
    ppermute x12, starting transfers between devices, swap(): return lax.ppermute(value, axis, [(i, i ^ mask) for i in range(size)])  13 us
    unnamed x16, local copies, waits for them, and re-layouts  3.4 us
    pallas_call x1, Pallas kernels, body(): call(functools.partial(stack_kernel, pairs, per_share), f32((height, lane...  2.24 us
  transfers between devices with their start and end apart: 12, of which 12 were waited for; matrix products, arithmetic and copies ran while one was open for 0% of the time, Pallas kernels for 0%

profile of v2, /device:TPU:0, one launch (start us, length us, event | category | flops | bytes accessed | tf_op | source)
XLA Modules:
  0.0 84.1 jit_solution(13090358690191607356)
XLA Ops:
  0.6 1.2 %copy-done = bf16[1024,500]{0,1:T(8,128)(2,1)S(1)} copy-done((bf16[1024,500]{0,1:T(8,128)(2,1)S(1)}, bf16[1024,500]{0,1:T(8,128)(2,1)}, u32[]{:S(2)}) %copy-start) | copy-done | bytes 1024024
  1.9 0.8 copy-done.1
  2.6 0.8 copy-done.3
  3.4 1.3 %local_gram.1 = (f32[1120,128]{1,0:T(8,128)S(1)}, bf16[512,1024]{1,0:T(8,128)(2,1)S(1)}) custom-call(bf16[500,1024]{1,0:T(8,128)(2,1)S(1)} %bitcast.12, f32[8,1024]{1,0:T(8,128)S(1)} %bitcast.13, s32[8,1024]{1,0:T(8,128)S(1)} %bitcast.15), custom_call_target="tpu_custom_call" | custom-call | tf_op jit(solution)/shard_map/local_gram/pallas_call | solution.py:430
  4.7 0.5 collective-permute-start
  5.2 1.2 %collective-permute-done = f32[560,128]{1,0:T(8,128)S(1)} collective-permute-done((f32[560,128]{1,0:T(8,128)S(1)}, f32[560,128]{1,0:T(8,128)S(1)}, u32[]{:S(2)}, u32[]{:S(2)}) %collective-permute-start) | collective-permute-done | bytes 286752 | tf_op jit(solution)/shard_map/ppermute | solution.py:384
  6.5 2.9 %collective-permute-start.1 = (f32[280,128]{1,0:T(8,128)S(1)}, f32[280,128]{1,0:T(8,128)S(1)}, u32[]{:S(2)}, u32[]{:S(2)}) collective-permute-start(f32[280,128]{1,0:T(8,128)S(1)} %slice_select_fusion.1), channel_id=1, source_target_pairs={{0,4},{2,6},{4,0},{6,2},{8,12},{10,14},{12,8},{14,10},{16,20},{18,... | collective-permute-start | bytes 430088 | tf_op jit(solution)/shard_map/ppermute | solution.py:384
  9.4 4.1 %collective-permute-done.1 = f32[280,128]{1,0:T(8,128)S(1)} collective-permute-done((f32[280,128]{1,0:T(8,128)S(1)}, f32[280,128]{1,0:T(8,128)S(1)}, u32[]{:S(2)}, u32[]{:S(2)}) %collective-permute-start.1) | collective-permute-done | bytes 143392 | tf_op jit(solution)/shard_map/ppermute | solution.py:384
  13.5 1.9 %collective-permute-start.2 = (f32[280,128]{1,0:T(8,128)S(1)}, f32[280,128]{1,0:T(8,128)S(1)}, u32[]{:S(2)}, u32[]{:S(2)}) collective-permute-start(f32[280,128]{1,0:T(8,128)S(1)} %select_add_fusion.1), channel_id=1, source_target_pairs={{0,8},{2,10},{4,12},{6,14},{8,0},{10,2},{12,4},{14,6},{16,24},{18,... | collective-permute-start | bytes 430088 | tf_op jit(solution)/shard_map/ppermute | solution.py:384
  15.4 3.5 %collective-permute-done.2 = f32[280,128]{1,0:T(8,128)S(1)} collective-permute-done((f32[280,128]{1,0:T(8,128)S(1)}, f32[280,128]{1,0:T(8,128)S(1)}, u32[]{:S(2)}, u32[]{:S(2)}) %collective-permute-start.2) | collective-permute-done | bytes 143392 | tf_op jit(solution)/shard_map/ppermute | solution.py:384
  18.9 2.7 %collective-permute-start.3 = (f32[280,128]{1,0:T(8,128)S(1)}, f32[280,128]{1,0:T(8,128)S(1)}, u32[]{:S(2)}, u32[]{:S(2)}) collective-permute-start(f32[280,128]{1,0:T(8,128)S(1)} %add.31), channel_id=1, source_target_pairs={{0,16},{2,18},{4,20},{6,22},{8,24},{10,26},{12,28},{14,30},{16,0},... | collective-permute-start | bytes 430088 | tf_op jit(solution)/shard_map/ppermute | solution.py:384
  21.6 5.7 %collective-permute-done.3 = f32[280,128]{1,0:T(8,128)S(1)} collective-permute-done((f32[280,128]{1,0:T(8,128)S(1)}, f32[280,128]{1,0:T(8,128)S(1)}, u32[]{:S(2)}, u32[]{:S(2)}) %collective-permute-start.3) | collective-permute-done | bytes 143392 | tf_op jit(solution)/shard_map/ppermute | solution.py:384
  27.4 1.0 %collective-permute-start.4 = (f32[280,128]{1,0:T(8,128)S(1)}, f32[280,128]{1,0:T(8,128)S(1)}, u32[]{:S(2)}, u32[]{:S(2)}) collective-permute-start(f32[280,128]{1,0:T(8,128)S(1)} %add.32), channel_id=1, source_target_pairs={{0,4},{2,6},{4,0},{6,2},{8,12},{10,14},{12,8},{14,10},{16,20},{18,... | collective-permute-start | bytes 430088 | tf_op jit(solution)/shard_map/ppermute | solution.py:384
  28.4 4.1 %collective-permute-done.4 = f32[280,128]{1,0:T(8,128)S(1)} collective-permute-done((f32[280,128]{1,0:T(8,128)S(1)}, f32[280,128]{1,0:T(8,128)S(1)}, u32[]{:S(2)}, u32[]{:S(2)}) %collective-permute-start.4) | collective-permute-done | bytes 143392 | tf_op jit(solution)/shard_map/ppermute | solution.py:384
  32.7 0.6 copy-done.6
  33.4 0.9 %collective-permute-done.5 = f32[560,128]{1,0:T(8,128)S(1)} collective-permute-done((f32[560,128]{1,0:T(8,128)S(1)}, f32[560,128]{1,0:T(8,128)S(1)}, u32[]{:S(2)}, u32[]{:S(2)}) %collective-permute-start.5) | collective-permute-done | bytes 286752 | tf_op jit(solution)/shard_map/ppermute | solution.py:384
  34.3 25.6 %ridge_fits.1 = (f32[3,8,512]{2,1,0:T(8,128)S(1)}, f32[8,128]{1,0:T(8,128)S(1)}, f32[8,512]{1,0:T(8,128)S(1)}) custom-call(f32[3]{0:T(128)S(1)} %broadcast_select_fusion.4.penalty, f32[1120,128]{1,0:T(8,128)S(1)} %pad_maximum_fusion.packed), custom_call_target="tpu_custom_call" | custom-call | tf_op jit(solution)/shard_map/ridge_fits/pallas_call | solution.py:451
  60.0 0.2 collective-permute-start.6
  60.1 0.1 pad_add_fusion.place
  60.2 1.0 %collective-permute-done.6.other = f32[3,8,512]{2,1,0:T(8,128)S(1)} collective-permute-done((f32[3,8,512]{2,1,0:T(8,128)S(1)}, f32[3,8,512]{2,1,0:T(8,128)S(1)}, u32[]{:S(2)}, u32[]{:S(2)}) %collective-permute-start.6) | collective-permute-done | bytes 49184 | tf_op jit(solution)/shard_map/ppermute | solution.py:384
  61.2 0.9 %predictions.1 = f32[2,24,1024]{2,1,0:T(8,128)S(1)} custom-call(s32[2]{0:T(128)S(1)} %pad_add_fusion.place, f32[3,8,512]{2,1,0:T(8,128)S(1)} %get-tuple-element.10.mine, f32[3,8,512]{2,1,0:T(8,128)S(1)} %collective-permute-done.6.other, f32[8,512]{1,0:T(8,128)S(1)} %get-tuple-element.11.centre, bf16[512,1024]{1,0:T(8,128)(2,1)S(1)} %get-tuple-element.12.padded), custom_call_target="tpu_custom_call" | custom-call | tf_op jit(solution)/shard_map/predictions/pallas_call | solution.py:468
  62.2 1.1 %collective-permute-start.7 = (f32[24,1024]{1,0:T(8,128)S(1)}, f32[24,1024]{1,0:T(8,128)S(1)}, u32[]{:S(2)}, u32[]{:S(2)}) collective-permute-start(f32[24,1024]{1,0:T(8,128)S(1)} %get-tuple-element.20), channel_id=1, source_target_pairs={{0,1},{1,0},{2,3},{3,2},{4,5},{5,4},{6,7},{7,6},{8,9},{9,8},{10,11... | collective-permute-start | bytes 294920 | tf_op jit(solution)/shard_map/ppermute | solution.py:384
  63.2 3.9 %collective-permute-done.7.other = f32[24,1024]{1,0:T(8,128)S(1)} collective-permute-done((f32[24,1024]{1,0:T(8,128)S(1)}, f32[24,1024]{1,0:T(8,128)S(1)}, u32[]{:S(2)}, u32[]{:S(2)}) %collective-permute-start.7) | collective-permute-done | bytes 98336 | tf_op jit(solution)/shard_map/ppermute | solution.py:384
  67.1 2.2 %stacking.1 = f32[16,256]{1,0:T(8,128)S(1)} custom-call(s32[2]{0:T(128)S(1)} %pad_add_fusion.place, f32[24,1024]{1,0:T(8,128)S(1)} %get-tuple-element.21.mine, f32[24,1024]{1,0:T(8,128)S(1)} %collective-permute-done.7.other, f32[8,128]{1,0:T(8,128)S(1)} %get-tuple-element.13.stats, f32[8,1024]{1,0:T(8,128)S(1)} %bitcast.14, s32[8,1024]{1,0:T(8,128)S(1)} %bitcast.16, ...), custom_call_target="tpu_custom_call" | custom-call | tf_op jit(solution)/shard_map/stacking/pallas_call | solution.py:485
  69.4 1.2 %collective-permute-done.8 = f32[16,256]{1,0:T(8,128)S(1)} collective-permute-done((f32[16,256]{1,0:T(8,128)S(1)}, f32[16,256]{1,0:T(8,128)S(1)}, u32[]{:S(2)}, u32[]{:S(2)}) %collective-permute-start.8) | collective-permute-done | bytes 16416 | tf_op jit(solution)/shard_map/ppermute | solution.py:384
  70.6 1.0 %collective-permute-start.9 = (f32[16,256]{1,0:T(8,128)S(1)}, f32[16,256]{1,0:T(8,128)S(1)}, u32[]{:S(2)}, u32[]{:S(2)}) collective-permute-start(f32[16,256]{1,0:T(8,128)S(1)} %add.33), channel_id=1, source_target_pairs={{0,4},{2,6},{4,0},{6,2},{8,12},{10,14},{12,8},{14,10},{16,20},{18,... | collective-permute-start | bytes 49160 | tf_op jit(solution)/shard_map/ppermute | solution.py:384
  71.6 2.8 %collective-permute-done.9 = f32[16,256]{1,0:T(8,128)S(1)} collective-permute-done((f32[16,256]{1,0:T(8,128)S(1)}, f32[16,256]{1,0:T(8,128)S(1)}, u32[]{:S(2)}, u32[]{:S(2)}) %collective-permute-start.9) | collective-permute-done | bytes 16416 | tf_op jit(solution)/shard_map/ppermute | solution.py:384
  74.3 0.2 collective-permute-start.10
  74.5 3.6 %collective-permute-done.10 = f32[16,256]{1,0:T(8,128)S(1)} collective-permute-done((f32[16,256]{1,0:T(8,128)S(1)}, f32[16,256]{1,0:T(8,128)S(1)}, u32[]{:S(2)}, u32[]{:S(2)}) %collective-permute-start.10) | collective-permute-done | bytes 16416 | tf_op jit(solution)/shard_map/ppermute | solution.py:384
  78.1 1.5 %collective-permute-start.11 = (f32[16,256]{1,0:T(8,128)S(1)}, f32[16,256]{1,0:T(8,128)S(1)}, u32[]{:S(2)}, u32[]{:S(2)}) collective-permute-start(f32[16,256]{1,0:T(8,128)S(1)} %add.35), channel_id=1, source_target_pairs={{0,16},{2,18},{4,20},{6,22},{8,24},{10,26},{12,28},{14,30},{16,0},... | collective-permute-start | bytes 49160 | tf_op jit(solution)/shard_map/ppermute | solution.py:384
  79.6 3.3 %collective-permute-done.11 = f32[16,256]{1,0:T(8,128)S(1)} collective-permute-done((f32[16,256]{1,0:T(8,128)S(1)}, f32[16,256]{1,0:T(8,128)S(1)}, u32[]{:S(2)}, u32[]{:S(2)}) %collective-permute-start.11) | collective-permute-done | bytes 16416 | tf_op jit(solution)/shard_map/ppermute | solution.py:384
  82.9 1.2 %standardize.1 = (f32[5,10,4,10]{3,2,1,0:T(4,128)}, f32[5,4,10]{2,1,0:T(4,128)}) custom-call(f32[16,256]{1,0:T(8,128)S(1)} %add.36.total), custom_call_target="tpu_custom_call" | custom-call | tf_op jit(solution)/shard_map/standardize/pallas_call | solution.py:493
  (30 shorter events, 0.5 us)
Async XLA Ops:
  0.6 1.2 %copy-start = (bf16[1024,500]{0,1:T(8,128)(2,1)S(1)}, bf16[1024,500]{0,1:T(8,128)(2,1)}, u32[]{:S(2)}) copy-start(bf16[1024,500]{0,1:T(8,128)(2,1)} %param.6) | copy-start | bytes 3072004
  1.9 0.8 copy-start.1
  2.6 0.8 copy-start.3
  4.7 1.7 %collective-permute-start = (f32[560,128]{1,0:T(8,128)S(1)}, f32[560,128]{1,0:T(8,128)S(1)}, u32[]{:S(2)}, u32[]{:S(2)}) collective-permute-start(f32[560,128]{1,0:T(8,128)S(1)} %slice_select_fusion), channel_id=1, source_target_pairs={{0,2},{2,0},{4,6},{6,4},{8,10},{10,8},{12,14},{14,12},{16,18},{18,... | collective-permute-start | bytes 860168 | tf_op jit(solution)/shard_map/ppermute | solution.py:384
  6.5 7.0 %collective-permute-start.1 = (f32[280,128]{1,0:T(8,128)S(1)}, f32[280,128]{1,0:T(8,128)S(1)}, u32[]{:S(2)}, u32[]{:S(2)}) collective-permute-start(f32[280,128]{1,0:T(8,128)S(1)} %slice_select_fusion.1), channel_id=1, source_target_pairs={{0,4},{2,6},{4,0},{6,2},{8,12},{10,14},{12,8},{14,10},{16,20},{18,... | collective-permute-start | bytes 430088 | tf_op jit(solution)/shard_map/ppermute | solution.py:384
  13.5 5.4 %collective-permute-start.2 = (f32[280,128]{1,0:T(8,128)S(1)}, f32[280,128]{1,0:T(8,128)S(1)}, u32[]{:S(2)}, u32[]{:S(2)}) collective-permute-start(f32[280,128]{1,0:T(8,128)S(1)} %select_add_fusion.1), channel_id=1, source_target_pairs={{0,8},{2,10},{4,12},{6,14},{8,0},{10,2},{12,4},{14,6},{16,24},{18,... | collective-permute-start | bytes 430088 | tf_op jit(solution)/shard_map/ppermute | solution.py:384
  18.9 8.4 %collective-permute-start.3 = (f32[280,128]{1,0:T(8,128)S(1)}, f32[280,128]{1,0:T(8,128)S(1)}, u32[]{:S(2)}, u32[]{:S(2)}) collective-permute-start(f32[280,128]{1,0:T(8,128)S(1)} %add.31), channel_id=1, source_target_pairs={{0,16},{2,18},{4,20},{6,22},{8,24},{10,26},{12,28},{14,30},{16,0},... | collective-permute-start | bytes 430088 | tf_op jit(solution)/shard_map/ppermute | solution.py:384
  27.4 5.2 %collective-permute-start.4 = (f32[280,128]{1,0:T(8,128)S(1)}, f32[280,128]{1,0:T(8,128)S(1)}, u32[]{:S(2)}, u32[]{:S(2)}) collective-permute-start(f32[280,128]{1,0:T(8,128)S(1)} %add.32), channel_id=1, source_target_pairs={{0,4},{2,6},{4,0},{6,2},{8,12},{10,14},{12,8},{14,10},{16,20},{18,... | collective-permute-start | bytes 430088 | tf_op jit(solution)/shard_map/ppermute | solution.py:384
  32.6 1.6 %collective-permute-start.5 = (f32[560,128]{1,0:T(8,128)S(1)}, f32[560,128]{1,0:T(8,128)S(1)}, u32[]{:S(2)}, u32[]{:S(2)}) collective-permute-start(f32[560,128]{1,0:T(8,128)S(1)} %pad_maximum_fusion.1), channel_id=1, source_target_pairs={{0,2},{2,0},{4,6},{6,4},{8,10},{10,8},{12,14},{14,12},{16,18},{18,... | collective-permute-start | bytes 860168 | tf_op jit(solution)/shard_map/ppermute | solution.py:384
  32.7 0.7 copy-start.6
  32.7 0.7 copy-start.7
  60.0 1.3 %collective-permute-start.6 = (f32[3,8,512]{2,1,0:T(8,128)S(1)}, f32[3,8,512]{2,1,0:T(8,128)S(1)}, u32[]{:S(2)}, u32[]{:S(2)}) collective-permute-start(f32[3,8,512]{2,1,0:T(8,128)S(1)} %get-tuple-element.10.mine), channel_id=1, source_target_pairs={{0,2},{2,0},{4,6},{6,4},{8,10},{10,8},{12,14},{14,12},{16,18},{18,... | collective-permute-start | bytes 147464 | tf_op jit(solution)/shard_map/ppermute | solution.py:384
  62.1 5.0 %copy-start.2 = (f32[1024,8]{0,1:T(8,128)S(1)}, f32[1024,8]{0,1:T(8,128)}, u32[]{:S(2)}) copy-start(f32[1024,8]{0,1:T(8,128)} %param.7) | copy-start | bytes 98308
  62.1 5.0 %copy-start.4 = (s32[1024,8]{0,1:T(8,128)S(1)}, s32[1024,8]{0,1:T(8,128)}, u32[]{:S(2)}) copy-start(s32[1024,8]{0,1:T(8,128)} %param.8) | copy-start | bytes 98308
  62.2 5.0 %copy-start.5 = (s32[1024]{0:T(1024)S(1)}, s32[1024]{0:T(1024)}, u32[]{:S(2)}) copy-start(s32[1024]{0:T(1024)} %param.9) | copy-start | bytes 12292
  62.2 4.9 %collective-permute-start.7 = (f32[24,1024]{1,0:T(8,128)S(1)}, f32[24,1024]{1,0:T(8,128)S(1)}, u32[]{:S(2)}, u32[]{:S(2)}) collective-permute-start(f32[24,1024]{1,0:T(8,128)S(1)} %get-tuple-element.20), channel_id=1, source_target_pairs={{0,1},{1,0},{2,3},{3,2},{4,5},{5,4},{6,7},{7,6},{8,9},{9,8},{10,11... | collective-permute-start | bytes 294920 | tf_op jit(solution)/shard_map/ppermute | solution.py:384
  69.4 1.2 %collective-permute-start.8 = (f32[16,256]{1,0:T(8,128)S(1)}, f32[16,256]{1,0:T(8,128)S(1)}, u32[]{:S(2)}, u32[]{:S(2)}) collective-permute-start(f32[16,256]{1,0:T(8,128)S(1)} %stacking.1), channel_id=1, source_target_pairs={{0,2},{2,0},{4,6},{6,4},{8,10},{10,8},{12,14},{14,12},{16,18},{18,... | collective-permute-start | bytes 49160 | tf_op jit(solution)/shard_map/ppermute | solution.py:384
  70.6 3.7 %collective-permute-start.9 = (f32[16,256]{1,0:T(8,128)S(1)}, f32[16,256]{1,0:T(8,128)S(1)}, u32[]{:S(2)}, u32[]{:S(2)}) collective-permute-start(f32[16,256]{1,0:T(8,128)S(1)} %add.33), channel_id=1, source_target_pairs={{0,4},{2,6},{4,0},{6,2},{8,12},{10,14},{12,8},{14,10},{16,20},{18,... | collective-permute-start | bytes 49160 | tf_op jit(solution)/shard_map/ppermute | solution.py:384
  74.3 3.7 %collective-permute-start.10 = (f32[16,256]{1,0:T(8,128)S(1)}, f32[16,256]{1,0:T(8,128)S(1)}, u32[]{:S(2)}, u32[]{:S(2)}) collective-permute-start(f32[16,256]{1,0:T(8,128)S(1)} %add.34), channel_id=1, source_target_pairs={{0,8},{2,10},{4,12},{6,14},{8,0},{10,2},{12,4},{14,6},{16,24},{18,... | collective-permute-start | bytes 49160 | tf_op jit(solution)/shard_map/ppermute | solution.py:384
  78.1 4.8 %collective-permute-start.11 = (f32[16,256]{1,0:T(8,128)S(1)}, f32[16,256]{1,0:T(8,128)S(1)}, u32[]{:S(2)}, u32[]{:S(2)}) collective-permute-start(f32[16,256]{1,0:T(8,128)S(1)} %add.35), channel_id=1, source_target_pairs={{0,16},{2,18},{4,20},{6,22},{8,24},{10,26},{12,28},{14,30},{16,0},... | collective-permute-start | bytes 49160 | tf_op jit(solution)/shard_map/ppermute | solution.py:384

commit v3 on v2

--- a/solution.py
+++ b/solution.py
@@ -45,20 +45,23 @@
     return lax.broadcasted_iota(jnp.int32, shape, dim)
 
 
-def dot_six(a, b, dims=NN):
-    if dims == TN:
-        a, dims = jnp.transpose(a), NN
-    (along_a,), (along_b,) = dims[0]
-    high_a, middle_a, low_a = split_three(a)
-    high_b, middle_b, low_b = split_three(b)
-
-    def part(x, y):
-        return dot_bf16(jnp.concatenate(x, along_a), jnp.concatenate(y, along_b), dims)
-
-    small = part([low_a, middle_a], [high_b, middle_b])
-    return (small + part([middle_a, high_a], [high_b, middle_b])) + part(
-        [high_a, high_a], [low_b, high_b]
-    )
+def left_parts(value):
+    high, middle, low = split_three(value)
+    return [jnp.concatenate(pair, 1) for pair in ((low, middle), (middle, high), (high, high))]
+
+
+def right_parts(value):
+    high, middle, low = split_three(value)
+    first = jnp.concatenate([high, middle], 0)
+    return [first, first, jnp.concatenate([low, high], 0)]
+
+
+def products(lefts, rights):
+    totals = [dot_bf16(a[0], b[0]) for a, b in zip(lefts, rights)]
+    for part in (1, 2):
+        terms = [dot_bf16(a[part], b[part]) for a, b in zip(lefts, rights)]
+        totals = [total + term for total, term in zip(totals, terms)]
+    return totals
 
 
 def block_rows(tiles):
@@ -87,7 +90,13 @@
     )
 
 
-def gram_kernel(markers, dosage, traits, observed, packed, padded):
+def gram_kernel(markers, dosage, traits, observed, packed, padded, held, seen, arrived):
+    copies = [
+        pltpu.make_async_copy(traits, held, arrived.at[0]),
+        pltpu.make_async_copy(observed, seen, arrived.at[1]),
+    ]
+    for copy in copies:
+        copy.start()
     width, rows = padded.shape
     tiles = width // TILE
     place, side = block_rows(tiles)
@@ -98,18 +107,10 @@
     padded[edge:edge + 16, :] = tail.astype(jnp.bfloat16)
     if edge + 16 < width:
         padded[edge + 16:, :] = jnp.zeros((width - edge - 16, rows), jnp.bfloat16)
-    values = traits[...]
-    present = observed[...].astype(jnp.float32)
-    masked = present * values
-    high, middle, low = (part.astype(jnp.float32) for part in split_three(masked))
-    ones = jnp.ones(present.shape, jnp.float32)
-    extra = jnp.concatenate([high, middle, low, present, ones, ones], 0).astype(jnp.bfloat16)
-    products = dot_bf16(extra, padded[...], NT)
-    sums = [jnp.sum(v, axis=1, keepdims=True) for v in (present, masked, masked * values)]
     lane, line = iota((TRAITS, TILE), 1), iota((TRAITS, TILE), 0)
     upper = iota((TILE, TILE), 0) <= iota((TILE, TILE), 1)
     eye = iota((TILE, TILE), 0) == iota((TILE, TILE), 1)
-    even = None
+    even, diagonals = None, []
     for i in range(tiles):
         here = dot_bf16(padded[i * TILE:(i + 1) * TILE, :], padded[i * TILE:, :], NT)
         for j in range(i + 1, tiles):
@@ -118,7 +119,18 @@
         if i % 2:
             packed[place[i, i]:place[i, i] + TILE, :] = jnp.where(upper, even, block)
         even = block
-        diagonal = jnp.sum(jnp.where(eye, block, 0.0), axis=0, keepdims=True)
+        diagonals.append(jnp.sum(jnp.where(eye, block, 0.0), axis=0, keepdims=True))
+    for copy in copies:
+        copy.wait()
+    values = held[...]
+    present = seen[...].astype(jnp.float32)
+    masked = present * values
+    high, middle, low = (part.astype(jnp.float32) for part in split_three(masked))
+    ones = jnp.ones(present.shape, jnp.float32)
+    extra = jnp.concatenate([high, middle, low, present, ones, ones], 0).astype(jnp.bfloat16)
+    products = dot_bf16(extra, padded[...], NT)
+    sums = [jnp.sum(v, axis=1, keepdims=True) for v in (present, masked, masked * values)]
+    for i in range(tiles):
         cols = slice(i * TILE, (i + 1) * TILE)
         row = side + SIDE * i
         total = products[0:8, cols] + products[8:16, cols] + products[16:24, cols]
@@ -127,13 +139,14 @@
                 total = jnp.where(lane == TILE - 1 - n, value, total)
         packed[row:row + 8, :] = total
         packed[row + 8:row + 16, :] = products[24:32, cols]
-        packed[row + 16:row + 24, :] = jnp.where(line == 0, products[32:40, cols], diagonal)
-
-
-def eliminate(work, old, fits):
+        packed[row + 16:row + 24, :] = jnp.where(line == 0, products[32:40, cols], diagonals[i])
+
+
+def eliminate(work, old, count):
+    fits = work.shape[0]
     shape = (fits, STEP, TILE)
     row, lane = iota(shape, 1), iota(shape, 2)
-    count, per = TILE // STEP, SUB // STEP
+    per = SUB // STEP
     for t in range(count):
         base = t * STEP
         panel = work[:, base:base + STEP, :]
@@ -155,7 +168,7 @@
         panel = panel * scale
         work[:, base:base + STEP, :] = panel
         rows = [jnp.broadcast_to(panel[:, q:q + 1, :], shape) for q in range(STEP)]
-        stop = (t // per + 1) * per
+        stop = min((t // per + 1) * per, count)
         for g in range(t + 1, stop):
             other = work[:, g * STEP:(g + 1) * STEP, :]
             total = jnp.where(inside, 0.0, other)
@@ -180,14 +193,11 @@
                 )
                 rest = work[f, last:, :]
                 work[f, last:, :] = jnp.where(done, 0.0, rest) - product[last:, :]
-    lower = iota(old.shape, 2) // STEP <= iota(old.shape, 1) // STEP
-    old[...] = jnp.where(lower, old[...], 0.0)
-    work[...] = jnp.where(lower, work[...], 0.0)
-
-
-def fit_kernel(samples, markers, penalty, packed, out, stats, centre, grid, wide, work, old, rhs):
+
+
+def fit_kernel(samples, markers, penalty, packed, out, stats, centre, grid, wide, work, old):
     fits = work.shape[0]
-    tiles = rhs.shape[-1] // TILE
+    tiles = out.shape[-1] // TILE
     end = tiles * TILE
     place, side = block_rows(tiles)
 
@@ -207,6 +217,7 @@
     share = 1.0 / samples
     totals = [part(i, 2)[0:1, :] for i in range(tiles)]
     squares = []
+    blank = jnp.zeros((TILE - TRAITS, TILE), jnp.float32)
     for i in range(tiles):
         mine = slice(i * TILE, (i + 1) * TILE)
         column = jnp.transpose(jnp.broadcast_to(totals[i], (TILE, TILE)))
@@ -223,12 +234,12 @@
                     block = jnp.where(eye, diagonal, block)
                 else:
                     block = jnp.where(upper, block, turned)
-            grid[i, :, j * TILE:(j + 1) * TILE] = block - column * totals[j] * share
-        side_i = (part(i, 0) - part(i, 1) * mean) / spread
-        if i == tiles - 1:
-            side_i = jnp.where(lane + i * TILE < markers, side_i, 0.0)
-        for f in range(fits):
-            rhs[f, :, mine] = side_i
+            block = block - column * totals[j] * share
+            if j == tiles - 1:
+                value = (part(i, 0) - part(i, 1) * mean) / spread
+                value = jnp.where(lane + i * TILE < markers, value, 0.0)
+                block = block + jnp.transpose(jnp.concatenate([blank, value], 0))
+            grid[i, :, j * TILE:(j + 1) * TILE] = block
 
     def ridge(i, f):
         value = jnp.where(line + i * TILE < markers, penalty[f] * squares[i], 1.0)
@@ -236,43 +247,51 @@
 
     for f in range(fits):
         work[f] = grid[0, :, 0:TILE] + ridge(0, f)
+    every = range(fits)
+    count = TILE // STEP
     for k in range(tiles):
         lo, hi = k * TILE, (k + 1) * TILE
-        eliminate(work, old, fits)
-        lefts, rights = [old[f] for f in range(fits)], [work[f] for f in range(fits)]
-        both = None
+        pivots = count if hi < end else count - 1
+        eliminate(work, old, pivots)
+        lower = jnp.logical_and(col // STEP <= row // STEP, row < pivots * STEP)
+        lefts = [jnp.where(lower, old[f], 0.0) for f in every]
         if hi < end:
-            above = [grid[0, :, hi:] if k == 0 else wide[f, k, :, hi:] for f in range(fits)]
-            both = [
-                dot_six(jnp.concatenate([lefts[f], rights[f]], 0), above[f]) for f in range(fits)
-            ]
-        for i in range(k + 1, tiles):
-            for f in range(fits):
+            rights = [jnp.where(lower, work[f], 0.0) for f in every]
+            above = [grid[0, :, hi:]] if k == 0 else [wide[f, k, :, hi:] for f in every]
+            above = [right_parts(value) for value in above] * (fits if k == 0 else 1)
+            stacked = [left_parts(jnp.concatenate([lefts[f], rights[f]], 0)) for f in every]
+            both = products(stacked, above)
+            factors = [left_parts(jnp.transpose(both[f][:TILE])) for f in every]
+            parts = [right_parts(both[f][TILE:]) for f in every]
+            for i in range(k + 1, tiles):
                 begin = i * TILE
-                left, weights = both[f][:TILE, begin - hi:begin - hi + TILE], both[f][TILE:, begin - hi:]
-                before = grid[i, :, begin:] if k == 0 else wide[f, i, :, begin:]
-                after = before - dot_six(left, weights, TN)
-                block = after[:, :TILE] + ridge(i, f) if k == 0 else after[:, :TILE]
-                if i == k + 1:
-                    work[f] = block
-                else:
-                    wide[f, i, :, begin:begin + TILE] = block
-                if i + 1 < tiles:
-                    wide[f, i, :, begin + TILE:] = after[:, TILE:]
-        for f in range(fits):
-            turned = dot(rhs[f, :, lo:hi], lefts[f], NT)
-            rhs[f, :, lo:hi] = dot(turned, rights[f])
+                after = products(
+                    [[p[begin - hi:begin - hi + TILE] for p in factors[f]] for f in every],
+                    [[p[:, begin - hi:] for p in parts[f]] for f in every],
+                )
+                for f in every:
+                    before = grid[i, :, begin:] if k == 0 else wide[f, i, :, begin:]
+                    value = before - after[f]
+                    block = value[:, :TILE] + ridge(i, f) if k == 0 else value[:, :TILE]
+                    if i == k + 1:
+                        work[f] = block
+                    else:
+                        wide[f, i, :, begin:begin + TILE] = block
+                    if i + 1 < tiles:
+                        wide[f, i, :, begin + TILE:] = value[:, TILE:]
+        else:
+            last = jnp.logical_and(row < pivots * STEP, col >= pivots * STEP)
+            parts = [right_parts(jnp.where(last, work[f], 0.0)) for f in every]
+        final = products([left_parts(jnp.transpose(left)) for left in lefts], parts)
+        for f in every:
             if hi < end:
-                weights = both[f][TILE:]
-                rhs[f, :, hi:] = rhs[f, :, hi:] - dot(turned, weights)
-                wide[f, k, :, hi:] = dot_six(lefts[f], weights, TN)
-    for k in reversed(range(tiles)):
-        for f in range(fits):
-            lo, hi = k * TILE, (k + 1) * TILE
-            value = rhs[f, :, lo:hi]
-            if hi < end:
-                value = value - dot(out[f, :, hi:], wide[f, k, :, hi:], NT)
-            out[f, :, lo:hi] = value
+                wide[f, k, :, hi:] = final[f]
+            out[f, :, lo:hi] = jnp.transpose(final[f][:, -TILE:])[TILE - TRAITS:, :]
+    for k in reversed(range(tiles - 1)):
+        lo, hi = k * TILE, (k + 1) * TILE
+        known = [dot(out[f, :, hi:], wide[f, k, :, hi:], NT) for f in every]
+        for f in every:
+            out[f, :, lo:hi] = out[f, :, lo:hi] - known[f]
 
 
 def predict_kernel(pairs, place, mine, other, centre, padded, out):
@@ -323,12 +342,18 @@
     spread = dot_bf16(
         jnp.where(pick, 1.0, 0.0).astype(jnp.bfloat16), present.astype(jnp.bfloat16)
     )
-    kept = levels * spread
-    left = [kept * jnp.where(folds[...] == k, 1.0, 0.0) for k in range(FOLDS)]
-    left = left + [jnp.zeros((width - FOLDS * count, samples), jnp.float32)]
-    left = jnp.concatenate(left, 0)
-    right = jnp.concatenate([levels, scaled], 0)
-    full = dot(right, left, NT)
+    masks = [
+        (spread * jnp.where(folds[...] == k, 1.0, 0.0)).astype(jnp.bfloat16) for k in range(FOLDS)
+    ]
+    right = split_three(jnp.concatenate([levels, scaled], 0))[:2]
+    none = jnp.zeros((width - FOLDS * count, samples), jnp.bfloat16)
+    left = [
+        jnp.concatenate([part * mask for mask in masks] + [none], 0)
+        for part in split_three(levels)[:2]
+    ]
+    full = dot_bf16(right[1], left[0], NT) + dot_bf16(
+        jnp.concatenate([right[0], right[0]], 1), jnp.concatenate([left[1], left[0]], 1), NT
+    )
     row, col = iota(full.shape, 0), iota(full.shape, 1)
     trait = jnp.where(row < count, row % per_share, row - count - first)
     full = jnp.where(trait == col % per_share, full, 0.0)
@@ -338,7 +363,9 @@
     group = jnp.where(slot % SLOTS < FITS, slot // SLOTS * FITS + slot % SLOTS, height)
     group = jnp.where(source < count, group, count // per_share // SLOTS * FITS)
     out[...] = dot(jnp.where(level == group, 1.0, 0.0), full)
-    energy = dot(jnp.ones((8, samples), jnp.float32), levels * levels, NT)
+    ones = jnp.ones((16, samples), jnp.bfloat16)
+    squares = split_three(levels * levels)
+    energy = dot_bf16(ones, squares[1], NT) + dot_bf16(ones, squares[0], NT)
     last = count // per_share // SLOTS * FITS + 1
     out[last:last + 1, 0:count] = energy[0:1, :]
 
@@ -379,6 +406,11 @@
             gram[k, l] = turned[row:row + per_share, 0:levels]
 
 
+def fit_scratch(fits, tiles, width):
+    shapes = [(tiles, TILE, width), (fits, tiles, TILE, width)] + [(fits, TILE, TILE)] * 2
+    return [pltpu.VMEM(shape, jnp.float32) for shape in shapes]
+
+
 def swap(value, axis, mask):
     size = lax.axis_size(axis)
     return lax.ppermute(value, axis, [(i, i ^ mask) for i in range(size)])
@@ -434,8 +466,13 @@
             f32((side + SIDE * tiles, TILE)),
             jax.ShapeDtypeStruct((width, local_rows), jnp.bfloat16),
         ],
-        in_specs=[whole((width, local_rows)), whole(traits.shape), whole(observed.shape)],
+        in_specs=[whole((width, local_rows))] + [pl.BlockSpec(memory_space=pltpu.HBM)] * 2,
         out_specs=[whole((side + SIDE * tiles, TILE)), whole((width, local_rows))],
+        scratch_shapes=[
+            pltpu.VMEM(traits.shape, traits.dtype),
+            pltpu.VMEM(observed.shape, observed.dtype),
+            pltpu.SemaphoreType.DMA((2,)),
+        ],
         compiler_params=pltpu.CompilerParams(vmem_limit_bytes=VMEM_BYTES),
         name="local_gram",
     )(genotypes.T, traits, observed)
@@ -452,13 +489,7 @@
         functools.partial(fit_kernel, samples, markers),
         [f32((HALF, TRAITS, width)), f32((TRAITS, TILE)), f32((8, width))],
         ["smem", "vmem"],
-        [
-            pltpu.VMEM((tiles, TILE, width), jnp.float32),
-            pltpu.VMEM((HALF, tiles, TILE, width), jnp.float32),
-            pltpu.VMEM((HALF, TILE, TILE), jnp.float32),
-            pltpu.VMEM((HALF, TILE, TILE), jnp.float32),
-            pltpu.VMEM((HALF, TRAITS, width), jnp.float32),
-        ],
+        fit_scratch(HALF, tiles, width),
         "ridge_fits",
     )(penalty, packed)
     other = swap(weights, "samp", 1)

time: 84.4 us -> 82.1 us (0.973)
  Pallas kernels: 31.2 us -> 29 us
    pallas_call x1, Pallas kernels: 25.6 us -> 24 us  [body(): call(functools.partial(fit_kernel, samples, markers), [f32((HALF, TRAITS,...]
where the time goes in v3:
time: 82.1 us; the launch traced here: 81.8 us
  waiting for transfers between devices  35.1 us (43%)
  Pallas kernels  29 us (35%)
  starting transfers between devices  13.1 us (16%)
  local copies, waits for them, and re-layouts  3.42 us (4%)
    ppermute x12, waiting for transfers between devices, swap(): return lax.ppermute(value, axis, [(i, i ^ mask) for i in range(size)])  35.1 us
    pallas_call x1, Pallas kernels, body(): call(functools.partial(fit_kernel, samples, markers), [f32((HALF, TRAITS,...  24 us
    ppermute x12, starting transfers between devices, swap(): return lax.ppermute(value, axis, [(i, i ^ mask) for i in range(size)])  13.1 us
    unnamed x16, local copies, waits for them, and re-layouts  3.4 us
  transfers between devices with their start and end apart: 12, of which 12 were waited for; matrix products, arithmetic and copies ran while one was open for 0% of the time, Pallas kernels for 0%

profile of v3, /device:TPU:0, one launch (start us, length us, event | category | flops | bytes accessed | tf_op | source)
XLA Modules:
  0.0 81.8 jit_solution(8995410384743521050)
XLA Ops:
  0.6 1.2 %copy-done = bf16[1024,500]{0,1:T(8,128)(2,1)S(1)} copy-done((bf16[1024,500]{0,1:T(8,128)(2,1)S(1)}, bf16[1024,500]{0,1:T(8,128)(2,1)}, u32[]{:S(2)}) %copy-start) | copy-done | bytes 1024024
  1.9 0.8 copy-done.1
  2.6 0.8 copy-done.3
  3.4 1.5 %local_gram.1 = (f32[1120,128]{1,0:T(8,128)S(1)}, bf16[512,1024]{1,0:T(8,128)(2,1)S(1)}) custom-call(bf16[500,1024]{1,0:T(8,128)(2,1)S(1)} %bitcast.12, f32[8,1024]{1,0:T(8,128)S(1)} %bitcast.13, s32[8,1024]{1,0:T(8,128)S(1)} %bitcast.15), custom_call_target="tpu_custom_call" | custom-call | tf_op jit(solution)/shard_map/local_gram/pallas_call | solution.py:462
  4.9 0.5 collective-permute-start
  5.4 1.2 %collective-permute-done = f32[560,128]{1,0:T(8,128)S(1)} collective-permute-done((f32[560,128]{1,0:T(8,128)S(1)}, f32[560,128]{1,0:T(8,128)S(1)}, u32[]{:S(2)}, u32[]{:S(2)}) %collective-permute-start) | collective-permute-done | bytes 286752 | tf_op jit(solution)/shard_map/ppermute | solution.py:416
  6.7 2.9 %collective-permute-start.1 = (f32[280,128]{1,0:T(8,128)S(1)}, f32[280,128]{1,0:T(8,128)S(1)}, u32[]{:S(2)}, u32[]{:S(2)}) collective-permute-start(f32[280,128]{1,0:T(8,128)S(1)} %slice_select_fusion.1), channel_id=1, source_target_pairs={{0,4},{2,6},{4,0},{6,2},{8,12},{10,14},{12,8},{14,10},{16,20},{18,... | collective-permute-start | bytes 430088 | tf_op jit(solution)/shard_map/ppermute | solution.py:416
  9.6 4.1 %collective-permute-done.1 = f32[280,128]{1,0:T(8,128)S(1)} collective-permute-done((f32[280,128]{1,0:T(8,128)S(1)}, f32[280,128]{1,0:T(8,128)S(1)}, u32[]{:S(2)}, u32[]{:S(2)}) %collective-permute-start.1) | collective-permute-done | bytes 143392 | tf_op jit(solution)/shard_map/ppermute | solution.py:416
  13.7 1.9 %collective-permute-start.2 = (f32[280,128]{1,0:T(8,128)S(1)}, f32[280,128]{1,0:T(8,128)S(1)}, u32[]{:S(2)}, u32[]{:S(2)}) collective-permute-start(f32[280,128]{1,0:T(8,128)S(1)} %select_add_fusion.1), channel_id=1, source_target_pairs={{0,8},{2,10},{4,12},{6,14},{8,0},{10,2},{12,4},{14,6},{16,24},{18,... | collective-permute-start | bytes 430088 | tf_op jit(solution)/shard_map/ppermute | solution.py:416
  15.6 3.5 %collective-permute-done.2 = f32[280,128]{1,0:T(8,128)S(1)} collective-permute-done((f32[280,128]{1,0:T(8,128)S(1)}, f32[280,128]{1,0:T(8,128)S(1)}, u32[]{:S(2)}, u32[]{:S(2)}) %collective-permute-start.2) | collective-permute-done | bytes 143392 | tf_op jit(solution)/shard_map/ppermute | solution.py:416
  19.1 2.7 %collective-permute-start.3 = (f32[280,128]{1,0:T(8,128)S(1)}, f32[280,128]{1,0:T(8,128)S(1)}, u32[]{:S(2)}, u32[]{:S(2)}) collective-permute-start(f32[280,128]{1,0:T(8,128)S(1)} %add.31), channel_id=1, source_target_pairs={{0,16},{2,18},{4,20},{6,22},{8,24},{10,26},{12,28},{14,30},{16,0},... | collective-permute-start | bytes 430088 | tf_op jit(solution)/shard_map/ppermute | solution.py:416
  21.8 5.7 %collective-permute-done.3 = f32[280,128]{1,0:T(8,128)S(1)} collective-permute-done((f32[280,128]{1,0:T(8,128)S(1)}, f32[280,128]{1,0:T(8,128)S(1)}, u32[]{:S(2)}, u32[]{:S(2)}) %collective-permute-start.3) | collective-permute-done | bytes 143392 | tf_op jit(solution)/shard_map/ppermute | solution.py:416
  27.5 1.0 %collective-permute-start.4 = (f32[280,128]{1,0:T(8,128)S(1)}, f32[280,128]{1,0:T(8,128)S(1)}, u32[]{:S(2)}, u32[]{:S(2)}) collective-permute-start(f32[280,128]{1,0:T(8,128)S(1)} %add.32), channel_id=1, source_target_pairs={{0,4},{2,6},{4,0},{6,2},{8,12},{10,14},{12,8},{14,10},{16,20},{18,... | collective-permute-start | bytes 430088 | tf_op jit(solution)/shard_map/ppermute | solution.py:416
  28.6 4.1 %collective-permute-done.4 = f32[280,128]{1,0:T(8,128)S(1)} collective-permute-done((f32[280,128]{1,0:T(8,128)S(1)}, f32[280,128]{1,0:T(8,128)S(1)}, u32[]{:S(2)}, u32[]{:S(2)}) %collective-permute-start.4) | collective-permute-done | bytes 143392 | tf_op jit(solution)/shard_map/ppermute | solution.py:416
  32.9 0.6 copy-done.6
  33.5 0.9 %collective-permute-done.5 = f32[560,128]{1,0:T(8,128)S(1)} collective-permute-done((f32[560,128]{1,0:T(8,128)S(1)}, f32[560,128]{1,0:T(8,128)S(1)}, u32[]{:S(2)}, u32[]{:S(2)}) %collective-permute-start.5) | collective-permute-done | bytes 286752 | tf_op jit(solution)/shard_map/ppermute | solution.py:416
  34.5 24.0 %ridge_fits.1 = (f32[3,8,512]{2,1,0:T(8,128)S(1)}, f32[8,128]{1,0:T(8,128)S(1)}, f32[8,512]{1,0:T(8,128)S(1)}) custom-call(f32[3]{0:T(128)S(1)} %broadcast_select_fusion.4.penalty, f32[1120,128]{1,0:T(8,128)S(1)} %pad_maximum_fusion.packed), custom_call_target="tpu_custom_call" | custom-call | tf_op jit(solution)/shard_map/ridge_fits/pallas_call | solution.py:488
  58.4 0.2 collective-permute-start.6
  58.6 0.1 pad_add_fusion.place
  58.7 1.0 %collective-permute-done.6.other = f32[3,8,512]{2,1,0:T(8,128)S(1)} collective-permute-done((f32[3,8,512]{2,1,0:T(8,128)S(1)}, f32[3,8,512]{2,1,0:T(8,128)S(1)}, u32[]{:S(2)}, u32[]{:S(2)}) %collective-permute-start.6) | collective-permute-done | bytes 49184 | tf_op jit(solution)/shard_map/ppermute | solution.py:416
  59.7 0.9 %predictions.1 = f32[2,24,1024]{2,1,0:T(8,128)S(1)} custom-call(s32[2]{0:T(128)S(1)} %pad_add_fusion.place, f32[3,8,512]{2,1,0:T(8,128)S(1)} %get-tuple-element.10.mine, f32[3,8,512]{2,1,0:T(8,128)S(1)} %collective-permute-done.6.other, f32[8,512]{1,0:T(8,128)S(1)} %get-tuple-element.11.centre, bf16[512,1024]{1,0:T(8,128)(2,1)S(1)} %get-tuple-element.12.padded), custom_call_target="tpu_custom_call" | custom-call | tf_op jit(solution)/shard_map/predictions/pallas_call | solution.py:499
  60.6 1.1 %collective-permute-start.7 = (f32[24,1024]{1,0:T(8,128)S(1)}, f32[24,1024]{1,0:T(8,128)S(1)}, u32[]{:S(2)}, u32[]{:S(2)}) collective-permute-start(f32[24,1024]{1,0:T(8,128)S(1)} %get-tuple-element.20), channel_id=1, source_target_pairs={{0,1},{1,0},{2,3},{3,2},{4,5},{5,4},{6,7},{7,6},{8,9},{9,8},{10,11... | collective-permute-start | bytes 294920 | tf_op jit(solution)/shard_map/ppermute | solution.py:416
  61.7 3.9 %collective-permute-done.7.other = f32[24,1024]{1,0:T(8,128)S(1)} collective-permute-done((f32[24,1024]{1,0:T(8,128)S(1)}, f32[24,1024]{1,0:T(8,128)S(1)}, u32[]{:S(2)}, u32[]{:S(2)}) %collective-permute-start.7) | collective-permute-done | bytes 98336 | tf_op jit(solution)/shard_map/ppermute | solution.py:416
  65.6 1.5 %stacking.1 = f32[16,256]{1,0:T(8,128)S(1)} custom-call(s32[2]{0:T(128)S(1)} %pad_add_fusion.place, f32[24,1024]{1,0:T(8,128)S(1)} %get-tuple-element.21.mine, f32[24,1024]{1,0:T(8,128)S(1)} %collective-permute-done.7.other, f32[8,128]{1,0:T(8,128)S(1)} %get-tuple-element.13.stats, f32[8,1024]{1,0:T(8,128)S(1)} %bitcast.14, s32[8,1024]{1,0:T(8,128)S(1)} %bitcast.16, ...), custom_call_target="tpu_custom_call" | custom-call | tf_op jit(solution)/shard_map/stacking/pallas_call | solution.py:516
  67.1 1.2 %collective-permute-done.8 = f32[16,256]{1,0:T(8,128)S(1)} collective-permute-done((f32[16,256]{1,0:T(8,128)S(1)}, f32[16,256]{1,0:T(8,128)S(1)}, u32[]{:S(2)}, u32[]{:S(2)}) %collective-permute-start.8) | collective-permute-done | bytes 16416 | tf_op jit(solution)/shard_map/ppermute | solution.py:416
  68.3 1.0 %collective-permute-start.9 = (f32[16,256]{1,0:T(8,128)S(1)}, f32[16,256]{1,0:T(8,128)S(1)}, u32[]{:S(2)}, u32[]{:S(2)}) collective-permute-start(f32[16,256]{1,0:T(8,128)S(1)} %add.33), channel_id=1, source_target_pairs={{0,4},{2,6},{4,0},{6,2},{8,12},{10,14},{12,8},{14,10},{16,20},{18,... | collective-permute-start | bytes 49160 | tf_op jit(solution)/shard_map/ppermute | solution.py:416
  69.3 2.8 %collective-permute-done.9 = f32[16,256]{1,0:T(8,128)S(1)} collective-permute-done((f32[16,256]{1,0:T(8,128)S(1)}, f32[16,256]{1,0:T(8,128)S(1)}, u32[]{:S(2)}, u32[]{:S(2)}) %collective-permute-start.9) | collective-permute-done | bytes 16416 | tf_op jit(solution)/shard_map/ppermute | solution.py:416
  72.1 0.2 collective-permute-start.10
  72.3 3.6 %collective-permute-done.10 = f32[16,256]{1,0:T(8,128)S(1)} collective-permute-done((f32[16,256]{1,0:T(8,128)S(1)}, f32[16,256]{1,0:T(8,128)S(1)}, u32[]{:S(2)}, u32[]{:S(2)}) %collective-permute-start.10) | collective-permute-done | bytes 16416 | tf_op jit(solution)/shard_map/ppermute | solution.py:416
  75.8 1.5 %collective-permute-start.11 = (f32[16,256]{1,0:T(8,128)S(1)}, f32[16,256]{1,0:T(8,128)S(1)}, u32[]{:S(2)}, u32[]{:S(2)}) collective-permute-start(f32[16,256]{1,0:T(8,128)S(1)} %add.35), channel_id=1, source_target_pairs={{0,16},{2,18},{4,20},{6,22},{8,24},{10,26},{12,28},{14,30},{16,0},... | collective-permute-start | bytes 49160 | tf_op jit(solution)/shard_map/ppermute | solution.py:416
  77.4 3.3 %collective-permute-done.11 = f32[16,256]{1,0:T(8,128)S(1)} collective-permute-done((f32[16,256]{1,0:T(8,128)S(1)}, f32[16,256]{1,0:T(8,128)S(1)}, u32[]{:S(2)}, u32[]{:S(2)}) %collective-permute-start.11) | collective-permute-done | bytes 16416 | tf_op jit(solution)/shard_map/ppermute | solution.py:416
  80.6 1.2 %standardize.1 = (f32[5,10,4,10]{3,2,1,0:T(4,128)}, f32[5,4,10]{2,1,0:T(4,128)}) custom-call(f32[16,256]{1,0:T(8,128)S(1)} %add.36.total), custom_call_target="tpu_custom_call" | custom-call | tf_op jit(solution)/shard_map/standardize/pallas_call | solution.py:524
  (30 shorter events, 0.5 us)
Async XLA Ops:
  0.6 1.2 %copy-start = (bf16[1024,500]{0,1:T(8,128)(2,1)S(1)}, bf16[1024,500]{0,1:T(8,128)(2,1)}, u32[]{:S(2)}) copy-start(bf16[1024,500]{0,1:T(8,128)(2,1)} %param.6) | copy-start | bytes 3072004
  1.9 0.8 copy-start.1
  2.6 0.8 copy-start.3
  4.9 1.7 %collective-permute-start = (f32[560,128]{1,0:T(8,128)S(1)}, f32[560,128]{1,0:T(8,128)S(1)}, u32[]{:S(2)}, u32[]{:S(2)}) collective-permute-start(f32[560,128]{1,0:T(8,128)S(1)} %slice_select_fusion), channel_id=1, source_target_pairs={{0,2},{2,0},{4,6},{6,4},{8,10},{10,8},{12,14},{14,12},{16,18},{18,... | collective-permute-start | bytes 860168 | tf_op jit(solution)/shard_map/ppermute | solution.py:416
  6.7 7.0 %collective-permute-start.1 = (f32[280,128]{1,0:T(8,128)S(1)}, f32[280,128]{1,0:T(8,128)S(1)}, u32[]{:S(2)}, u32[]{:S(2)}) collective-permute-start(f32[280,128]{1,0:T(8,128)S(1)} %slice_select_fusion.1), channel_id=1, source_target_pairs={{0,4},{2,6},{4,0},{6,2},{8,12},{10,14},{12,8},{14,10},{16,20},{18,... | collective-permute-start | bytes 430088 | tf_op jit(solution)/shard_map/ppermute | solution.py:416
  13.7 5.4 %collective-permute-start.2 = (f32[280,128]{1,0:T(8,128)S(1)}, f32[280,128]{1,0:T(8,128)S(1)}, u32[]{:S(2)}, u32[]{:S(2)}) collective-permute-start(f32[280,128]{1,0:T(8,128)S(1)} %select_add_fusion.1), channel_id=1, source_target_pairs={{0,8},{2,10},{4,12},{6,14},{8,0},{10,2},{12,4},{14,6},{16,24},{18,... | collective-permute-start | bytes 430088 | tf_op jit(solution)/shard_map/ppermute | solution.py:416
  19.1 8.4 %collective-permute-start.3 = (f32[280,128]{1,0:T(8,128)S(1)}, f32[280,128]{1,0:T(8,128)S(1)}, u32[]{:S(2)}, u32[]{:S(2)}) collective-permute-start(f32[280,128]{1,0:T(8,128)S(1)} %add.31), channel_id=1, source_target_pairs={{0,16},{2,18},{4,20},{6,22},{8,24},{10,26},{12,28},{14,30},{16,0},... | collective-permute-start | bytes 430088 | tf_op jit(solution)/shard_map/ppermute | solution.py:416
  27.5 5.2 %collective-permute-start.4 = (f32[280,128]{1,0:T(8,128)S(1)}, f32[280,128]{1,0:T(8,128)S(1)}, u32[]{:S(2)}, u32[]{:S(2)}) collective-permute-start(f32[280,128]{1,0:T(8,128)S(1)} %add.32), channel_id=1, source_target_pairs={{0,4},{2,6},{4,0},{6,2},{8,12},{10,14},{12,8},{14,10},{16,20},{18,... | collective-permute-start | bytes 430088 | tf_op jit(solution)/shard_map/ppermute | solution.py:416
  32.8 1.6 %collective-permute-start.5 = (f32[560,128]{1,0:T(8,128)S(1)}, f32[560,128]{1,0:T(8,128)S(1)}, u32[]{:S(2)}, u32[]{:S(2)}) collective-permute-start(f32[560,128]{1,0:T(8,128)S(1)} %pad_maximum_fusion.1), channel_id=1, source_target_pairs={{0,2},{2,0},{4,6},{6,4},{8,10},{10,8},{12,14},{14,12},{16,18},{18,... | collective-permute-start | bytes 860168 | tf_op jit(solution)/shard_map/ppermute | solution.py:416
  32.8 0.7 copy-start.6
  32.9 0.7 copy-start.7
  58.4 1.3 %collective-permute-start.6 = (f32[3,8,512]{2,1,0:T(8,128)S(1)}, f32[3,8,512]{2,1,0:T(8,128)S(1)}, u32[]{:S(2)}, u32[]{:S(2)}) collective-permute-start(f32[3,8,512]{2,1,0:T(8,128)S(1)} %get-tuple-element.10.mine), channel_id=1, source_target_pairs={{0,2},{2,0},{4,6},{6,4},{8,10},{10,8},{12,14},{14,12},{16,18},{18,... | collective-permute-start | bytes 147464 | tf_op jit(solution)/shard_map/ppermute | solution.py:416
  60.6 5.0 %copy-start.2 = (f32[1024,8]{0,1:T(8,128)S(1)}, f32[1024,8]{0,1:T(8,128)}, u32[]{:S(2)}) copy-start(f32[1024,8]{0,1:T(8,128)} %param.7) | copy-start | bytes 98308
  60.6 5.0 %copy-start.4 = (s32[1024,8]{0,1:T(8,128)S(1)}, s32[1024,8]{0,1:T(8,128)}, u32[]{:S(2)}) copy-start(s32[1024,8]{0,1:T(8,128)} %param.8) | copy-start | bytes 98308
  60.6 5.0 %copy-start.5 = (s32[1024]{0:T(1024)S(1)}, s32[1024]{0:T(1024)}, u32[]{:S(2)}) copy-start(s32[1024]{0:T(1024)} %param.9) | copy-start | bytes 12292
  60.6 4.9 %collective-permute-start.7 = (f32[24,1024]{1,0:T(8,128)S(1)}, f32[24,1024]{1,0:T(8,128)S(1)}, u32[]{:S(2)}, u32[]{:S(2)}) collective-permute-start(f32[24,1024]{1,0:T(8,128)S(1)} %get-tuple-element.20), channel_id=1, source_target_pairs={{0,1},{1,0},{2,3},{3,2},{4,5},{5,4},{6,7},{7,6},{8,9},{9,8},{10,11... | collective-permute-start | bytes 294920 | tf_op jit(solution)/shard_map/ppermute | solution.py:416
  67.1 1.2 %collective-permute-start.8 = (f32[16,256]{1,0:T(8,128)S(1)}, f32[16,256]{1,0:T(8,128)S(1)}, u32[]{:S(2)}, u32[]{:S(2)}) collective-permute-start(f32[16,256]{1,0:T(8,128)S(1)} %stacking.1), channel_id=1, source_target_pairs={{0,2},{2,0},{4,6},{6,4},{8,10},{10,8},{12,14},{14,12},{16,18},{18,... | collective-permute-start | bytes 49160 | tf_op jit(solution)/shard_map/ppermute | solution.py:416
  68.3 3.7 %collective-permute-start.9 = (f32[16,256]{1,0:T(8,128)S(1)}, f32[16,256]{1,0:T(8,128)S(1)}, u32[]{:S(2)}, u32[]{:S(2)}) collective-permute-start(f32[16,256]{1,0:T(8,128)S(1)} %add.33), channel_id=1, source_target_pairs={{0,4},{2,6},{4,0},{6,2},{8,12},{10,14},{12,8},{14,10},{16,20},{18,... | collective-permute-start | bytes 49160 | tf_op jit(solution)/shard_map/ppermute | solution.py:416
  72.1 3.7 %collective-permute-start.10 = (f32[16,256]{1,0:T(8,128)S(1)}, f32[16,256]{1,0:T(8,128)S(1)}, u32[]{:S(2)}, u32[]{:S(2)}) collective-permute-start(f32[16,256]{1,0:T(8,128)S(1)} %add.34), channel_id=1, source_target_pairs={{0,8},{2,10},{4,12},{6,14},{8,0},{10,2},{12,4},{14,6},{16,24},{18,... | collective-permute-start | bytes 49160 | tf_op jit(solution)/shard_map/ppermute | solution.py:416
  75.8 4.8 %collective-permute-start.11 = (f32[16,256]{1,0:T(8,128)S(1)}, f32[16,256]{1,0:T(8,128)S(1)}, u32[]{:S(2)}, u32[]{:S(2)}) collective-permute-start(f32[16,256]{1,0:T(8,128)S(1)} %add.35), channel_id=1, source_target_pairs={{0,16},{2,18},{4,20},{6,22},{8,24},{10,26},{12,28},{14,30},{16,0},... | collective-permute-start | bytes 49160 | tf_op jit(solution)/shard_map/ppermute | solution.py:416

commit v4 on v3

--- a/solution.py
+++ b/solution.py
@@ -13,6 +13,8 @@
 STEP = 8
 SIDE = 24
 SUB = 32
+TILES = 4
+HALF_ROWS = 4 * TILE + 2 * SIDE
 FITS = len(HERITABILITY)
 SLOTS = 6
 HALF = SLOTS // 2
@@ -64,19 +66,11 @@
     return totals
 
 
-def block_rows(tiles):
-    place, row = {}, 0
-    for i in range(tiles):
-        for j in range(i + 1, tiles):
-            place[i, j] = row
-            row += TILE
-    for i in range(0, tiles, 2):
-        place[i, i] = place[i + 1, i + 1] = row
-        row += TILE
-    return place, row
-
-
-def call(kernel, out_shape, in_specs, scratch, name):
+def half_rows(part):
+    return {"square": 0, "between": TILE, "cross": 2 * TILE, "side": 4 * TILE}[part]
+
+
+def call(kernel, out_shape, in_specs, scratch, name, cost=None):
     vmem = pl.BlockSpec(memory_space=pltpu.VMEM)
     smem = pl.BlockSpec(memory_space=pltpu.SMEM)
     return pl.pallas_call(
@@ -86,6 +80,7 @@
         out_specs=jax.tree.map(lambda _: vmem, out_shape),
         scratch_shapes=scratch,
         compiler_params=pltpu.CompilerParams(vmem_limit_bytes=VMEM_BYTES),
+        cost_estimate=cost,
         name=name,
     )
 
@@ -99,7 +94,6 @@
         copy.start()
     width, rows = padded.shape
     tiles = width // TILE
-    place, side = block_rows(tiles)
     edge = markers // 16 * 16
     padded[0:edge, :] = dosage[0:edge, :]
     tail = dosage[edge:edge + 16, :].astype(jnp.float32)
@@ -113,11 +107,17 @@
     even, diagonals = None, []
     for i in range(tiles):
         here = dot_bf16(padded[i * TILE:(i + 1) * TILE, :], padded[i * TILE:, :], NT)
+        top = i // 2 * HALF_ROWS
         for j in range(i + 1, tiles):
-            packed[place[i, j]:place[i, j] + TILE, :] = here[:, (j - i) * TILE:(j - i + 1) * TILE]
+            if j // 2 == i // 2:
+                row = top + half_rows("between")
+            else:
+                row = i * HALF_ROWS + half_rows("cross") + j % 2 * TILE
+            packed[row:row + TILE, :] = here[:, (j - i) * TILE:(j - i + 1) * TILE]
         block = here[:, :TILE]
         if i % 2:
-            packed[place[i, i]:place[i, i] + TILE, :] = jnp.where(upper, even, block)
+            row = top + half_rows("square")
+            packed[row:row + TILE, :] = jnp.where(upper, even, block)
         even = block
         diagonals.append(jnp.sum(jnp.where(eye, block, 0.0), axis=0, keepdims=True))
     for copy in copies:
@@ -132,7 +132,7 @@
     sums = [jnp.sum(v, axis=1, keepdims=True) for v in (present, masked, masked * values)]
     for i in range(tiles):
         cols = slice(i * TILE, (i + 1) * TILE)
-        row = side + SIDE * i
+        row = i // 2 * HALF_ROWS + half_rows("side") + i % 2 * SIDE
         total = products[0:8, cols] + products[8:16, cols] + products[16:24, cols]
         if i == tiles - 1:
             for n, value in enumerate(sums):
@@ -142,156 +142,283 @@
         packed[row + 16:row + 24, :] = jnp.where(line == 0, products[32:40, cols], diagonals[i])
 
 
-def eliminate(work, old, count):
-    fits = work.shape[0]
-    shape = (fits, STEP, TILE)
-    row, lane = iota(shape, 1), iota(shape, 2)
-    per = SUB // STEP
+def own(ref, fit, first=0, last=TILE):
+    return ref.at[fit * TILE + first:fit * TILE + last, :]
+
+
+def eliminate(work, old, fits):
+    count, per, every = TILE // STEP, SUB // STEP, range(fits)
+    lane, lane_step = iota((fits, TILE), 1), iota((STEP, TILE), 1)
+    shape = (STEP, TILE)
     for t in range(count):
         base = t * STEP
-        panel = work[:, base:base + STEP, :]
-        cols = [
-            jnp.broadcast_to(panel[:, :, base + m:base + m + 1], shape) for m in range(STEP)
+        rows = [work[pl.ds(base + i, fits, stride=TILE), :] for i in range(STEP)]
+        cells = [
+            [jnp.broadcast_to(rows[i][:, base + j:base + j + 1], rows[i].shape) for j in range(i + 1)]
+            for i in range(STEP)
         ]
         inside = jnp.logical_and(lane >= base, lane < base + STEP)
-        panel = jnp.where(inside, jnp.where(lane - base == row, 1.0, 0.0), panel)
-        old[:, base:base + STEP, :] = panel
-        scale = None
+        for i in range(STEP):
+            rows[i] = jnp.where(inside, jnp.where(lane == base + i, 1.0, 0.0), rows[i])
+            old[pl.ds(base + i, fits, stride=TILE), :] = rows[i]
+        gains, inverses = {}, []
         for j in range(STEP):
-            inverse = jnp.broadcast_to(1.0 / cols[j][:, j:j + 1, :], shape)
-            here = row == j
-            gain = jnp.where(here, 0.0, cols[j] * inverse)
-            scale = inverse if scale is None else jnp.where(here, inverse, scale)
-            for m in range(j + 1, STEP):
-                cols[m] = cols[m] - gain * cols[m][:, j:j + 1, :]
-            panel = panel - gain * panel[:, j:j + 1, :]
-        panel = panel * scale
-        work[:, base:base + STEP, :] = panel
-        rows = [jnp.broadcast_to(panel[:, q:q + 1, :], shape) for q in range(STEP)]
-        stop = min((t // per + 1) * per, count)
-        for g in range(t + 1, stop):
-            other = work[:, g * STEP:(g + 1) * STEP, :]
-            total = jnp.where(inside, 0.0, other)
-            for q in range(STEP):
-                total = total - jnp.broadcast_to(
-                    other[:, :, base + q:base + q + 1], shape
-                ) * rows[q]
-            work[:, g * STEP:(g + 1) * STEP, :] = total
-        if t + 1 == stop and stop < count:
+            inverses.append(1.0 / cells[j][j])
+            for i in range(j + 1, STEP):
+                gains[i, j] = cells[i][j] * inverses[j]
+            for i in range(j + 1, STEP):
+                for m in range(j + 1, i + 1):
+                    cells[i][m] = cells[i][m] - gains[i, j] * cells[m][j]
+            for i in range(j + 1, STEP):
+                rows[i] = rows[i] - gains[i, j] * rows[j]
+        rows = [value * inverse for value, inverse in zip(rows, inverses)]
+        for j in reversed(range(1, STEP)):
+            for i in range(j):
+                rows[i] = rows[i] - gains[j, i] * rows[j]
+        for i in range(STEP):
+            work[pl.ds(base + i, fits, stride=TILE), :] = rows[i]
+        stop = (t // per + 1) * per
+        if t + 1 < stop:
+            spread = [
+                [
+                    jnp.broadcast_to(own(work, f, base + q, base + q + 1)[...], shape)
+                    for f in every
+                ]
+                for q in range(STEP)
+            ]
+            inside = jnp.logical_and(lane_step >= base, lane_step < base + STEP)
+            for g in range(t + 1, stop):
+                refs = [own(work, f, g * STEP, (g + 1) * STEP) for f in every]
+                others = [ref[...] for ref in refs]
+                totals = [jnp.where(inside, 0.0, other) for other in others]
+                for q in range(STEP):
+                    for f in every:
+                        factor = jnp.broadcast_to(others[f][:, base + q:base + q + 1], shape)
+                        totals[f] = totals[f] - factor * spread[q][f]
+                for f in every:
+                    refs[f][...] = totals[f]
+        elif stop < count:
             first, last = (t + 1 - per) * STEP, stop * STEP
             line, column = iota((SUB, TILE), 0) + first, iota((SUB, TILE), 1)
             keep = jnp.logical_or(column >= last, column // STEP <= line // STEP)
             column = iota((TILE - last, TILE), 1)
             done = jnp.logical_and(column >= first, column < last)
-            for f in range(fits):
-                left = split_three(old[f, first:last, :])
-                right = split_three(jnp.where(keep, work[f, first:last, :], 0.0))
-                product = dot_bf16(
-                    jnp.concatenate([left[i] for i in (0, 0, 0, 1, 1, 2)], 0),
-                    jnp.concatenate([right[i] for i in (0, 1, 2, 0, 1, 0)], 0),
-                    TN,
-                )
-                rest = work[f, last:, :]
-                work[f, last:, :] = jnp.where(done, 0.0, rest) - product[last:, :]
-
-
-def fit_kernel(samples, markers, penalty, packed, out, stats, centre, grid, wide, work, old):
-    fits = work.shape[0]
-    tiles = out.shape[-1] // TILE
-    end = tiles * TILE
-    place, side = block_rows(tiles)
-
-    def part(tile, which):
-        row = side + SIDE * tile + 8 * which
-        return packed[row:row + 8, :]
-
-    sums = part(tiles - 1, 0)
+            lefts, rights = [], []
+            for f in every:
+                left = split_three(own(old, f, first, last)[...])
+                right = split_three(jnp.where(keep, own(work, f, first, last)[...], 0.0))
+                lefts.append(jnp.concatenate([left[i] for i in (0, 0, 0, 1, 1, 2)], 0))
+                rights.append(jnp.concatenate([right[i] for i in (0, 1, 2, 0, 1, 0)], 0))
+            terms = [dot_bf16(a, b, TN) for a, b in zip(lefts, rights)]
+            for f in every:
+                rest = own(work, f, last)
+                rest[...] = jnp.where(done, 0.0, rest[...]) - terms[f][last:, :]
+
+
+class Half:
+    def __init__(self, ref, first, samples, markers):
+        row, col = iota((TILE, TILE), 0), iota((TILE, TILE), 1)
+        self.eye, self.ref, self.share = row == col, ref, 1.0 / samples
+        self.totals, self.squares, self.valid = [], [], []
+        for tile in range(2):
+            start = half_rows("side") + SIDE * tile + 16
+            total, diagonal = ref[start:start + 1, :], ref[start + 1:start + 2, :]
+            middle = total * self.share
+            self.totals.append(total)
+            self.squares.append(diagonal * self.share - middle * middle + 1e-05)
+            self.valid.append(iota((1, TILE), 1) + (first + tile) * TILE < markers)
+        self.columns = [jnp.transpose(jnp.broadcast_to(t, (TILE, TILE))) for t in self.totals]
+
+    def block(self, part, index=0):
+        row = half_rows(part) + index * TILE
+        return self.ref[row:row + TILE, :]
+
+    def centred(self):
+        square = self.block("square")
+        turned = jnp.transpose(square)
+        upper = iota((TILE, TILE), 0) <= iota((TILE, TILE), 1)
+        start = half_rows("side") + SIDE + 16
+        second = jnp.where(upper, turned, square)
+        second = jnp.where(self.eye, self.ref[start + 1:start + 2, :], second)
+        blocks = [jnp.where(upper, square, turned), self.block("between"), second]
+        pairs = [(0, 0), (0, 1), (1, 1)]
+        return [
+            block - self.columns[i] * self.totals[j] * self.share
+            for block, (i, j) in zip(blocks, pairs)
+        ]
+
+    def ridge(self, tile, penalty):
+        value = jnp.where(self.valid[tile], penalty * self.squares[tile], 1.0)
+        return jnp.where(self.eye, value, 0.0)
+
+    def side(self, tile, which):
+        start = half_rows("side") + SIDE * tile + 8 * which
+        return self.ref[start:start + 8, :]
+
+
+def lower_part(value):
+    keep = iota((TILE, TILE), 1) // STEP <= iota((TILE, TILE), 0) // STEP
+    return jnp.where(keep, value, 0.0)
+
+
+def first_kernel(samples, markers, penalty, place, mine, lefts, rights, above, weights, work, old):
+    fits = lefts.shape[0]
+    every = range(fits)
+    half = Half(mine, 2 * place[2], samples, markers)
+    first, between, second = half.centred()
+    for f in every:
+        own(work, f)[...] = first + half.ridge(0, penalty[f])
+    eliminate(work, old, fits)
+    for f in every:
+        lefts[f, 0], rights[f, 0] = lower_part(own(old, f)[...]), lower_part(own(work, f)[...])
+    parts = right_parts(between)
+    both = products(
+        [left_parts(jnp.concatenate([lefts[f, 0], rights[f, 0]], 0)) for f in every],
+        [parts for f in every],
+    )
+    after = products(
+        [left_parts(jnp.transpose(both[f][:TILE])) for f in every],
+        [right_parts(both[f][TILE:]) for f in every],
+    )
+    for f in every:
+        above[f], weights[f] = both[f][:TILE], both[f][TILE:]
+        own(work, f)[...] = second - after[f] + half.ridge(1, penalty[f])
+    eliminate(work, old, fits)
+    for f in every:
+        lefts[f, 1], rights[f, 1] = lower_part(own(old, f)[...]), lower_part(own(work, f)[...])
+
+
+def second_kernel(
+    samples, markers, penalty, place, mine, theirs, lefts, rights, above, weights,
+    out, stats, centre, wide, work, old, rhs, scratch,
+):
+    fits = out.shape[0]
+    every = range(fits)
+    late = place[2] == 1
+    halves = [Half(mine, 2 * place[2], samples, markers)]
+    halves.append(Half(theirs, 2 - 2 * place[2], samples, markers))
+    sums = jnp.where(late, halves[0].side(1, 0), halves[1].side(1, 0))
     counts, first, second = (sums[:, TILE - 1 - n:TILE - n] for n in range(3))
     mean = first / counts
     spread = jnp.sqrt(second / counts - mean * mean + 1e-05)
     lane = iota((TRAITS, TILE), 1)
     stats[...] = jnp.where(lane == 0, mean, jnp.where(lane == 1, spread, 0.0))
-    row, col = iota((TILE, TILE), 0), iota((TILE, TILE), 1)
-    eye, upper = row == col, row <= col
-    line = iota((1, TILE), 1)
     share = 1.0 / samples
-    totals = [part(i, 2)[0:1, :] for i in range(tiles)]
-    squares = []
-    blank = jnp.zeros((TILE - TRAITS, TILE), jnp.float32)
-    for i in range(tiles):
-        mine = slice(i * TILE, (i + 1) * TILE)
-        column = jnp.transpose(jnp.broadcast_to(totals[i], (TILE, TILE)))
-        diagonal = part(i, 2)[1:2, :]
-        middle = totals[i] * share
-        centre[:, mine] = jnp.broadcast_to(middle, (8, TILE))
-        squares.append(diagonal * share - middle * middle + 1e-05)
-        for j in range(i, tiles):
-            block = packed[place[i, j]:place[i, j] + TILE, :]
-            if i == j:
-                turned = jnp.transpose(block)
-                if i % 2:
-                    block = jnp.where(upper, turned, block)
-                    block = jnp.where(eye, diagonal, block)
-                else:
-                    block = jnp.where(upper, block, turned)
-            block = block - column * totals[j] * share
-            if j == tiles - 1:
-                value = (part(i, 0) - part(i, 1) * mean) / spread
-                value = jnp.where(lane + i * TILE < markers, value, 0.0)
-                block = block + jnp.transpose(jnp.concatenate([blank, value], 0))
-            grid[i, :, j * TILE:(j + 1) * TILE] = block
-
-    def ridge(i, f):
-        value = jnp.where(line + i * TILE < markers, penalty[f] * squares[i], 1.0)
-        return jnp.where(eye, value, 0.0)
-
-    for f in range(fits):
-        work[f] = grid[0, :, 0:TILE] + ridge(0, f)
-    every = range(fits)
-    count = TILE // STEP
-    for k in range(tiles):
+
+    def place_tiles(ref, index, tiles):
+        for t in range(TILES):
+            value = jnp.where(late, tiles[(t + 2) % TILES], tiles[t])
+            cols = slice(t * TILE, (t + 1) * TILE)
+            if index is None:
+                ref[:, cols] = value
+            else:
+                ref[index, :, cols] = value
+
+    tiles = [(halves[t // 2], t % 2) for t in range(TILES)]
+    totals = [half.totals[t] for half, t in tiles]
+    place_tiles(centre, None, [jnp.broadcast_to(t * share, (8, TILE)) for t in totals])
+    for t, (half, tile) in enumerate(tiles):
+        value = (half.side(tile, 0) - half.side(tile, 1) * mean) / spread
+        value = jnp.where(half.valid[tile], value, 0.0)
+        for f in every:
+            rhs[f, :, t * TILE:(t + 1) * TILE] = value
+    a, b = (halves[0].block("cross", n) for n in range(2))
+    c, d = (halves[1].block("cross", n) for n in range(2))
+    crosses = [
+        [jnp.where(late, c.T, a), jnp.where(late, a.T, b)],
+        [jnp.where(late, d.T, c), jnp.where(late, b.T, d)],
+    ]
+    rows = []
+    for i in range(2):
+        column = halves[0].columns[i]
+        rows.append(
+            jnp.concatenate(
+                [crosses[i][j] - column * totals[2 + j] * share for j in range(2)], 1
+            )
+        )
+    blocks = halves[1].centred()
+    corner = [jnp.concatenate(blocks[:2], 1), blocks[2]]
+    ridge = [[halves[1].ridge(t, penalty[f]) for t in range(2)] for f in every]
+
+    def stacked(k):
+        return [left_parts(jnp.concatenate([lefts[f, k], rights[f, k]], 0)) for f in every]
+
+    def side_step(k, left, right, later):
         lo, hi = k * TILE, (k + 1) * TILE
-        pivots = count if hi < end else count - 1
-        eliminate(work, old, pivots)
-        lower = jnp.logical_and(col // STEP <= row // STEP, row < pivots * STEP)
-        lefts = [jnp.where(lower, old[f], 0.0) for f in every]
-        if hi < end:
-            rights = [jnp.where(lower, work[f], 0.0) for f in every]
-            above = [grid[0, :, hi:]] if k == 0 else [wide[f, k, :, hi:] for f in every]
-            above = [right_parts(value) for value in above] * (fits if k == 0 else 1)
-            stacked = [left_parts(jnp.concatenate([lefts[f], rights[f]], 0)) for f in every]
-            both = products(stacked, above)
-            factors = [left_parts(jnp.transpose(both[f][:TILE])) for f in every]
-            parts = [right_parts(both[f][TILE:]) for f in every]
-            for i in range(k + 1, tiles):
-                begin = i * TILE
-                after = products(
-                    [[p[begin - hi:begin - hi + TILE] for p in factors[f]] for f in every],
-                    [[p[:, begin - hi:] for p in parts[f]] for f in every],
-                )
-                for f in every:
-                    before = grid[i, :, begin:] if k == 0 else wide[f, i, :, begin:]
-                    value = before - after[f]
-                    block = value[:, :TILE] + ridge(i, f) if k == 0 else value[:, :TILE]
-                    if i == k + 1:
-                        work[f] = block
-                    else:
-                        wide[f, i, :, begin:begin + TILE] = block
-                    if i + 1 < tiles:
-                        wide[f, i, :, begin + TILE:] = value[:, TILE:]
-        else:
-            last = jnp.logical_and(row < pivots * STEP, col >= pivots * STEP)
-            parts = [right_parts(jnp.where(last, work[f], 0.0)) for f in every]
-        final = products([left_parts(jnp.transpose(left)) for left in lefts], parts)
+        turned = [dot(rhs[f, :, lo:hi], left[f], NT) for f in every]
         for f in every:
-            if hi < end:
-                wide[f, k, :, hi:] = final[f]
-            out[f, :, lo:hi] = jnp.transpose(final[f][:, -TILE:])[TILE - TRAITS:, :]
-    for k in reversed(range(tiles - 1)):
+            rhs[f, :, lo:hi] = dot(turned[f], right[f])
+            if later is not None:
+                rhs[f, :, hi:] = rhs[f, :, hi:] - dot(turned[f], later[f])
+
+    parts = right_parts(rows[0])
+    both = products(stacked(0), [parts for f in every])
+    after = products(
+        [left_parts(jnp.transpose(above[f])) for f in every],
+        [right_parts(both[f][TILE:]) for f in every],
+    )
+    parts = [right_parts(rows[1] - after[f]) for f in every]
+    more = products(stacked(1), parts)
+    upper = [jnp.concatenate([both[f][:TILE], more[f][:TILE]], 0) for f in every]
+    lower = [jnp.concatenate([both[f][TILE:], more[f][TILE:]], 0) for f in every]
+    factors = [left_parts(jnp.transpose(upper[f])) for f in every]
+    parts = [right_parts(lower[f]) for f in every]
+    for i in range(2):
+        cut = i * TILE
+        after = products(
+            [[p[cut:cut + TILE] for p in factors[f]] for f in every],
+            [[p[:, cut:] for p in parts[f]] for f in every],
+        )
+        for f in every:
+            value = corner[i] - after[f]
+            block = value[:, :TILE] + ridge[f][i]
+            if i == 0:
+                own(work, f)[...] = block
+                scratch[f, 0] = value[:, TILE:]
+            else:
+                scratch[f, 1] = block
+    later = [jnp.concatenate([weights[f], both[f][TILE:]], 1) for f in every]
+    side_step(0, [lefts[f, 0] for f in every], [rights[f, 0] for f in every], later)
+    final = products(
+        [left_parts(jnp.transpose(lefts[f, 0])) for f in every], [right_parts(v) for v in later]
+    )
+    for f in every:
+        wide[f, 0, :, TILE:] = final[f]
+    later = [more[f][TILE:] for f in every]
+    side_step(1, [lefts[f, 1] for f in every], [rights[f, 1] for f in every], later)
+    final = products(
+        [left_parts(jnp.transpose(lefts[f, 1])) for f in every], [right_parts(v) for v in later]
+    )
+    for f in every:
+        wide[f, 1, :, 2 * TILE:] = final[f]
+
+    eliminate(work, old, fits)
+    left = [lower_part(own(old, f)[...]) for f in every]
+    right = [lower_part(own(work, f)[...]) for f in every]
+    both = products(
+        [left_parts(jnp.concatenate([left[f], right[f]], 0)) for f in every],
+        [right_parts(scratch[f, 0]) for f in every],
+    )
+    later = [both[f][TILE:] for f in every]
+    parts = [right_parts(v) for v in later]
+    after = products([left_parts(jnp.transpose(both[f][:TILE])) for f in every], parts)
+    for f in every:
+        own(work, f)[...] = scratch[f, 1] - after[f]
+    side_step(2, left, right, later)
+    final = products([left_parts(jnp.transpose(left[f])) for f in every], parts)
+    for f in every:
+        wide[f, 2, :, 3 * TILE:] = final[f]
+    eliminate(work, old, fits)
+    left = [lower_part(own(old, f)[...]) for f in every]
+    right = [lower_part(own(work, f)[...]) for f in every]
+    side_step(3, left, right, None)
+    for k in reversed(range(TILES - 1)):
         lo, hi = k * TILE, (k + 1) * TILE
-        known = [dot(out[f, :, hi:], wide[f, k, :, hi:], NT) for f in every]
+        known = [dot(rhs[f, :, hi:], wide[f, k, :, hi:], NT) for f in every]
         for f in every:
-            out[f, :, lo:hi] = out[f, :, lo:hi] - known[f]
+            rhs[f, :, lo:hi] = rhs[f, :, lo:hi] - known[f]
+    for f in every:
+        place_tiles(out, f, [rhs[f, :, t * TILE:(t + 1) * TILE] for t in range(TILES)])
 
 
 def predict_kernel(pairs, place, mine, other, centre, padded, out):
@@ -406,11 +533,6 @@
             gram[k, l] = turned[row:row + per_share, 0:levels]
 
 
-def fit_scratch(fits, tiles, width):
-    shapes = [(tiles, TILE, width), (fits, tiles, TILE, width)] + [(fits, TILE, TILE)] * 2
-    return [pltpu.VMEM(shape, jnp.float32) for shape in shapes]
-
-
 def swap(value, axis, mask):
     size = lax.axis_size(axis)
     return lax.ppermute(value, axis, [(i, i ^ mask) for i in range(size)])
@@ -424,20 +546,9 @@
     return found
 
 
-def sum_over(value, axis, halvings):
-    masks = masks_of(axis)
-    position = lax.axis_index(axis)
-    for mask in masks[:halvings]:
-        half = value.shape[0] // 2
-        low, high = value[:half], value[half:]
-        up = (position & mask) != 0
-        value = jnp.where(up, high, low) + swap(jnp.where(up, low, high), axis, mask)
-    for mask in masks[halvings:]:
+def sum_over(value, axis):
+    for mask in masks_of(axis):
         value = value + swap(value, axis, mask)
-    for mask in reversed(masks[:halvings]):
-        up = (position & mask) != 0
-        other = swap(value, axis, mask)
-        value = jnp.concatenate([jnp.where(up, other, value), jnp.where(up, value, other)], 0)
     return value
 
 
@@ -448,26 +559,26 @@
     samples = local_rows * sample_devices
     all_markers = markers * block_devices
     width = -(-markers // TILE) * TILE
-    tiles = width // TILE
+    assert width == TILES * TILE and markers + 3 <= width
     per_share = TRAITS // block_devices
     pairs = block_devices == 2
     f32 = functools.partial(jax.ShapeDtypeStruct, dtype=jnp.float32)
     position, block = lax.axis_index("samp"), lax.axis_index("blk")
     odd = position % 2
-    place = jnp.stack([odd, block]).astype(jnp.int32)
+    late = position // 2 % 2
+    place = jnp.stack([odd, block, late]).astype(jnp.int32)
     traits, observed = traits.T, observed.T
-    _, side = block_rows(tiles)
 
     whole = lambda shape: pl.BlockSpec(shape, lambda _: (0, 0))
     packed, padded = pl.pallas_call(
         functools.partial(gram_kernel, markers),
         grid=(1,),
         out_shape=[
-            f32((side + SIDE * tiles, TILE)),
+            f32((2 * HALF_ROWS, TILE)),
             jax.ShapeDtypeStruct((width, local_rows), jnp.bfloat16),
         ],
         in_specs=[whole((width, local_rows))] + [pl.BlockSpec(memory_space=pltpu.HBM)] * 2,
-        out_specs=[whole((side + SIDE * tiles, TILE)), whole((width, local_rows))],
+        out_specs=[whole((2 * HALF_ROWS, TILE)), whole((width, local_rows))],
         scratch_shapes=[
             pltpu.VMEM(traits.shape, traits.dtype),
             pltpu.VMEM(observed.shape, observed.dtype),
@@ -476,7 +587,17 @@
         compiler_params=pltpu.CompilerParams(vmem_limit_bytes=VMEM_BYTES),
         name="local_gram",
     )(genotypes.T, traits, observed)
-    packed = sum_over(packed, "samp", 2)
+    quarters = packed.reshape(2, 2, HALF_ROWS // 2, TILE)
+    up = odd == 1
+    keep = jnp.where(up, quarters[:, 1], quarters[:, 0])
+    value = keep + swap(jnp.where(up, quarters[:, 0], quarters[:, 1]), "samp", 1)
+    keep = jnp.where(late == 1, value[1], value[0])
+    value = keep + swap(jnp.where(late == 1, value[0], value[1]), "samp", 2)
+    for mask in masks_of("samp")[2:]:
+        value = value + swap(value, "samp", mask)
+    other = swap(value, "samp", 1)
+    half = jnp.concatenate([jnp.where(up, other, value), jnp.where(up, value, other)], 0)
+    theirs = swap(half, "samp", 2)
 
     penalties = [all_markers * (1.0 - h) / h for h in HERITABILITY]
     penalties = penalties + [penalties[-1]] * (SLOTS - len(penalties))
@@ -485,13 +606,28 @@
         jnp.array(penalties[HALF:], jnp.float32),
         jnp.array(penalties[:HALF], jnp.float32),
     )
+    square = (HALF, TILE, TILE)
+    started = call(
+        functools.partial(first_kernel, samples, markers),
+        [f32((HALF, 2, TILE, TILE)), f32((HALF, 2, TILE, TILE)), f32(square), f32(square)],
+        ["smem", "smem", "vmem"],
+        [pltpu.VMEM((HALF * TILE, TILE), jnp.float32)] * 2,
+        "first_fits",
+        cost=pl.CostEstimate(flops=4 * 10**9, bytes_accessed=2**21, transcendentals=0),
+    )(penalty, place, half)
     weights, stats, centre = call(
-        functools.partial(fit_kernel, samples, markers),
+        functools.partial(second_kernel, samples, markers),
         [f32((HALF, TRAITS, width)), f32((TRAITS, TILE)), f32((8, width))],
-        ["smem", "vmem"],
-        fit_scratch(HALF, tiles, width),
-        "ridge_fits",
-    )(penalty, packed)
+        ["smem", "smem"] + ["vmem"] * 6,
+        [
+            pltpu.VMEM((HALF, TILES, TILE, width), jnp.float32),
+            pltpu.VMEM((HALF * TILE, TILE), jnp.float32),
+            pltpu.VMEM((HALF * TILE, TILE), jnp.float32),
+            pltpu.VMEM((HALF, TRAITS, width), jnp.float32),
+            pltpu.VMEM((HALF, 2, TILE, TILE), jnp.float32),
+        ],
+        "second_fits",
+    )(penalty, place, half, theirs, *started)
     other = swap(weights, "samp", 1)
 
     count = SLOTS * TRAITS
@@ -520,7 +656,7 @@
         [],
         "stacking",
     )(place, mine, theirs, stats, traits, observed, fold_index[None, :])
-    products = sum_over(products, "samp", 0)
+    products = sum_over(products, "samp")
     gram, cross = call(
         functools.partial(scale_kernel, per_share, block_devices, samples),
         [f32((FOLDS, levels, per_share, levels)), f32((FOLDS, per_share, levels))],

time: 82.1 us -> 78.2 us (0.952)
  waiting for transfers between devices: 35.1 us -> 29.8 us
  starting transfers between devices: 13.1 us -> 14.5 us
    ppermute x12, waiting for transfers between devices: 35.1 us -> 29.8 us  [swap(): return lax.ppermute(value, axis, [(i, i ^ mask) for i in range(size)])]
    ppermute x12, starting transfers between devices: 13.1 us -> 14.5 us  [swap(): return lax.ppermute(value, axis, [(i, i ^ mask) for i in range(size)])]
    unnamed x16 -> x14, local copies, waits for them, and re-layouts: 3.4 us -> 2.74 us
    pallas_call x1 -> x2, Pallas kernels: 24 us -> 24.6 us  [the longest x1 15.1 us: body(): call(functools.partial(second_kernel, samples, markers), [f32((HALF, TRAI...]
  transfers between devices with their start and end apart: 12 -> 12, of which waited for: 12 -> 11; matrix products, arithmetic and copies ran while one was open for 0% -> 0% of each run, Pallas kernels for 0% -> 12%
where the time goes in v4:
time: 78.2 us; the launch traced here: 77.9 us
  waiting for transfers between devices  29.8 us (38%)
  Pallas kernels  29.6 us (38%)
  starting transfers between devices  14.5 us (19%)
  local copies, waits for them, and re-layouts  2.75 us (4%)
  between operations  0.81 us (1%)
    ppermute x12, waiting for transfers between devices, swap(): return lax.ppermute(value, axis, [(i, i ^ mask) for i in range(size)])  29.8 us
    pallas_call x1, Pallas kernels, body(): call(functools.partial(second_kernel, samples, markers), [f32((HALF, TRAI...  15.1 us
    ppermute x12, starting transfers between devices, swap(): return lax.ppermute(value, axis, [(i, i ^ mask) for i in range(size)])  14.5 us
    pallas_call x1, Pallas kernels, body(): call(functools.partial(first_kernel, samples, markers), [f32((HALF, 2, TI...  9.51 us
    unnamed x14, local copies, waits for them, and re-layouts  2.74 us
  transfers between devices with their start and end apart: 12, of which 11 were waited for; matrix products, arithmetic and copies ran while one was open for 0% of the time, Pallas kernels for 12%

profile of v4, /device:TPU:0, one launch (start us, length us, event | category | flops | bytes accessed | tf_op | source)
XLA Modules:
  0.0 77.9 jit_solution(14929253326140274763)
XLA Ops:
  0.7 0.7 copy-done.1
  1.4 1.2 %copy-done = bf16[1024,500]{0,1:T(8,128)(2,1)S(1)} copy-done((bf16[1024,500]{0,1:T(8,128)(2,1)S(1)}, bf16[1024,500]{0,1:T(8,128)(2,1)}, u32[]{:S(2)}) %copy-start) | copy-done | bytes 1024024
  2.6 0.8 copy-done.2
  3.4 1.5 %local_gram.1 = (f32[1120,128]{1,0:T(8,128)S(1)}, bf16[512,1024]{1,0:T(8,128)(2,1)S(1)}) custom-call(bf16[500,1024]{1,0:T(8,128)(2,1)S(1)} %bitcast.36, f32[8,1024]{1,0:T(8,128)S(1)} %bitcast.37, s32[8,1024]{1,0:T(8,128)S(1)} %bitcast.39), custom_call_target="tpu_custom_call" | custom-call | tf_op jit(solution)/shard_map/local_gram/pallas_call | solution.py:573
  4.9 0.5 collective-permute-start
  5.4 1.2 %collective-permute-done = f32[2,280,128]{2,1,0:T(8,128)S(1)} collective-permute-done((f32[2,280,128]{2,1,0:T(8,128)S(1)}, f32[2,280,128]{2,1,0:T(8,128)S(1)}, u32[]{:S(2)}, u32[]{:S(2)}) %collective-permute-start) | collective-permute-done | bytes 286752 | tf_op jit(solution)/shard_map/ppermute | solution.py:538
  6.6 0.1 bitcast_add_fusion
  6.7 2.9 %collective-permute-start.1 = (f32[280,128]{1,0:T(8,128)S(1)}, f32[280,128]{1,0:T(8,128)S(1)}, u32[]{:S(2)}, u32[]{:S(2)}) collective-permute-start(f32[280,128]{1,0:T(8,128)S(1)} %select_bitcast_fusion.1), channel_id=1, source_target_pairs={{0,4},{2,6},{4,0},{6,2},{8,12},{10,14},{12,8},{14,10},{16,20},{18,... | collective-permute-start | bytes 430088 | tf_op jit(solution)/shard_map/ppermute | solution.py:538
  9.6 4.1 %collective-permute-done.1 = f32[280,128]{1,0:T(8,128)S(1)} collective-permute-done((f32[280,128]{1,0:T(8,128)S(1)}, f32[280,128]{1,0:T(8,128)S(1)}, u32[]{:S(2)}, u32[]{:S(2)}) %collective-permute-start.1) | collective-permute-done | bytes 143392 | tf_op jit(solution)/shard_map/ppermute | solution.py:538
  13.7 1.9 %collective-permute-start.2 = (f32[280,128]{1,0:T(8,128)S(1)}, f32[280,128]{1,0:T(8,128)S(1)}, u32[]{:S(2)}, u32[]{:S(2)}) collective-permute-start(f32[280,128]{1,0:T(8,128)S(1)} %bitcast_add_fusion.1), channel_id=1, source_target_pairs={{0,8},{2,10},{4,12},{6,14},{8,0},{10,2},{12,4},{14,6},{16,24},{18,... | collective-permute-start | bytes 430088 | tf_op jit(solution)/shard_map/ppermute | solution.py:538
  15.6 3.5 %collective-permute-done.2 = f32[280,128]{1,0:T(8,128)S(1)} collective-permute-done((f32[280,128]{1,0:T(8,128)S(1)}, f32[280,128]{1,0:T(8,128)S(1)}, u32[]{:S(2)}, u32[]{:S(2)}) %collective-permute-start.2) | collective-permute-done | bytes 143392 | tf_op jit(solution)/shard_map/ppermute | solution.py:538
  19.1 2.7 %collective-permute-start.3 = (f32[280,128]{1,0:T(8,128)S(1)}, f32[280,128]{1,0:T(8,128)S(1)}, u32[]{:S(2)}, u32[]{:S(2)}) collective-permute-start(f32[280,128]{1,0:T(8,128)S(1)} %add.36), channel_id=1, source_target_pairs={{0,16},{2,18},{4,20},{6,22},{8,24},{10,26},{12,28},{14,30},{16,0},... | collective-permute-start | bytes 430088 | tf_op jit(solution)/shard_map/ppermute | solution.py:538
  21.8 5.7 %collective-permute-done.3 = f32[280,128]{1,0:T(8,128)S(1)} collective-permute-done((f32[280,128]{1,0:T(8,128)S(1)}, f32[280,128]{1,0:T(8,128)S(1)}, u32[]{:S(2)}, u32[]{:S(2)}) %collective-permute-start.3) | collective-permute-done | bytes 143392 | tf_op jit(solution)/shard_map/ppermute | solution.py:538
  27.5 0.1 collective-permute-start.4
  27.7 0.1 pad_add_fusion.place
  27.7 1.2 %collective-permute-done.4 = f32[280,128]{1,0:T(8,128)S(1)} collective-permute-done((f32[280,128]{1,0:T(8,128)S(1)}, f32[280,128]{1,0:T(8,128)S(1)}, u32[]{:S(2)}, u32[]{:S(2)}) %collective-permute-start.4) | collective-permute-done | bytes 143392 | tf_op jit(solution)/shard_map/ppermute | solution.py:538
  29.0 1.0 %collective-permute-start.5 = (f32[560,128]{1,0:T(8,128)S(1)}, f32[560,128]{1,0:T(8,128)S(1)}, u32[]{:S(2)}, u32[]{:S(2)}) collective-permute-start(f32[560,128]{1,0:T(8,128)S(1)} %pad_maximum_fusion.mine), channel_id=1, source_target_pairs={{0,4},{2,6},{4,0},{6,2},{8,12},{10,14},{12,8},{14,10},{16,20},{18,... | collective-permute-start | bytes 860168 | tf_op jit(solution)/shard_map/ppermute | solution.py:538
  30.1 9.5 %first_fits.1 = (f32[3,2,128,128]{3,2,1,0:T(8,128)S(1)}, f32[3,2,128,128]{3,2,1,0:T(8,128)S(1)}, f32[3,128,128]{2,1,0:T(8,128)S(1)}, f32[3,128,128]{2,1,0:T(8,128)S(1)}) custom-call(f32[3]{0:T(128)S(1)} %broadcast_select_fusion.2.penalty, s32[3]{0:T(128)S(1)} %pad_add_fusion.place, f32[560,128]{1,0:T(8,128)S(1)} %pad_maximum_fusion.mine), custom_call_target="tpu_custom_call" | custom-call | flops 4000000000 | bytes 2097152 | tf_op jit(solution)/shard_map/first_fits/pallas_call | solution.py:610
  39.6 15.1 %second_fits.1 = (f32[3,8,512]{2,1,0:T(8,128)S(1)}, f32[8,128]{1,0:T(8,128)S(1)}, f32[8,512]{1,0:T(8,128)S(1)}) custom-call(f32[3]{0:T(128)S(1)} %broadcast_select_fusion.2.penalty, s32[3]{0:T(128)S(1)} %pad_add_fusion.place, f32[560,128]{1,0:T(8,128)S(1)} %pad_maximum_fusion.mine, f32[560,128]{1,0:T(8,128)S(1)} %collective-permute-done.5.theirs, ...), custom_call_target="tpu_custom_call" | custom-call | tf_op jit(solution)/shard_map/second_fits/pallas_call | solution.py:618
  54.7 1.3 %collective-permute-done.6.other = f32[3,8,512]{2,1,0:T(8,128)S(1)} collective-permute-done((f32[3,8,512]{2,1,0:T(8,128)S(1)}, f32[3,8,512]{2,1,0:T(8,128)S(1)}, u32[]{:S(2)}, u32[]{:S(2)}) %collective-permute-start.6) | collective-permute-done | bytes 49184 | tf_op jit(solution)/shard_map/ppermute | solution.py:538
  55.9 0.9 %predictions.1 = f32[2,24,1024]{2,1,0:T(8,128)S(1)} custom-call(s32[3]{0:T(128)S(1)} %pad_add_fusion.place, f32[3,8,512]{2,1,0:T(8,128)S(1)} %get-tuple-element.18.mine, f32[3,8,512]{2,1,0:T(8,128)S(1)} %collective-permute-done.6.other, f32[8,512]{1,0:T(8,128)S(1)} %get-tuple-element.19.centre, bf16[512,1024]{1,0:T(8,128)(2,1)S(1)} %get-tuple-element.20.padded), custom_call_target="tpu_custom_call" | custom-call | tf_op jit(solution)/shard_map/predictions/pallas_call | solution.py:635
  56.9 1.6 %collective-permute-start.7 = (f32[24,1024]{1,0:T(8,128)S(1)}, f32[24,1024]{1,0:T(8,128)S(1)}, u32[]{:S(2)}, u32[]{:S(2)}) collective-permute-start(f32[24,1024]{1,0:T(8,128)S(1)} %get-tuple-element.26), channel_id=1, source_target_pairs={{0,1},{1,0},{2,3},{3,2},{4,5},{5,4},{6,7},{7,6},{8,9},{9,8},{10,11... | collective-permute-start | bytes 294920 | tf_op jit(solution)/shard_map/ppermute | solution.py:538
  58.4 3.3 %collective-permute-done.7.other = f32[24,1024]{1,0:T(8,128)S(1)} collective-permute-done((f32[24,1024]{1,0:T(8,128)S(1)}, f32[24,1024]{1,0:T(8,128)S(1)}, u32[]{:S(2)}, u32[]{:S(2)}) %collective-permute-start.7) | collective-permute-done | bytes 98336 | tf_op jit(solution)/shard_map/ppermute | solution.py:538
  61.8 1.5 %stacking.1 = f32[16,256]{1,0:T(8,128)S(1)} custom-call(s32[3]{0:T(128)S(1)} %pad_add_fusion.place, f32[24,1024]{1,0:T(8,128)S(1)} %get-tuple-element.27.mine, f32[24,1024]{1,0:T(8,128)S(1)} %collective-permute-done.7.other, f32[8,128]{1,0:T(8,128)S(1)} %get-tuple-element.21.stats, f32[8,1024]{1,0:T(8,128)S(1)} %bitcast.38, s32[8,1024]{1,0:T(8,128)S(1)} %bitcast.40, ...), custom_call_target="tpu_custom_call" | custom-call | tf_op jit(solution)/shard_map/stacking/pallas_call | solution.py:652
  63.3 1.2 %collective-permute-done.8 = f32[16,256]{1,0:T(8,128)S(1)} collective-permute-done((f32[16,256]{1,0:T(8,128)S(1)}, f32[16,256]{1,0:T(8,128)S(1)}, u32[]{:S(2)}, u32[]{:S(2)}) %collective-permute-start.8) | collective-permute-done | bytes 16416 | tf_op jit(solution)/shard_map/ppermute | solution.py:538
  64.6 1.1 %collective-permute-start.9 = (f32[16,256]{1,0:T(8,128)S(1)}, f32[16,256]{1,0:T(8,128)S(1)}, u32[]{:S(2)}, u32[]{:S(2)}) collective-permute-start(f32[16,256]{1,0:T(8,128)S(1)} %add.38), channel_id=1, source_target_pairs={{0,4},{2,6},{4,0},{6,2},{8,12},{10,14},{12,8},{14,10},{16,20},{18,... | collective-permute-start | bytes 49160 | tf_op jit(solution)/shard_map/ppermute | solution.py:538
  65.6 2.7 %collective-permute-done.9 = f32[16,256]{1,0:T(8,128)S(1)} collective-permute-done((f32[16,256]{1,0:T(8,128)S(1)}, f32[16,256]{1,0:T(8,128)S(1)}, u32[]{:S(2)}, u32[]{:S(2)}) %collective-permute-start.9) | collective-permute-done | bytes 16416 | tf_op jit(solution)/shard_map/ppermute | solution.py:538
  68.3 0.7 collective-permute-start.10
  69.0 3.1 %collective-permute-done.10 = f32[16,256]{1,0:T(8,128)S(1)} collective-permute-done((f32[16,256]{1,0:T(8,128)S(1)}, f32[16,256]{1,0:T(8,128)S(1)}, u32[]{:S(2)}, u32[]{:S(2)}) %collective-permute-start.10) | collective-permute-done | bytes 16416 | tf_op jit(solution)/shard_map/ppermute | solution.py:538
  72.0 2.0 %collective-permute-start.11 = (f32[16,256]{1,0:T(8,128)S(1)}, f32[16,256]{1,0:T(8,128)S(1)}, u32[]{:S(2)}, u32[]{:S(2)}) collective-permute-start(f32[16,256]{1,0:T(8,128)S(1)} %add.40), channel_id=1, source_target_pairs={{0,16},{2,18},{4,20},{6,22},{8,24},{10,26},{12,28},{14,30},{16,0},... | collective-permute-start | bytes 49160 | tf_op jit(solution)/shard_map/ppermute | solution.py:538
  74.1 2.6 %collective-permute-done.11 = f32[16,256]{1,0:T(8,128)S(1)} collective-permute-done((f32[16,256]{1,0:T(8,128)S(1)}, f32[16,256]{1,0:T(8,128)S(1)}, u32[]{:S(2)}, u32[]{:S(2)}) %collective-permute-start.11) | collective-permute-done | bytes 16416 | tf_op jit(solution)/shard_map/ppermute | solution.py:538
  76.7 1.2 %standardize.1 = (f32[5,10,4,10]{3,2,1,0:T(4,128)}, f32[5,4,10]{2,1,0:T(4,128)}) custom-call(f32[16,256]{1,0:T(8,128)S(1)} %add.41.total), custom_call_target="tpu_custom_call" | custom-call | tf_op jit(solution)/shard_map/standardize/pallas_call | solution.py:660
  (27 shorter events, 0.2 us)
Async XLA Ops:
  0.6 0.8 copy-start.1
  1.4 1.2 %copy-start = (bf16[1024,500]{0,1:T(8,128)(2,1)S(1)}, bf16[1024,500]{0,1:T(8,128)(2,1)}, u32[]{:S(2)}) copy-start(bf16[1024,500]{0,1:T(8,128)(2,1)} %param.6) | copy-start | bytes 3072004
  2.6 0.8 copy-start.2
  4.9 1.7 %collective-permute-start = (f32[2,280,128]{2,1,0:T(8,128)S(1)}, f32[2,280,128]{2,1,0:T(8,128)S(1)}, u32[]{:S(2)}, u32[]{:S(2)}) collective-permute-start(f32[2,280,128]{2,1,0:T(8,128)S(1)} %select_bitcast_fusion), channel_id=1, source_target_pairs={{0,2},{2,0},{4,6},{6,4},{8,10},{10,8},{12,14},{14,12},{16,18},{18,... | collective-permute-start | bytes 860168 | tf_op jit(solution)/shard_map/ppermute | solution.py:538
  6.7 7.0 %collective-permute-start.1 = (f32[280,128]{1,0:T(8,128)S(1)}, f32[280,128]{1,0:T(8,128)S(1)}, u32[]{:S(2)}, u32[]{:S(2)}) collective-permute-start(f32[280,128]{1,0:T(8,128)S(1)} %select_bitcast_fusion.1), channel_id=1, source_target_pairs={{0,4},{2,6},{4,0},{6,2},{8,12},{10,14},{12,8},{14,10},{16,20},{18,... | collective-permute-start | bytes 430088 | tf_op jit(solution)/shard_map/ppermute | solution.py:538
  13.7 5.4 %collective-permute-start.2 = (f32[280,128]{1,0:T(8,128)S(1)}, f32[280,128]{1,0:T(8,128)S(1)}, u32[]{:S(2)}, u32[]{:S(2)}) collective-permute-start(f32[280,128]{1,0:T(8,128)S(1)} %bitcast_add_fusion.1), channel_id=1, source_target_pairs={{0,8},{2,10},{4,12},{6,14},{8,0},{10,2},{12,4},{14,6},{16,24},{18,... | collective-permute-start | bytes 430088 | tf_op jit(solution)/shard_map/ppermute | solution.py:538
  19.1 8.6 %copy-start.5 = (f32[3]{0:T(128)S(1)}, f32[3]{0:T(128)}, u32[]{:S(2)}) copy-start(f32[3]{0:T(128)} %constant.42.clone) | copy-start | bytes 40
  19.1 8.6 %copy-start.6 = (f32[3]{0:T(128)S(1)}, f32[3]{0:T(128)}, u32[]{:S(2)}) copy-start(f32[3]{0:T(128)} %constant.41.clone) | copy-start | bytes 40
  19.1 8.4 %collective-permute-start.3 = (f32[280,128]{1,0:T(8,128)S(1)}, f32[280,128]{1,0:T(8,128)S(1)}, u32[]{:S(2)}, u32[]{:S(2)}) collective-permute-start(f32[280,128]{1,0:T(8,128)S(1)} %add.36), channel_id=1, source_target_pairs={{0,16},{2,18},{4,20},{6,22},{8,24},{10,26},{12,28},{14,30},{16,0},... | collective-permute-start | bytes 430088 | tf_op jit(solution)/shard_map/ppermute | solution.py:538
  27.5 1.4 %collective-permute-start.4 = (f32[280,128]{1,0:T(8,128)S(1)}, f32[280,128]{1,0:T(8,128)S(1)}, u32[]{:S(2)}, u32[]{:S(2)}) collective-permute-start(f32[280,128]{1,0:T(8,128)S(1)} %add.37), channel_id=1, source_target_pairs={{0,2},{2,0},{4,6},{6,4},{8,10},{10,8},{12,14},{14,12},{16,18},{18,... | collective-permute-start | bytes 430088 | tf_op jit(solution)/shard_map/ppermute | solution.py:538
  29.0 10.6 %collective-permute-start.5 = (f32[560,128]{1,0:T(8,128)S(1)}, f32[560,128]{1,0:T(8,128)S(1)}, u32[]{:S(2)}, u32[]{:S(2)}) collective-permute-start(f32[560,128]{1,0:T(8,128)S(1)} %pad_maximum_fusion.mine), channel_id=1, source_target_pairs={{0,4},{2,6},{4,0},{6,2},{8,12},{10,14},{12,8},{14,10},{16,20},{18,... | collective-permute-start | bytes 860168 | tf_op jit(solution)/shard_map/ppermute | solution.py:538
  54.7 1.3 %collective-permute-start.6 = (f32[3,8,512]{2,1,0:T(8,128)S(1)}, f32[3,8,512]{2,1,0:T(8,128)S(1)}, u32[]{:S(2)}, u32[]{:S(2)}) collective-permute-start(f32[3,8,512]{2,1,0:T(8,128)S(1)} %get-tuple-element.18.mine), channel_id=1, source_target_pairs={{0,2},{2,0},{4,6},{6,4},{8,10},{10,8},{12,14},{14,12},{16,18},{18,... | collective-permute-start | bytes 147464 | tf_op jit(solution)/shard_map/ppermute | solution.py:538
  56.8 5.0 %copy-start.3 = (s32[1024,8]{0,1:T(8,128)S(1)}, s32[1024,8]{0,1:T(8,128)}, u32[]{:S(2)}) copy-start(s32[1024,8]{0,1:T(8,128)} %param.8) | copy-start | bytes 98308
  56.8 5.0 %copy-start.4 = (s32[1024]{0:T(1024)S(1)}, s32[1024]{0:T(1024)}, u32[]{:S(2)}) copy-start(s32[1024]{0:T(1024)} %param.9) | copy-start | bytes 12292
  56.9 4.9 %collective-permute-start.7 = (f32[24,1024]{1,0:T(8,128)S(1)}, f32[24,1024]{1,0:T(8,128)S(1)}, u32[]{:S(2)}, u32[]{:S(2)}) collective-permute-start(f32[24,1024]{1,0:T(8,128)S(1)} %get-tuple-element.26), channel_id=1, source_target_pairs={{0,1},{1,0},{2,3},{3,2},{4,5},{5,4},{6,7},{7,6},{8,9},{9,8},{10,11... | collective-permute-start | bytes 294920 | tf_op jit(solution)/shard_map/ppermute | solution.py:538
  63.3 1.2 %collective-permute-start.8 = (f32[16,256]{1,0:T(8,128)S(1)}, f32[16,256]{1,0:T(8,128)S(1)}, u32[]{:S(2)}, u32[]{:S(2)}) collective-permute-start(f32[16,256]{1,0:T(8,128)S(1)} %stacking.1), channel_id=1, source_target_pairs={{0,2},{2,0},{4,6},{6,4},{8,10},{10,8},{12,14},{14,12},{16,18},{18,... | collective-permute-start | bytes 49160 | tf_op jit(solution)/shard_map/ppermute | solution.py:538
  64.6 3.7 %collective-permute-start.9 = (f32[16,256]{1,0:T(8,128)S(1)}, f32[16,256]{1,0:T(8,128)S(1)}, u32[]{:S(2)}, u32[]{:S(2)}) collective-permute-start(f32[16,256]{1,0:T(8,128)S(1)} %add.38), channel_id=1, source_target_pairs={{0,4},{2,6},{4,0},{6,2},{8,12},{10,14},{12,8},{14,10},{16,20},{18,... | collective-permute-start | bytes 49160 | tf_op jit(solution)/shard_map/ppermute | solution.py:538
  68.3 3.7 %collective-permute-start.10 = (f32[16,256]{1,0:T(8,128)S(1)}, f32[16,256]{1,0:T(8,128)S(1)}, u32[]{:S(2)}, u32[]{:S(2)}) collective-permute-start(f32[16,256]{1,0:T(8,128)S(1)} %add.39), channel_id=1, source_target_pairs={{0,8},{2,10},{4,12},{6,14},{8,0},{10,2},{12,4},{14,6},{16,24},{18,... | collective-permute-start | bytes 49160 | tf_op jit(solution)/shard_map/ppermute | solution.py:538
  72.0 4.6 %collective-permute-start.11 = (f32[16,256]{1,0:T(8,128)S(1)}, f32[16,256]{1,0:T(8,128)S(1)}, u32[]{:S(2)}, u32[]{:S(2)}) collective-permute-start(f32[16,256]{1,0:T(8,128)S(1)} %add.40), channel_id=1, source_target_pairs={{0,16},{2,18},{4,20},{6,22},{8,24},{10,26},{12,28},{14,30},{16,0},... | collective-permute-start | bytes 49160 | tf_op jit(solution)/shard_map/ppermute | solution.py:538

commit v5 on v4

--- a/solution.py
+++ b/solution.py
@@ -85,13 +85,7 @@
     )
 
 
-def gram_kernel(markers, dosage, traits, observed, packed, padded, held, seen, arrived):
-    copies = [
-        pltpu.make_async_copy(traits, held, arrived.at[0]),
-        pltpu.make_async_copy(observed, seen, arrived.at[1]),
-    ]
-    for copy in copies:
-        copy.start()
+def gram_kernel(markers, dosage, masked, present, packed, padded):
     width, rows = padded.shape
     tiles = width // TILE
     edge = markers // 16 * 16
@@ -120,16 +114,12 @@
             packed[row:row + TILE, :] = jnp.where(upper, even, block)
         even = block
         diagonals.append(jnp.sum(jnp.where(eye, block, 0.0), axis=0, keepdims=True))
-    for copy in copies:
-        copy.wait()
-    values = held[...]
-    present = seen[...].astype(jnp.float32)
-    masked = present * values
+    masked, present = masked[...], present[...]
     high, middle, low = (part.astype(jnp.float32) for part in split_three(masked))
     ones = jnp.ones(present.shape, jnp.float32)
     extra = jnp.concatenate([high, middle, low, present, ones, ones], 0).astype(jnp.bfloat16)
     products = dot_bf16(extra, padded[...], NT)
-    sums = [jnp.sum(v, axis=1, keepdims=True) for v in (present, masked, masked * values)]
+    sums = [jnp.sum(v, axis=1, keepdims=True) for v in (present, masked, masked * masked)]
     for i in range(tiles):
         cols = slice(i * TILE, (i + 1) * TILE)
         row = i // 2 * HALF_ROWS + half_rows("side") + i % 2 * SIDE
@@ -146,73 +136,92 @@
     return ref.at[fit * TILE + first:fit * TILE + last, :]
 
 
-def eliminate(work, old, fits):
-    count, per, every = TILE // STEP, SUB // STEP, range(fits)
-    lane, lane_step = iota((fits, TILE), 1), iota((STEP, TILE), 1)
+def eliminate(work, old, flat, turned, fits):
+    per, every = SUB // STEP, range(fits)
+    lane, lane_step, row_step = iota((fits, TILE), 1), iota((STEP, TILE), 1), iota((STEP, TILE), 0)
     shape = (STEP, TILE)
-    for t in range(count):
-        base = t * STEP
-        rows = [work[pl.ds(base + i, fits, stride=TILE), :] for i in range(STEP)]
-        cells = [
-            [jnp.broadcast_to(rows[i][:, base + j:base + j + 1], rows[i].shape) for j in range(i + 1)]
-            for i in range(STEP)
+
+    def spread(value, column):
+        return jnp.broadcast_to(value[:, column:column + 1], value.shape)
+
+    for first in range(0, TILE, SUB):
+        last = first + SUB
+        groups = [
+            [own(work, f, first + g * STEP, first + (g + 1) * STEP)[...] for f in every]
+            for g in range(per)
         ]
-        inside = jnp.logical_and(lane >= base, lane < base + STEP)
-        for i in range(STEP):
-            rows[i] = jnp.where(inside, jnp.where(lane == base + i, 1.0, 0.0), rows[i])
-            old[pl.ds(base + i, fits, stride=TILE), :] = rows[i]
-        gains, inverses = {}, []
-        for j in range(STEP):
-            inverses.append(1.0 / cells[j][j])
-            for i in range(j + 1, STEP):
-                gains[i, j] = cells[i][j] * inverses[j]
-            for i in range(j + 1, STEP):
-                for m in range(j + 1, i + 1):
-                    cells[i][m] = cells[i][m] - gains[i, j] * cells[m][j]
-            for i in range(j + 1, STEP):
-                rows[i] = rows[i] - gains[i, j] * rows[j]
-        rows = [value * inverse for value, inverse in zip(rows, inverses)]
-        for j in reversed(range(1, STEP)):
-            for i in range(j):
-                rows[i] = rows[i] - gains[j, i] * rows[j]
-        for i in range(STEP):
-            work[pl.ds(base + i, fits, stride=TILE), :] = rows[i]
-        stop = (t // per + 1) * per
-        if t + 1 < stop:
-            spread = [
+        before = []
+        for t in range(per):
+            base = first + t * STEP
+            here, there = flat.at[t % 2], turned.at[t % 2]
+            for f in every:
+                here[f * STEP:(f + 1) * STEP, :] = groups[t][f]
+            ready = []
+            if t + 1 < per:
+                ready = [[spread(groups[t + 1][f], base + q) for f in every] for q in range(STEP)]
+            inside = jnp.logical_and(lane_step >= base, lane_step < base + STEP)
+            unit = jnp.where(lane_step == row_step + base, 1.0, 0.0)
+            before.append([jnp.where(inside, unit, groups[t][f]) for f in every])
+            if t + 1 == per and last < TILE:
+                lefts = []
+                for f in every:
+                    part = split_three(jnp.concatenate([rows[f] for rows in before], 0))
+                    lefts.append(jnp.transpose(jnp.concatenate([part[i] for i in (0, 0, 0, 1, 1, 2)], 0))[last:, :])
+            rows = [here[pl.ds(i, fits, stride=STEP), :] for i in range(STEP)]
+            cells = [[spread(rows[i], base + j) for j in range(i + 1)] for i in range(STEP)]
+            within = jnp.logical_and(lane >= base, lane < base + STEP)
+            for i in range(STEP):
+                rows[i] = jnp.where(within, jnp.where(lane == base + i, 1.0, 0.0), rows[i])
+            gains, inverses = {}, []
+            for j in range(STEP):
+                inverses.append(1.0 / cells[j][j])
+                for i in range(j + 1, STEP):
+                    gains[i, j] = cells[i][j] * inverses[j]
+                for i in range(j + 1, STEP):
+                    for m in range(j + 1, i + 1):
+                        cells[i][m] = cells[i][m] - gains[i, j] * cells[m][j]
+                for i in range(j + 1, STEP):
+                    rows[i] = rows[i] - gains[i, j] * rows[j]
+            rows = [value * inverse for value, inverse in zip(rows, inverses)]
+            for j in reversed(range(1, STEP)):
+                for i in range(j):
+                    rows[i] = rows[i] - gains[j, i] * rows[j]
+            for i in range(STEP):
+                there[pl.ds(i, fits, stride=STEP), :] = rows[i]
+            groups[t] = [there[f * STEP:(f + 1) * STEP, :] for f in every]
+            if t + 1 == per:
+                continue
+            wide = [
                 [
-                    jnp.broadcast_to(own(work, f, base + q, base + q + 1)[...], shape)
+                    jnp.broadcast_to(there[f * STEP + q:f * STEP + q + 1, :], shape)
                     for f in every
                 ]
                 for q in range(STEP)
             ]
-            inside = jnp.logical_and(lane_step >= base, lane_step < base + STEP)
-            for g in range(t + 1, stop):
-                refs = [own(work, f, g * STEP, (g + 1) * STEP) for f in every]
-                others = [ref[...] for ref in refs]
-                totals = [jnp.where(inside, 0.0, other) for other in others]
+            for g in range(t + 1, per):
+                if g > t + 1:
+                    ready = [[spread(groups[g][f], base + q) for f in every] for q in range(STEP)]
+                totals = [jnp.where(inside, 0.0, groups[g][f]) for f in every]
                 for q in range(STEP):
-                    for f in every:
-                        factor = jnp.broadcast_to(others[f][:, base + q:base + q + 1], shape)
-                        totals[f] = totals[f] - factor * spread[q][f]
-                for f in every:
-                    refs[f][...] = totals[f]
-        elif stop < count:
-            first, last = (t + 1 - per) * STEP, stop * STEP
+                    totals = [totals[f] - ready[q][f] * wide[q][f] for f in every]
+                groups[g] = totals
+        for f in every:
+            own(work, f, first, last)[...] = jnp.concatenate([rows[f] for rows in groups], 0)
+            own(old, f, first, last)[...] = jnp.concatenate([rows[f] for rows in before], 0)
+        if last < TILE:
             line, column = iota((SUB, TILE), 0) + first, iota((SUB, TILE), 1)
             keep = jnp.logical_or(column >= last, column // STEP <= line // STEP)
             column = iota((TILE - last, TILE), 1)
             done = jnp.logical_and(column >= first, column < last)
-            lefts, rights = [], []
+            rights = []
             for f in every:
-                left = split_three(own(old, f, first, last)[...])
-                right = split_three(jnp.where(keep, own(work, f, first, last)[...], 0.0))
-                lefts.append(jnp.concatenate([left[i] for i in (0, 0, 0, 1, 1, 2)], 0))
-                rights.append(jnp.concatenate([right[i] for i in (0, 1, 2, 0, 1, 0)], 0))
-            terms = [dot_bf16(a, b, TN) for a, b in zip(lefts, rights)]
+                part = jnp.where(keep, jnp.concatenate([rows[f] for rows in groups], 0), 0.0)
+                part = split_three(part)
+                rights.append(jnp.concatenate([part[i] for i in (0, 1, 2, 0, 1, 0)], 0))
+            terms = [dot_bf16(a, b) for a, b in zip(lefts, rights)]
             for f in every:
                 rest = own(work, f, last)
-                rest[...] = jnp.where(done, 0.0, rest[...]) - terms[f][last:, :]
+                rest[...] = jnp.where(done, 0.0, rest[...]) - terms[f]
 
 
 class Half:
@@ -261,14 +270,15 @@
     return jnp.where(keep, value, 0.0)
 
 
-def first_kernel(samples, markers, penalty, place, mine, lefts, rights, above, weights, work, old):
+def first_kernel(samples, markers, penalty, place, mine, lefts, rights, above, weights, work, old,
+                 flat, turned):
     fits = lefts.shape[0]
     every = range(fits)
     half = Half(mine, 2 * place[2], samples, markers)
     first, between, second = half.centred()
     for f in every:
         own(work, f)[...] = first + half.ridge(0, penalty[f])
-    eliminate(work, old, fits)
+    eliminate(work, old, flat, turned, fits)
     for f in every:
         lefts[f, 0], rights[f, 0] = lower_part(own(old, f)[...]), lower_part(own(work, f)[...])
     parts = right_parts(between)
@@ -283,14 +293,14 @@
     for f in every:
         above[f], weights[f] = both[f][:TILE], both[f][TILE:]
         own(work, f)[...] = second - after[f] + half.ridge(1, penalty[f])
-    eliminate(work, old, fits)
+    eliminate(work, old, flat, turned, fits)
     for f in every:
         lefts[f, 1], rights[f, 1] = lower_part(own(old, f)[...]), lower_part(own(work, f)[...])
 
 
 def second_kernel(
     samples, markers, penalty, place, mine, theirs, lefts, rights, above, weights,
-    out, stats, centre, wide, work, old, rhs, scratch,
+    out, stats, centre, wide, work, old, flat, turned, rhs, scratch,
 ):
     fits = out.shape[0]
     every = range(fits)
@@ -345,11 +355,16 @@
 
     def side_step(k, left, right, later):
         lo, hi = k * TILE, (k + 1) * TILE
-        turned = [dot(rhs[f, :, lo:hi], left[f], NT) for f in every]
+        turned = products(
+            [left_parts(rhs[f, :, lo:hi]) for f in every],
+            [right_parts(jnp.transpose(left[f])) for f in every],
+        )
+        value = [right[f] if later is None else jnp.concatenate([right[f], later[f]], 1) for f in every]
+        value = products([left_parts(turned[f]) for f in every], [right_parts(v) for v in value])
         for f in every:
-            rhs[f, :, lo:hi] = dot(turned[f], right[f])
+            rhs[f, :, lo:hi] = value[f][:, :TILE]
             if later is not None:
-                rhs[f, :, hi:] = rhs[f, :, hi:] - dot(turned[f], later[f])
+                rhs[f, :, hi:] = rhs[f, :, hi:] - value[f][:, TILE:]
 
     parts = right_parts(rows[0])
     both = products(stacked(0), [parts for f in every])
@@ -392,7 +407,7 @@
     for f in every:
         wide[f, 1, :, 2 * TILE:] = final[f]
 
-    eliminate(work, old, fits)
+    eliminate(work, old, flat, turned, fits)
     left = [lower_part(own(old, f)[...]) for f in every]
     right = [lower_part(own(work, f)[...]) for f in every]
     both = products(
@@ -408,7 +423,7 @@
     final = products([left_parts(jnp.transpose(left[f])) for f in every], parts)
     for f in every:
         wide[f, 2, :, 3 * TILE:] = final[f]
-    eliminate(work, old, fits)
+    eliminate(work, old, flat, turned, fits)
     left = [lower_part(own(old, f)[...]) for f in every]
     right = [lower_part(own(work, f)[...]) for f in every]
     side_step(3, left, right, None)
@@ -452,7 +467,7 @@
         out[...] = total
 
 
-def stack_kernel(pairs, per_share, place, mine, other, stats, traits, observed, folds, out):
+def stack_kernel(pairs, per_share, place, mine, other, stats, masked, present, folds, out):
     first = place[1] * per_share
     if pairs:
         second = place[1] == 1
@@ -463,8 +478,8 @@
         levels = mine[...]
     count, samples = levels.shape
     height, width = out.shape
-    present = observed[...].astype(jnp.float32)
-    scaled = present * (traits[...] - stats[:, 0:1]) / stats[:, 1:2]
+    present = present[...]
+    scaled = (masked[...] - present * stats[:, 0:1]) / stats[:, 1:2]
     pick = iota((count, TRAITS), 1) == first + iota((count, TRAITS), 0) % per_share
     spread = dot_bf16(
         jnp.where(pick, 1.0, 0.0).astype(jnp.bfloat16), present.astype(jnp.bfloat16)
@@ -567,7 +582,8 @@
     odd = position % 2
     late = position // 2 % 2
     place = jnp.stack([odd, block, late]).astype(jnp.int32)
-    traits, observed = traits.T, observed.T
+    present = observed.T.astype(jnp.float32)
+    masked = present * traits.T
 
     whole = lambda shape: pl.BlockSpec(shape, lambda _: (0, 0))
     packed, padded = pl.pallas_call(
@@ -577,16 +593,11 @@
             f32((2 * HALF_ROWS, TILE)),
             jax.ShapeDtypeStruct((width, local_rows), jnp.bfloat16),
         ],
-        in_specs=[whole((width, local_rows))] + [pl.BlockSpec(memory_space=pltpu.HBM)] * 2,
+        in_specs=[whole((width, local_rows)), whole(masked.shape), whole(present.shape)],
         out_specs=[whole((2 * HALF_ROWS, TILE)), whole((width, local_rows))],
-        scratch_shapes=[
-            pltpu.VMEM(traits.shape, traits.dtype),
-            pltpu.VMEM(observed.shape, observed.dtype),
-            pltpu.SemaphoreType.DMA((2,)),
-        ],
         compiler_params=pltpu.CompilerParams(vmem_limit_bytes=VMEM_BYTES),
         name="local_gram",
-    )(genotypes.T, traits, observed)
+    )(genotypes.T, masked, present)
     quarters = packed.reshape(2, 2, HALF_ROWS // 2, TILE)
     up = odd == 1
     keep = jnp.where(up, quarters[:, 1], quarters[:, 0])
@@ -607,11 +618,13 @@
         jnp.array(penalties[:HALF], jnp.float32),
     )
     square = (HALF, TILE, TILE)
+    blocks = [pltpu.VMEM((HALF * TILE, TILE), jnp.float32)] * 2
+    turns = [pltpu.VMEM((2, HALF * STEP, TILE), jnp.float32)] * 2
     started = call(
         functools.partial(first_kernel, samples, markers),
         [f32((HALF, 2, TILE, TILE)), f32((HALF, 2, TILE, TILE)), f32(square), f32(square)],
         ["smem", "smem", "vmem"],
-        [pltpu.VMEM((HALF * TILE, TILE), jnp.float32)] * 2,
+        blocks + turns,
         "first_fits",
         cost=pl.CostEstimate(flops=4 * 10**9, bytes_accessed=2**21, transcendentals=0),
     )(penalty, place, half)
@@ -621,8 +634,8 @@
         ["smem", "smem"] + ["vmem"] * 6,
         [
             pltpu.VMEM((HALF, TILES, TILE, width), jnp.float32),
-            pltpu.VMEM((HALF * TILE, TILE), jnp.float32),
-            pltpu.VMEM((HALF * TILE, TILE), jnp.float32),
+            *blocks,
+            *turns,
             pltpu.VMEM((HALF, TRAITS, width), jnp.float32),
             pltpu.VMEM((HALF, 2, TILE, TILE), jnp.float32),
         ],
@@ -655,7 +668,7 @@
         ["smem"] + ["vmem"] * 6,
         [],
         "stacking",
-    )(place, mine, theirs, stats, traits, observed, fold_index[None, :])
+    )(place, mine, theirs, stats, masked, present, fold_index[None, :])
     products = sum_over(products, "samp")
     gram, cross = call(
         functools.partial(scale_kernel, per_share, block_devices, samples),

time: 78.2 us -> 75.8 us (0.969)
  Pallas kernels: 29.6 us -> 28 us
  local copies, waits for them, and re-layouts: 2.75 us -> 1.26 us
  other arithmetic: 0.32 us -> 1.15 us
    unnamed x14 -> x12, local copies, waits for them, and re-layouts: 2.74 us -> 1.24 us
    pallas_call x1, Pallas kernels: 15.1 us -> 14 us  [body(): call(functools.partial(second_kernel, samples, markers), [f32((HALF, TRAI...]
    convert_element_type x0 -> x1, other arithmetic: none -> 0.82 us  [body(): present = observed.T.astype(jnp.float32)]
where the time goes in v5:
time: 75.8 us; the launch traced here: 75.6 us
  waiting for transfers between devices  29.9 us (39%)
  Pallas kernels  28 us (37%)
  starting transfers between devices  14.5 us (19%)
  local copies, waits for them, and re-layouts  1.26 us (2%)
  other arithmetic  1.15 us (2%)
  between operations  0.82 us (1%)
    ppermute x12, waiting for transfers between devices, swap(): return lax.ppermute(value, axis, [(i, i ^ mask) for i in range(size)])  29.9 us
    ppermute x12, starting transfers between devices, swap(): return lax.ppermute(value, axis, [(i, i ^ mask) for i in range(size)])  14.5 us
    pallas_call x1, Pallas kernels, body(): call(functools.partial(second_kernel, samples, markers), [f32((HALF, TRAI...  14 us
    pallas_call x1, Pallas kernels, body(): call(functools.partial(first_kernel, samples, markers), [f32((HALF, 2, TI...  9.15 us
    pallas_call x1, Pallas kernels, body(): call(functools.partial(stack_kernel, pairs, per_share), f32((height, lane...  1.54 us
  transfers between devices with their start and end apart: 12, of which 11 were waited for; matrix products, arithmetic and copies ran while one was open for 0% of the time, Pallas kernels for 12%

profile of v5, /device:TPU:0, one launch (start us, length us, event | category | flops | bytes accessed | tf_op | source)
XLA Modules:
  0.0 75.6 jit_solution(11203660624208536971)
XLA Ops:
  0.7 0.8 %convert_bitcast_fusion.present = f32[8,1024]{1,0:T(8,128)S(1)} fusion(s32[1024,8]{0,1:T(8,128)} %param.8), kind=kLoop, calls=%fused_computation.12 | loop fusion | flops 8192 | bytes 65536 | tf_op jit(solution)/shard_map/convert_element_type | solution.py:585
  1.5 1.2 %copy-done = bf16[1024,500]{0,1:T(8,128)(2,1)S(1)} copy-done((bf16[1024,500]{0,1:T(8,128)(2,1)S(1)}, bf16[1024,500]{0,1:T(8,128)(2,1)}, u32[]{:S(2)}) %copy-start) | copy-done | bytes 1024024
  2.7 1.2 %local_gram.1 = (f32[1120,128]{1,0:T(8,128)S(1)}, bf16[512,1024]{1,0:T(8,128)(2,1)S(1)}) custom-call(bf16[500,1024]{1,0:T(8,128)(2,1)S(1)} %bitcast.40, f32[8,1024]{1,0:T(8,128)S(1)} %bitcast_multiply_fusion.masked, f32[8,1024]{1,0:T(8,128)S(1)} %convert_bitcast_fusion.present), custom_call_target="tpu_custom_call" | custom-call | tf_op jit(solution)/shard_map/local_gram/pallas_call | solution.py:589
  4.0 0.5 collective-permute-start
  4.5 1.2 %collective-permute-done = f32[2,280,128]{2,1,0:T(8,128)S(1)} collective-permute-done((f32[2,280,128]{2,1,0:T(8,128)S(1)}, f32[2,280,128]{2,1,0:T(8,128)S(1)}, u32[]{:S(2)}, u32[]{:S(2)}) %collective-permute-start) | collective-permute-done | bytes 286752 | tf_op jit(solution)/shard_map/ppermute | solution.py:553
  5.7 0.1 bitcast_add_fusion
  5.8 2.9 %collective-permute-start.1 = (f32[280,128]{1,0:T(8,128)S(1)}, f32[280,128]{1,0:T(8,128)S(1)}, u32[]{:S(2)}, u32[]{:S(2)}) collective-permute-start(f32[280,128]{1,0:T(8,128)S(1)} %select_bitcast_fusion.1), channel_id=1, source_target_pairs={{0,4},{2,6},{4,0},{6,2},{8,12},{10,14},{12,8},{14,10},{16,20},{18,... | collective-permute-start | bytes 430088 | tf_op jit(solution)/shard_map/ppermute | solution.py:553
  8.7 4.1 %collective-permute-done.1 = f32[280,128]{1,0:T(8,128)S(1)} collective-permute-done((f32[280,128]{1,0:T(8,128)S(1)}, f32[280,128]{1,0:T(8,128)S(1)}, u32[]{:S(2)}, u32[]{:S(2)}) %collective-permute-start.1) | collective-permute-done | bytes 143392 | tf_op jit(solution)/shard_map/ppermute | solution.py:553
  12.8 1.9 %collective-permute-start.2 = (f32[280,128]{1,0:T(8,128)S(1)}, f32[280,128]{1,0:T(8,128)S(1)}, u32[]{:S(2)}, u32[]{:S(2)}) collective-permute-start(f32[280,128]{1,0:T(8,128)S(1)} %bitcast_add_fusion.1), channel_id=1, source_target_pairs={{0,8},{2,10},{4,12},{6,14},{8,0},{10,2},{12,4},{14,6},{16,24},{18,... | collective-permute-start | bytes 430088 | tf_op jit(solution)/shard_map/ppermute | solution.py:553
  14.7 3.5 %collective-permute-done.2 = f32[280,128]{1,0:T(8,128)S(1)} collective-permute-done((f32[280,128]{1,0:T(8,128)S(1)}, f32[280,128]{1,0:T(8,128)S(1)}, u32[]{:S(2)}, u32[]{:S(2)}) %collective-permute-start.2) | collective-permute-done | bytes 143392 | tf_op jit(solution)/shard_map/ppermute | solution.py:553
  18.2 0.0 copy-start.4
  18.2 2.7 %collective-permute-start.3 = (f32[280,128]{1,0:T(8,128)S(1)}, f32[280,128]{1,0:T(8,128)S(1)}, u32[]{:S(2)}, u32[]{:S(2)}) collective-permute-start(f32[280,128]{1,0:T(8,128)S(1)} %add.36), channel_id=1, source_target_pairs={{0,16},{2,18},{4,20},{6,22},{8,24},{10,26},{12,28},{14,30},{16,0},... | collective-permute-start | bytes 430088 | tf_op jit(solution)/shard_map/ppermute | solution.py:553
  20.9 5.7 %collective-permute-done.3 = f32[280,128]{1,0:T(8,128)S(1)} collective-permute-done((f32[280,128]{1,0:T(8,128)S(1)}, f32[280,128]{1,0:T(8,128)S(1)}, u32[]{:S(2)}, u32[]{:S(2)}) %collective-permute-start.3) | collective-permute-done | bytes 143392 | tf_op jit(solution)/shard_map/ppermute | solution.py:553
  26.7 0.1 collective-permute-start.4
  26.8 0.1 pad_add_fusion.place
  26.9 1.2 %collective-permute-done.4 = f32[280,128]{1,0:T(8,128)S(1)} collective-permute-done((f32[280,128]{1,0:T(8,128)S(1)}, f32[280,128]{1,0:T(8,128)S(1)}, u32[]{:S(2)}, u32[]{:S(2)}) %collective-permute-start.4) | collective-permute-done | bytes 143392 | tf_op jit(solution)/shard_map/ppermute | solution.py:553
  28.2 1.0 %collective-permute-start.5 = (f32[560,128]{1,0:T(8,128)S(1)}, f32[560,128]{1,0:T(8,128)S(1)}, u32[]{:S(2)}, u32[]{:S(2)}) collective-permute-start(f32[560,128]{1,0:T(8,128)S(1)} %pad_maximum_fusion.mine), channel_id=1, source_target_pairs={{0,4},{2,6},{4,0},{6,2},{8,12},{10,14},{12,8},{14,10},{16,20},{18,... | collective-permute-start | bytes 860168 | tf_op jit(solution)/shard_map/ppermute | solution.py:553
  29.2 9.1 %first_fits.1 = (f32[3,2,128,128]{3,2,1,0:T(8,128)S(1)}, f32[3,2,128,128]{3,2,1,0:T(8,128)S(1)}, f32[3,128,128]{2,1,0:T(8,128)S(1)}, f32[3,128,128]{2,1,0:T(8,128)S(1)}) custom-call(f32[3]{0:T(128)S(1)} %broadcast_select_fusion.2.penalty, s32[3]{0:T(128)S(1)} %pad_add_fusion.place, f32[560,128]{1,0:T(8,128)S(1)} %pad_maximum_fusion.mine), custom_call_target="tpu_custom_call" | custom-call | flops 4000000000 | bytes 2097152 | tf_op jit(solution)/shard_map/first_fits/pallas_call | solution.py:623
  38.4 14.0 %second_fits.1 = (f32[3,8,512]{2,1,0:T(8,128)S(1)}, f32[8,128]{1,0:T(8,128)S(1)}, f32[8,512]{1,0:T(8,128)S(1)}) custom-call(f32[3]{0:T(128)S(1)} %broadcast_select_fusion.2.penalty, s32[3]{0:T(128)S(1)} %pad_add_fusion.place, f32[560,128]{1,0:T(8,128)S(1)} %pad_maximum_fusion.mine, f32[560,128]{1,0:T(8,128)S(1)} %collective-permute-done.5.theirs, ...), custom_call_target="tpu_custom_call" | custom-call | tf_op jit(solution)/shard_map/second_fits/pallas_call | solution.py:631
  52.4 1.3 %collective-permute-done.6.other = f32[3,8,512]{2,1,0:T(8,128)S(1)} collective-permute-done((f32[3,8,512]{2,1,0:T(8,128)S(1)}, f32[3,8,512]{2,1,0:T(8,128)S(1)}, u32[]{:S(2)}, u32[]{:S(2)}) %collective-permute-start.6) | collective-permute-done | bytes 49184 | tf_op jit(solution)/shard_map/ppermute | solution.py:553
  53.6 0.9 %predictions.1 = f32[2,24,1024]{2,1,0:T(8,128)S(1)} custom-call(s32[3]{0:T(128)S(1)} %pad_add_fusion.place, f32[3,8,512]{2,1,0:T(8,128)S(1)} %get-tuple-element.18.mine, f32[3,8,512]{2,1,0:T(8,128)S(1)} %collective-permute-done.6.other, f32[8,512]{1,0:T(8,128)S(1)} %get-tuple-element.19.centre, bf16[512,1024]{1,0:T(8,128)(2,1)S(1)} %get-tuple-element.20.padded), custom_call_target="tpu_custom_call" | custom-call | tf_op jit(solution)/shard_map/predictions/pallas_call | solution.py:648
  54.6 1.6 %collective-permute-start.7 = (f32[24,1024]{1,0:T(8,128)S(1)}, f32[24,1024]{1,0:T(8,128)S(1)}, u32[]{:S(2)}, u32[]{:S(2)}) collective-permute-start(f32[24,1024]{1,0:T(8,128)S(1)} %get-tuple-element.26), channel_id=1, source_target_pairs={{0,1},{1,0},{2,3},{3,2},{4,5},{5,4},{6,7},{7,6},{8,9},{9,8},{10,11... | collective-permute-start | bytes 294920 | tf_op jit(solution)/shard_map/ppermute | solution.py:553
  56.1 3.3 %collective-permute-done.7.other = f32[24,1024]{1,0:T(8,128)S(1)} collective-permute-done((f32[24,1024]{1,0:T(8,128)S(1)}, f32[24,1024]{1,0:T(8,128)S(1)}, u32[]{:S(2)}, u32[]{:S(2)}) %collective-permute-start.7) | collective-permute-done | bytes 98336 | tf_op jit(solution)/shard_map/ppermute | solution.py:553
  59.5 1.5 %stacking.1 = f32[16,256]{1,0:T(8,128)S(1)} custom-call(s32[3]{0:T(128)S(1)} %pad_add_fusion.place, f32[24,1024]{1,0:T(8,128)S(1)} %get-tuple-element.27.mine, f32[24,1024]{1,0:T(8,128)S(1)} %collective-permute-done.7.other, f32[8,128]{1,0:T(8,128)S(1)} %get-tuple-element.21.stats, f32[8,1024]{1,0:T(8,128)S(1)} %bitcast_multiply_fusion.masked, ...), custom_call_target="tpu_custom_call" | custom-call | tf_op jit(solution)/shard_map/stacking/pallas_call | solution.py:665
  61.0 1.2 %collective-permute-done.8 = f32[16,256]{1,0:T(8,128)S(1)} collective-permute-done((f32[16,256]{1,0:T(8,128)S(1)}, f32[16,256]{1,0:T(8,128)S(1)}, u32[]{:S(2)}, u32[]{:S(2)}) %collective-permute-start.8) | collective-permute-done | bytes 16416 | tf_op jit(solution)/shard_map/ppermute | solution.py:553
  62.2 1.0 %collective-permute-start.9 = (f32[16,256]{1,0:T(8,128)S(1)}, f32[16,256]{1,0:T(8,128)S(1)}, u32[]{:S(2)}, u32[]{:S(2)}) collective-permute-start(f32[16,256]{1,0:T(8,128)S(1)} %add.38), channel_id=1, source_target_pairs={{0,4},{2,6},{4,0},{6,2},{8,12},{10,14},{12,8},{14,10},{16,20},{18,... | collective-permute-start | bytes 49160 | tf_op jit(solution)/shard_map/ppermute | solution.py:553
  63.3 2.7 %collective-permute-done.9 = f32[16,256]{1,0:T(8,128)S(1)} collective-permute-done((f32[16,256]{1,0:T(8,128)S(1)}, f32[16,256]{1,0:T(8,128)S(1)}, u32[]{:S(2)}, u32[]{:S(2)}) %collective-permute-start.9) | collective-permute-done | bytes 16416 | tf_op jit(solution)/shard_map/ppermute | solution.py:553
  66.0 0.7 collective-permute-start.10
  66.7 3.1 %collective-permute-done.10 = f32[16,256]{1,0:T(8,128)S(1)} collective-permute-done((f32[16,256]{1,0:T(8,128)S(1)}, f32[16,256]{1,0:T(8,128)S(1)}, u32[]{:S(2)}, u32[]{:S(2)}) %collective-permute-start.10) | collective-permute-done | bytes 16416 | tf_op jit(solution)/shard_map/ppermute | solution.py:553
  69.7 2.0 %collective-permute-start.11 = (f32[16,256]{1,0:T(8,128)S(1)}, f32[16,256]{1,0:T(8,128)S(1)}, u32[]{:S(2)}, u32[]{:S(2)}) collective-permute-start(f32[16,256]{1,0:T(8,128)S(1)} %add.40), channel_id=1, source_target_pairs={{0,16},{2,18},{4,20},{6,22},{8,24},{10,26},{12,28},{14,30},{16,0},... | collective-permute-start | bytes 49160 | tf_op jit(solution)/shard_map/ppermute | solution.py:553
  71.8 2.6 %collective-permute-done.11 = f32[16,256]{1,0:T(8,128)S(1)} collective-permute-done((f32[16,256]{1,0:T(8,128)S(1)}, f32[16,256]{1,0:T(8,128)S(1)}, u32[]{:S(2)}, u32[]{:S(2)}) %collective-permute-start.11) | collective-permute-done | bytes 16416 | tf_op jit(solution)/shard_map/ppermute | solution.py:553
  74.4 1.2 %standardize.1 = (f32[5,10,4,10]{3,2,1,0:T(4,128)}, f32[5,4,10]{2,1,0:T(4,128)}) custom-call(f32[16,256]{1,0:T(8,128)S(1)} %add.41.total), custom_call_target="tpu_custom_call" | custom-call | tf_op jit(solution)/shard_map/standardize/pallas_call | solution.py:673
  (27 shorter events, 0.2 us)
Async XLA Ops:
  0.6 0.8 %copy-start.2 = (s32[1024,8]{0,1:T(8,128)S(1)}, s32[1024,8]{0,1:T(8,128)}, u32[]{:S(2)}) copy-start(s32[1024,8]{0,1:T(8,128)} %param.8) | copy-start | bytes 98308
  0.7 0.8 %copy-start.3 = (f32[1024,8]{0,1:T(8,128)S(1)}, f32[1024,8]{0,1:T(8,128)}, u32[]{:S(2)}) copy-start(f32[1024,8]{0,1:T(8,128)} %param.7) | copy-start | bytes 98308
  1.5 1.2 %copy-start = (bf16[1024,500]{0,1:T(8,128)(2,1)S(1)}, bf16[1024,500]{0,1:T(8,128)(2,1)}, u32[]{:S(2)}) copy-start(bf16[1024,500]{0,1:T(8,128)(2,1)} %param.6) | copy-start | bytes 3072004
  4.0 1.7 %collective-permute-start = (f32[2,280,128]{2,1,0:T(8,128)S(1)}, f32[2,280,128]{2,1,0:T(8,128)S(1)}, u32[]{:S(2)}, u32[]{:S(2)}) collective-permute-start(f32[2,280,128]{2,1,0:T(8,128)S(1)} %select_bitcast_fusion), channel_id=1, source_target_pairs={{0,2},{2,0},{4,6},{6,4},{8,10},{10,8},{12,14},{14,12},{16,18},{18,... | collective-permute-start | bytes 860168 | tf_op jit(solution)/shard_map/ppermute | solution.py:553
  5.8 7.0 %collective-permute-start.1 = (f32[280,128]{1,0:T(8,128)S(1)}, f32[280,128]{1,0:T(8,128)S(1)}, u32[]{:S(2)}, u32[]{:S(2)}) collective-permute-start(f32[280,128]{1,0:T(8,128)S(1)} %select_bitcast_fusion.1), channel_id=1, source_target_pairs={{0,4},{2,6},{4,0},{6,2},{8,12},{10,14},{12,8},{14,10},{16,20},{18,... | collective-permute-start | bytes 430088 | tf_op jit(solution)/shard_map/ppermute | solution.py:553
  12.8 5.4 %collective-permute-start.2 = (f32[280,128]{1,0:T(8,128)S(1)}, f32[280,128]{1,0:T(8,128)S(1)}, u32[]{:S(2)}, u32[]{:S(2)}) collective-permute-start(f32[280,128]{1,0:T(8,128)S(1)} %bitcast_add_fusion.1), channel_id=1, source_target_pairs={{0,8},{2,10},{4,12},{6,14},{8,0},{10,2},{12,4},{14,6},{16,24},{18,... | collective-permute-start | bytes 430088 | tf_op jit(solution)/shard_map/ppermute | solution.py:553
  18.2 8.6 %copy-start.4 = (f32[3]{0:T(128)S(1)}, f32[3]{0:T(128)}, u32[]{:S(2)}) copy-start(f32[3]{0:T(128)} %constant.42.clone) | copy-start | bytes 40
  18.2 8.6 %copy-start.5 = (f32[3]{0:T(128)S(1)}, f32[3]{0:T(128)}, u32[]{:S(2)}) copy-start(f32[3]{0:T(128)} %constant.41.clone) | copy-start | bytes 40
  18.2 8.4 %collective-permute-start.3 = (f32[280,128]{1,0:T(8,128)S(1)}, f32[280,128]{1,0:T(8,128)S(1)}, u32[]{:S(2)}, u32[]{:S(2)}) collective-permute-start(f32[280,128]{1,0:T(8,128)S(1)} %add.36), channel_id=1, source_target_pairs={{0,16},{2,18},{4,20},{6,22},{8,24},{10,26},{12,28},{14,30},{16,0},... | collective-permute-start | bytes 430088 | tf_op jit(solution)/shard_map/ppermute | solution.py:553
  26.7 1.4 %collective-permute-start.4 = (f32[280,128]{1,0:T(8,128)S(1)}, f32[280,128]{1,0:T(8,128)S(1)}, u32[]{:S(2)}, u32[]{:S(2)}) collective-permute-start(f32[280,128]{1,0:T(8,128)S(1)} %add.37), channel_id=1, source_target_pairs={{0,2},{2,0},{4,6},{6,4},{8,10},{10,8},{12,14},{14,12},{16,18},{18,... | collective-permute-start | bytes 430088 | tf_op jit(solution)/shard_map/ppermute | solution.py:553
  28.2 10.2 %collective-permute-start.5 = (f32[560,128]{1,0:T(8,128)S(1)}, f32[560,128]{1,0:T(8,128)S(1)}, u32[]{:S(2)}, u32[]{:S(2)}) collective-permute-start(f32[560,128]{1,0:T(8,128)S(1)} %pad_maximum_fusion.mine), channel_id=1, source_target_pairs={{0,4},{2,6},{4,0},{6,2},{8,12},{10,14},{12,8},{14,10},{16,20},{18,... | collective-permute-start | bytes 860168 | tf_op jit(solution)/shard_map/ppermute | solution.py:553
  52.4 1.3 %collective-permute-start.6 = (f32[3,8,512]{2,1,0:T(8,128)S(1)}, f32[3,8,512]{2,1,0:T(8,128)S(1)}, u32[]{:S(2)}, u32[]{:S(2)}) collective-permute-start(f32[3,8,512]{2,1,0:T(8,128)S(1)} %get-tuple-element.18.mine), channel_id=1, source_target_pairs={{0,2},{2,0},{4,6},{6,4},{8,10},{10,8},{12,14},{14,12},{16,18},{18,... | collective-permute-start | bytes 147464 | tf_op jit(solution)/shard_map/ppermute | solution.py:553
  54.6 4.9 %copy-start.1 = (s32[1024]{0:T(1024)S(1)}, s32[1024]{0:T(1024)}, u32[]{:S(2)}) copy-start(s32[1024]{0:T(1024)} %param.9) | copy-start | bytes 12292
  54.6 4.9 %collective-permute-start.7 = (f32[24,1024]{1,0:T(8,128)S(1)}, f32[24,1024]{1,0:T(8,128)S(1)}, u32[]{:S(2)}, u32[]{:S(2)}) collective-permute-start(f32[24,1024]{1,0:T(8,128)S(1)} %get-tuple-element.26), channel_id=1, source_target_pairs={{0,1},{1,0},{2,3},{3,2},{4,5},{5,4},{6,7},{7,6},{8,9},{9,8},{10,11... | collective-permute-start | bytes 294920 | tf_op jit(solution)/shard_map/ppermute | solution.py:553
  61.0 1.2 %collective-permute-start.8 = (f32[16,256]{1,0:T(8,128)S(1)}, f32[16,256]{1,0:T(8,128)S(1)}, u32[]{:S(2)}, u32[]{:S(2)}) collective-permute-start(f32[16,256]{1,0:T(8,128)S(1)} %stacking.1), channel_id=1, source_target_pairs={{0,2},{2,0},{4,6},{6,4},{8,10},{10,8},{12,14},{14,12},{16,18},{18,... | collective-permute-start | bytes 49160 | tf_op jit(solution)/shard_map/ppermute | solution.py:553
  62.2 3.7 %collective-permute-start.9 = (f32[16,256]{1,0:T(8,128)S(1)}, f32[16,256]{1,0:T(8,128)S(1)}, u32[]{:S(2)}, u32[]{:S(2)}) collective-permute-start(f32[16,256]{1,0:T(8,128)S(1)} %add.38), channel_id=1, source_target_pairs={{0,4},{2,6},{4,0},{6,2},{8,12},{10,14},{12,8},{14,10},{16,20},{18,... | collective-permute-start | bytes 49160 | tf_op jit(solution)/shard_map/ppermute | solution.py:553
  66.0 3.7 %collective-permute-start.10 = (f32[16,256]{1,0:T(8,128)S(1)}, f32[16,256]{1,0:T(8,128)S(1)}, u32[]{:S(2)}, u32[]{:S(2)}) collective-permute-start(f32[16,256]{1,0:T(8,128)S(1)} %add.39), channel_id=1, source_target_pairs={{0,8},{2,10},{4,12},{6,14},{8,0},{10,2},{12,4},{14,6},{16,24},{18,... | collective-permute-start | bytes 49160 | tf_op jit(solution)/shard_map/ppermute | solution.py:553
  69.7 4.6 %collective-permute-start.11 = (f32[16,256]{1,0:T(8,128)S(1)}, f32[16,256]{1,0:T(8,128)S(1)}, u32[]{:S(2)}, u32[]{:S(2)}) collective-permute-start(f32[16,256]{1,0:T(8,128)S(1)} %add.40), channel_id=1, source_target_pairs={{0,16},{2,18},{4,20},{6,22},{8,24},{10,26},{12,28},{14,30},{16,0},... | collective-permute-start | bytes 49160 | tf_op jit(solution)/shard_map/ppermute | solution.py:553

commit v6 on v5

--- a/solution.py
+++ b/solution.py
@@ -429,7 +429,8 @@
     side_step(3, left, right, None)
     for k in reversed(range(TILES - 1)):
         lo, hi = k * TILE, (k + 1) * TILE
-        known = [dot(rhs[f, :, hi:], wide[f, k, :, hi:], NT) for f in every]
+        known = [right_parts(jnp.transpose(wide[f, k, :, hi:])) for f in every]
+        known = products([left_parts(rhs[f, :, hi:]) for f in every], known)
         for f in every:
             rhs[f, :, lo:hi] = rhs[f, :, lo:hi] - known[f]
     for f in every:

time: 75.8 us -> 74.9 us (0.988)
  Pallas kernels: 28 us -> 27 us
    pallas_call x1, Pallas kernels: 14 us -> 13.1 us  [body(): call(functools.partial(second_kernel, samples, markers), [f32((HALF, TRAI...]
where the time goes in v6:
time: 74.9 us; the launch traced here: 74.7 us
  waiting for transfers between devices  29.8 us (40%)
  Pallas kernels  27 us (36%)
  starting transfers between devices  14.6 us (19%)
  local copies, waits for them, and re-layouts  1.26 us (2%)
  other arithmetic  1.15 us (2%)
  between operations  0.83 us (1%)
    ppermute x12, waiting for transfers between devices, swap(): return lax.ppermute(value, axis, [(i, i ^ mask) for i in range(size)])  29.8 us
    ppermute x12, starting transfers between devices, swap(): return lax.ppermute(value, axis, [(i, i ^ mask) for i in range(size)])  14.6 us
    pallas_call x1, Pallas kernels, body(): call(functools.partial(second_kernel, samples, markers), [f32((HALF, TRAI...  13.1 us
    pallas_call x1, Pallas kernels, body(): call(functools.partial(first_kernel, samples, markers), [f32((HALF, 2, TI...  9.15 us
    pallas_call x1, Pallas kernels, body(): call(functools.partial(stack_kernel, pairs, per_share), f32((height, lane...  1.53 us
  transfers between devices with their start and end apart: 12, of which 11 were waited for; matrix products, arithmetic and copies ran while one was open for 0% of the time, Pallas kernels for 12%

profile of v6, /device:TPU:0, one launch (start us, length us, event | category | flops | bytes accessed | tf_op | source)
XLA Modules:
  0.0 74.7 jit_solution(4419442665326534102)
XLA Ops:
  0.7 0.8 %convert_bitcast_fusion.present = f32[8,1024]{1,0:T(8,128)S(1)} fusion(s32[1024,8]{0,1:T(8,128)} %param.8), kind=kLoop, calls=%fused_computation.12 | loop fusion | flops 8192 | bytes 65536 | tf_op jit(solution)/shard_map/convert_element_type | solution.py:586
  1.5 1.2 %copy-done = bf16[1024,500]{0,1:T(8,128)(2,1)S(1)} copy-done((bf16[1024,500]{0,1:T(8,128)(2,1)S(1)}, bf16[1024,500]{0,1:T(8,128)(2,1)}, u32[]{:S(2)}) %copy-start) | copy-done | bytes 1024024
  2.7 1.2 %local_gram.1 = (f32[1120,128]{1,0:T(8,128)S(1)}, bf16[512,1024]{1,0:T(8,128)(2,1)S(1)}) custom-call(bf16[500,1024]{1,0:T(8,128)(2,1)S(1)} %bitcast.40, f32[8,1024]{1,0:T(8,128)S(1)} %bitcast_multiply_fusion.masked, f32[8,1024]{1,0:T(8,128)S(1)} %convert_bitcast_fusion.present), custom_call_target="tpu_custom_call" | custom-call | tf_op jit(solution)/shard_map/local_gram/pallas_call | solution.py:590
  4.0 0.5 collective-permute-start
  4.5 1.2 %collective-permute-done = f32[2,280,128]{2,1,0:T(8,128)S(1)} collective-permute-done((f32[2,280,128]{2,1,0:T(8,128)S(1)}, f32[2,280,128]{2,1,0:T(8,128)S(1)}, u32[]{:S(2)}, u32[]{:S(2)}) %collective-permute-start) | collective-permute-done | bytes 286752 | tf_op jit(solution)/shard_map/ppermute | solution.py:554
  5.7 0.1 bitcast_add_fusion
  5.8 2.9 %collective-permute-start.1 = (f32[280,128]{1,0:T(8,128)S(1)}, f32[280,128]{1,0:T(8,128)S(1)}, u32[]{:S(2)}, u32[]{:S(2)}) collective-permute-start(f32[280,128]{1,0:T(8,128)S(1)} %select_bitcast_fusion.1), channel_id=1, source_target_pairs={{0,4},{2,6},{4,0},{6,2},{8,12},{10,14},{12,8},{14,10},{16,20},{18,... | collective-permute-start | bytes 430088 | tf_op jit(solution)/shard_map/ppermute | solution.py:554
  8.7 4.1 %collective-permute-done.1 = f32[280,128]{1,0:T(8,128)S(1)} collective-permute-done((f32[280,128]{1,0:T(8,128)S(1)}, f32[280,128]{1,0:T(8,128)S(1)}, u32[]{:S(2)}, u32[]{:S(2)}) %collective-permute-start.1) | collective-permute-done | bytes 143392 | tf_op jit(solution)/shard_map/ppermute | solution.py:554
  12.8 1.9 %collective-permute-start.2 = (f32[280,128]{1,0:T(8,128)S(1)}, f32[280,128]{1,0:T(8,128)S(1)}, u32[]{:S(2)}, u32[]{:S(2)}) collective-permute-start(f32[280,128]{1,0:T(8,128)S(1)} %bitcast_add_fusion.1), channel_id=1, source_target_pairs={{0,8},{2,10},{4,12},{6,14},{8,0},{10,2},{12,4},{14,6},{16,24},{18,... | collective-permute-start | bytes 430088 | tf_op jit(solution)/shard_map/ppermute | solution.py:554
  14.7 3.5 %collective-permute-done.2 = f32[280,128]{1,0:T(8,128)S(1)} collective-permute-done((f32[280,128]{1,0:T(8,128)S(1)}, f32[280,128]{1,0:T(8,128)S(1)}, u32[]{:S(2)}, u32[]{:S(2)}) %collective-permute-start.2) | collective-permute-done | bytes 143392 | tf_op jit(solution)/shard_map/ppermute | solution.py:554
  18.2 2.7 %collective-permute-start.3 = (f32[280,128]{1,0:T(8,128)S(1)}, f32[280,128]{1,0:T(8,128)S(1)}, u32[]{:S(2)}, u32[]{:S(2)}) collective-permute-start(f32[280,128]{1,0:T(8,128)S(1)} %add.36), channel_id=1, source_target_pairs={{0,16},{2,18},{4,20},{6,22},{8,24},{10,26},{12,28},{14,30},{16,0},... | collective-permute-start | bytes 430088 | tf_op jit(solution)/shard_map/ppermute | solution.py:554
  20.9 5.7 %collective-permute-done.3 = f32[280,128]{1,0:T(8,128)S(1)} collective-permute-done((f32[280,128]{1,0:T(8,128)S(1)}, f32[280,128]{1,0:T(8,128)S(1)}, u32[]{:S(2)}, u32[]{:S(2)}) %collective-permute-start.3) | collective-permute-done | bytes 143392 | tf_op jit(solution)/shard_map/ppermute | solution.py:554
  26.7 0.1 collective-permute-start.4
  26.8 0.1 pad_add_fusion.place
  26.9 1.2 %collective-permute-done.4 = f32[280,128]{1,0:T(8,128)S(1)} collective-permute-done((f32[280,128]{1,0:T(8,128)S(1)}, f32[280,128]{1,0:T(8,128)S(1)}, u32[]{:S(2)}, u32[]{:S(2)}) %collective-permute-start.4) | collective-permute-done | bytes 143392 | tf_op jit(solution)/shard_map/ppermute | solution.py:554
  28.2 1.0 %collective-permute-start.5 = (f32[560,128]{1,0:T(8,128)S(1)}, f32[560,128]{1,0:T(8,128)S(1)}, u32[]{:S(2)}, u32[]{:S(2)}) collective-permute-start(f32[560,128]{1,0:T(8,128)S(1)} %pad_maximum_fusion.mine), channel_id=1, source_target_pairs={{0,4},{2,6},{4,0},{6,2},{8,12},{10,14},{12,8},{14,10},{16,20},{18,... | collective-permute-start | bytes 860168 | tf_op jit(solution)/shard_map/ppermute | solution.py:554
  29.2 9.1 %first_fits.1 = (f32[3,2,128,128]{3,2,1,0:T(8,128)S(1)}, f32[3,2,128,128]{3,2,1,0:T(8,128)S(1)}, f32[3,128,128]{2,1,0:T(8,128)S(1)}, f32[3,128,128]{2,1,0:T(8,128)S(1)}) custom-call(f32[3]{0:T(128)S(1)} %broadcast_select_fusion.2.penalty, s32[3]{0:T(128)S(1)} %pad_add_fusion.place, f32[560,128]{1,0:T(8,128)S(1)} %pad_maximum_fusion.mine), custom_call_target="tpu_custom_call" | custom-call | flops 4000000000 | bytes 2097152 | tf_op jit(solution)/shard_map/first_fits/pallas_call | solution.py:624
  38.4 13.1 %second_fits.1 = (f32[3,8,512]{2,1,0:T(8,128)S(1)}, f32[8,128]{1,0:T(8,128)S(1)}, f32[8,512]{1,0:T(8,128)S(1)}) custom-call(f32[3]{0:T(128)S(1)} %broadcast_select_fusion.2.penalty, s32[3]{0:T(128)S(1)} %pad_add_fusion.place, f32[560,128]{1,0:T(8,128)S(1)} %pad_maximum_fusion.mine, f32[560,128]{1,0:T(8,128)S(1)} %collective-permute-done.5.theirs, ...), custom_call_target="tpu_custom_call" | custom-call | tf_op jit(solution)/shard_map/second_fits/pallas_call | solution.py:632
  51.5 0.1 collective-permute-start.6
  51.5 1.2 %collective-permute-done.6.other = f32[3,8,512]{2,1,0:T(8,128)S(1)} collective-permute-done((f32[3,8,512]{2,1,0:T(8,128)S(1)}, f32[3,8,512]{2,1,0:T(8,128)S(1)}, u32[]{:S(2)}, u32[]{:S(2)}) %collective-permute-start.6) | collective-permute-done | bytes 49184 | tf_op jit(solution)/shard_map/ppermute | solution.py:554
  52.8 0.9 %predictions.1 = f32[2,24,1024]{2,1,0:T(8,128)S(1)} custom-call(s32[3]{0:T(128)S(1)} %pad_add_fusion.place, f32[3,8,512]{2,1,0:T(8,128)S(1)} %get-tuple-element.18.mine, f32[3,8,512]{2,1,0:T(8,128)S(1)} %collective-permute-done.6.other, f32[8,512]{1,0:T(8,128)S(1)} %get-tuple-element.19.centre, bf16[512,1024]{1,0:T(8,128)(2,1)S(1)} %get-tuple-element.20.padded), custom_call_target="tpu_custom_call" | custom-call | tf_op jit(solution)/shard_map/predictions/pallas_call | solution.py:649
  53.7 1.6 %collective-permute-start.7 = (f32[24,1024]{1,0:T(8,128)S(1)}, f32[24,1024]{1,0:T(8,128)S(1)}, u32[]{:S(2)}, u32[]{:S(2)}) collective-permute-start(f32[24,1024]{1,0:T(8,128)S(1)} %get-tuple-element.26), channel_id=1, source_target_pairs={{0,1},{1,0},{2,3},{3,2},{4,5},{5,4},{6,7},{7,6},{8,9},{9,8},{10,11... | collective-permute-start | bytes 294920 | tf_op jit(solution)/shard_map/ppermute | solution.py:554
  55.2 3.4 %collective-permute-done.7.other = f32[24,1024]{1,0:T(8,128)S(1)} collective-permute-done((f32[24,1024]{1,0:T(8,128)S(1)}, f32[24,1024]{1,0:T(8,128)S(1)}, u32[]{:S(2)}, u32[]{:S(2)}) %collective-permute-start.7) | collective-permute-done | bytes 98336 | tf_op jit(solution)/shard_map/ppermute | solution.py:554
  58.6 1.5 %stacking.1 = f32[16,256]{1,0:T(8,128)S(1)} custom-call(s32[3]{0:T(128)S(1)} %pad_add_fusion.place, f32[24,1024]{1,0:T(8,128)S(1)} %get-tuple-element.27.mine, f32[24,1024]{1,0:T(8,128)S(1)} %collective-permute-done.7.other, f32[8,128]{1,0:T(8,128)S(1)} %get-tuple-element.21.stats, f32[8,1024]{1,0:T(8,128)S(1)} %bitcast_multiply_fusion.masked, ...), custom_call_target="tpu_custom_call" | custom-call | tf_op jit(solution)/shard_map/stacking/pallas_call | solution.py:666
  60.1 1.2 %collective-permute-done.8 = f32[16,256]{1,0:T(8,128)S(1)} collective-permute-done((f32[16,256]{1,0:T(8,128)S(1)}, f32[16,256]{1,0:T(8,128)S(1)}, u32[]{:S(2)}, u32[]{:S(2)}) %collective-permute-start.8) | collective-permute-done | bytes 16416 | tf_op jit(solution)/shard_map/ppermute | solution.py:554
  61.4 1.1 %collective-permute-start.9 = (f32[16,256]{1,0:T(8,128)S(1)}, f32[16,256]{1,0:T(8,128)S(1)}, u32[]{:S(2)}, u32[]{:S(2)}) collective-permute-start(f32[16,256]{1,0:T(8,128)S(1)} %add.38), channel_id=1, source_target_pairs={{0,4},{2,6},{4,0},{6,2},{8,12},{10,14},{12,8},{14,10},{16,20},{18,... | collective-permute-start | bytes 49160 | tf_op jit(solution)/shard_map/ppermute | solution.py:554
  62.4 2.7 %collective-permute-done.9 = f32[16,256]{1,0:T(8,128)S(1)} collective-permute-done((f32[16,256]{1,0:T(8,128)S(1)}, f32[16,256]{1,0:T(8,128)S(1)}, u32[]{:S(2)}, u32[]{:S(2)}) %collective-permute-start.9) | collective-permute-done | bytes 16416 | tf_op jit(solution)/shard_map/ppermute | solution.py:554
  65.1 0.7 collective-permute-start.10
  65.8 3.1 %collective-permute-done.10 = f32[16,256]{1,0:T(8,128)S(1)} collective-permute-done((f32[16,256]{1,0:T(8,128)S(1)}, f32[16,256]{1,0:T(8,128)S(1)}, u32[]{:S(2)}, u32[]{:S(2)}) %collective-permute-start.10) | collective-permute-done | bytes 16416 | tf_op jit(solution)/shard_map/ppermute | solution.py:554
  68.8 2.0 %collective-permute-start.11 = (f32[16,256]{1,0:T(8,128)S(1)}, f32[16,256]{1,0:T(8,128)S(1)}, u32[]{:S(2)}, u32[]{:S(2)}) collective-permute-start(f32[16,256]{1,0:T(8,128)S(1)} %add.40), channel_id=1, source_target_pairs={{0,16},{2,18},{4,20},{6,22},{8,24},{10,26},{12,28},{14,30},{16,0},... | collective-permute-start | bytes 49160 | tf_op jit(solution)/shard_map/ppermute | solution.py:554
  70.9 2.6 %collective-permute-done.11 = f32[16,256]{1,0:T(8,128)S(1)} collective-permute-done((f32[16,256]{1,0:T(8,128)S(1)}, f32[16,256]{1,0:T(8,128)S(1)}, u32[]{:S(2)}, u32[]{:S(2)}) %collective-permute-start.11) | collective-permute-done | bytes 16416 | tf_op jit(solution)/shard_map/ppermute | solution.py:554
  73.5 1.2 %standardize.1 = (f32[5,10,4,10]{3,2,1,0:T(4,128)}, f32[5,4,10]{2,1,0:T(4,128)}) custom-call(f32[16,256]{1,0:T(8,128)S(1)} %add.41.total), custom_call_target="tpu_custom_call" | custom-call | tf_op jit(solution)/shard_map/standardize/pallas_call | solution.py:674
  (27 shorter events, 0.2 us)
Async XLA Ops:
  0.6 0.8 %copy-start.2 = (s32[1024,8]{0,1:T(8,128)S(1)}, s32[1024,8]{0,1:T(8,128)}, u32[]{:S(2)}) copy-start(s32[1024,8]{0,1:T(8,128)} %param.8) | copy-start | bytes 98308
  0.7 0.8 %copy-start.3 = (f32[1024,8]{0,1:T(8,128)S(1)}, f32[1024,8]{0,1:T(8,128)}, u32[]{:S(2)}) copy-start(f32[1024,8]{0,1:T(8,128)} %param.7) | copy-start | bytes 98308
  1.5 1.2 %copy-start = (bf16[1024,500]{0,1:T(8,128)(2,1)S(1)}, bf16[1024,500]{0,1:T(8,128)(2,1)}, u32[]{:S(2)}) copy-start(bf16[1024,500]{0,1:T(8,128)(2,1)} %param.6) | copy-start | bytes 3072004
  4.0 1.7 %collective-permute-start = (f32[2,280,128]{2,1,0:T(8,128)S(1)}, f32[2,280,128]{2,1,0:T(8,128)S(1)}, u32[]{:S(2)}, u32[]{:S(2)}) collective-permute-start(f32[2,280,128]{2,1,0:T(8,128)S(1)} %select_bitcast_fusion), channel_id=1, source_target_pairs={{0,2},{2,0},{4,6},{6,4},{8,10},{10,8},{12,14},{14,12},{16,18},{18,... | collective-permute-start | bytes 860168 | tf_op jit(solution)/shard_map/ppermute | solution.py:554
  5.8 7.0 %collective-permute-start.1 = (f32[280,128]{1,0:T(8,128)S(1)}, f32[280,128]{1,0:T(8,128)S(1)}, u32[]{:S(2)}, u32[]{:S(2)}) collective-permute-start(f32[280,128]{1,0:T(8,128)S(1)} %select_bitcast_fusion.1), channel_id=1, source_target_pairs={{0,4},{2,6},{4,0},{6,2},{8,12},{10,14},{12,8},{14,10},{16,20},{18,... | collective-permute-start | bytes 430088 | tf_op jit(solution)/shard_map/ppermute | solution.py:554
  12.8 5.4 %collective-permute-start.2 = (f32[280,128]{1,0:T(8,128)S(1)}, f32[280,128]{1,0:T(8,128)S(1)}, u32[]{:S(2)}, u32[]{:S(2)}) collective-permute-start(f32[280,128]{1,0:T(8,128)S(1)} %bitcast_add_fusion.1), channel_id=1, source_target_pairs={{0,8},{2,10},{4,12},{6,14},{8,0},{10,2},{12,4},{14,6},{16,24},{18,... | collective-permute-start | bytes 430088 | tf_op jit(solution)/shard_map/ppermute | solution.py:554
  18.2 8.6 %copy-start.4 = (f32[3]{0:T(128)S(1)}, f32[3]{0:T(128)}, u32[]{:S(2)}) copy-start(f32[3]{0:T(128)} %constant.42.clone) | copy-start | bytes 40
  18.2 8.6 %copy-start.5 = (f32[3]{0:T(128)S(1)}, f32[3]{0:T(128)}, u32[]{:S(2)}) copy-start(f32[3]{0:T(128)} %constant.41.clone) | copy-start | bytes 40
  18.2 8.4 %collective-permute-start.3 = (f32[280,128]{1,0:T(8,128)S(1)}, f32[280,128]{1,0:T(8,128)S(1)}, u32[]{:S(2)}, u32[]{:S(2)}) collective-permute-start(f32[280,128]{1,0:T(8,128)S(1)} %add.36), channel_id=1, source_target_pairs={{0,16},{2,18},{4,20},{6,22},{8,24},{10,26},{12,28},{14,30},{16,0},... | collective-permute-start | bytes 430088 | tf_op jit(solution)/shard_map/ppermute | solution.py:554
  26.7 1.4 %collective-permute-start.4 = (f32[280,128]{1,0:T(8,128)S(1)}, f32[280,128]{1,0:T(8,128)S(1)}, u32[]{:S(2)}, u32[]{:S(2)}) collective-permute-start(f32[280,128]{1,0:T(8,128)S(1)} %add.37), channel_id=1, source_target_pairs={{0,2},{2,0},{4,6},{6,4},{8,10},{10,8},{12,14},{14,12},{16,18},{18,... | collective-permute-start | bytes 430088 | tf_op jit(solution)/shard_map/ppermute | solution.py:554
  28.2 10.2 %collective-permute-start.5 = (f32[560,128]{1,0:T(8,128)S(1)}, f32[560,128]{1,0:T(8,128)S(1)}, u32[]{:S(2)}, u32[]{:S(2)}) collective-permute-start(f32[560,128]{1,0:T(8,128)S(1)} %pad_maximum_fusion.mine), channel_id=1, source_target_pairs={{0,4},{2,6},{4,0},{6,2},{8,12},{10,14},{12,8},{14,10},{16,20},{18,... | collective-permute-start | bytes 860168 | tf_op jit(solution)/shard_map/ppermute | solution.py:554
  51.5 1.3 %collective-permute-start.6 = (f32[3,8,512]{2,1,0:T(8,128)S(1)}, f32[3,8,512]{2,1,0:T(8,128)S(1)}, u32[]{:S(2)}, u32[]{:S(2)}) collective-permute-start(f32[3,8,512]{2,1,0:T(8,128)S(1)} %get-tuple-element.18.mine), channel_id=1, source_target_pairs={{0,2},{2,0},{4,6},{6,4},{8,10},{10,8},{12,14},{14,12},{16,18},{18,... | collective-permute-start | bytes 147464 | tf_op jit(solution)/shard_map/ppermute | solution.py:554
  53.7 5.0 %copy-start.1 = (s32[1024]{0:T(1024)S(1)}, s32[1024]{0:T(1024)}, u32[]{:S(2)}) copy-start(s32[1024]{0:T(1024)} %param.9) | copy-start | bytes 12292
  53.7 4.9 %collective-permute-start.7 = (f32[24,1024]{1,0:T(8,128)S(1)}, f32[24,1024]{1,0:T(8,128)S(1)}, u32[]{:S(2)}, u32[]{:S(2)}) collective-permute-start(f32[24,1024]{1,0:T(8,128)S(1)} %get-tuple-element.26), channel_id=1, source_target_pairs={{0,1},{1,0},{2,3},{3,2},{4,5},{5,4},{6,7},{7,6},{8,9},{9,8},{10,11... | collective-permute-start | bytes 294920 | tf_op jit(solution)/shard_map/ppermute | solution.py:554
  60.1 1.2 %collective-permute-start.8 = (f32[16,256]{1,0:T(8,128)S(1)}, f32[16,256]{1,0:T(8,128)S(1)}, u32[]{:S(2)}, u32[]{:S(2)}) collective-permute-start(f32[16,256]{1,0:T(8,128)S(1)} %stacking.1), channel_id=1, source_target_pairs={{0,2},{2,0},{4,6},{6,4},{8,10},{10,8},{12,14},{14,12},{16,18},{18,... | collective-permute-start | bytes 49160 | tf_op jit(solution)/shard_map/ppermute | solution.py:554
  61.4 3.7 %collective-permute-start.9 = (f32[16,256]{1,0:T(8,128)S(1)}, f32[16,256]{1,0:T(8,128)S(1)}, u32[]{:S(2)}, u32[]{:S(2)}) collective-permute-start(f32[16,256]{1,0:T(8,128)S(1)} %add.38), channel_id=1, source_target_pairs={{0,4},{2,6},{4,0},{6,2},{8,12},{10,14},{12,8},{14,10},{16,20},{18,... | collective-permute-start | bytes 49160 | tf_op jit(solution)/shard_map/ppermute | solution.py:554
  65.1 3.7 %collective-permute-start.10 = (f32[16,256]{1,0:T(8,128)S(1)}, f32[16,256]{1,0:T(8,128)S(1)}, u32[]{:S(2)}, u32[]{:S(2)}) collective-permute-start(f32[16,256]{1,0:T(8,128)S(1)} %add.39), channel_id=1, source_target_pairs={{0,8},{2,10},{4,12},{6,14},{8,0},{10,2},{12,4},{14,6},{16,24},{18,... | collective-permute-start | bytes 49160 | tf_op jit(solution)/shard_map/ppermute | solution.py:554
  68.8 4.6 %collective-permute-start.11 = (f32[16,256]{1,0:T(8,128)S(1)}, f32[16,256]{1,0:T(8,128)S(1)}, u32[]{:S(2)}, u32[]{:S(2)}) collective-permute-start(f32[16,256]{1,0:T(8,128)S(1)} %add.40), channel_id=1, source_target_pairs={{0,16},{2,18},{4,20},{6,22},{8,24},{10,26},{12,28},{14,30},{16,0},... | collective-permute-start | bytes 49160 | tf_op jit(solution)/shard_map/ppermute | solution.py:554

commit v7 on v6

--- a/solution.py
+++ b/solution.py
@@ -620,7 +620,7 @@
     )
     square = (HALF, TILE, TILE)
     blocks = [pltpu.VMEM((HALF * TILE, TILE), jnp.float32)] * 2
-    turns = [pltpu.VMEM((2, HALF * STEP, TILE), jnp.float32)] * 2
+    turns = [pltpu.VMEM((2, (HALF + 1) * STEP, TILE), jnp.float32)] * 2
     started = call(
         functools.partial(first_kernel, samples, markers),
         [f32((HALF, 2, TILE, TILE)), f32((HALF, 2, TILE, TILE)), f32(square), f32(square)],

time: 74.9 us -> 74.9 us (level)
  no operation moved by 1% of the time
where the time goes in v7:
time: 74.9 us; the launch traced here: 74.7 us
  waiting for transfers between devices  29.8 us (40%)
  Pallas kernels  27 us (36%)
  starting transfers between devices  14.6 us (19%)
  local copies, waits for them, and re-layouts  1.26 us (2%)
  other arithmetic  1.15 us (2%)
  between operations  0.83 us (1%)
    ppermute x12, waiting for transfers between devices, swap(): return lax.ppermute(value, axis, [(i, i ^ mask) for i in range(size)])  29.8 us
    ppermute x12, starting transfers between devices, swap(): return lax.ppermute(value, axis, [(i, i ^ mask) for i in range(size)])  14.6 us
    pallas_call x1, Pallas kernels, body(): call(functools.partial(second_kernel, samples, markers), [f32((HALF, TRAI...  13.1 us
    pallas_call x1, Pallas kernels, body(): call(functools.partial(first_kernel, samples, markers), [f32((HALF, 2, TI...  9.14 us
    pallas_call x1, Pallas kernels, body(): call(functools.partial(stack_kernel, pairs, per_share), f32((height, lane...  1.54 us
  transfers between devices with their start and end apart: 12, of which 11 were waited for; matrix products, arithmetic and copies ran while one was open for 0% of the time, Pallas kernels for 12%

profile of v7, /device:TPU:0, one launch (start us, length us, event | category | flops | bytes accessed | tf_op | source)
XLA Modules:
  0.0 74.7 jit_solution(9414258305477908255)
XLA Ops:
  0.7 0.8 %convert_bitcast_fusion.present = f32[8,1024]{1,0:T(8,128)S(1)} fusion(s32[1024,8]{0,1:T(8,128)} %param.8), kind=kLoop, calls=%fused_computation.12 | loop fusion | flops 8192 | bytes 65536 | tf_op jit(solution)/shard_map/convert_element_type | solution.py:586
  1.5 1.2 %copy-done = bf16[1024,500]{0,1:T(8,128)(2,1)S(1)} copy-done((bf16[1024,500]{0,1:T(8,128)(2,1)S(1)}, bf16[1024,500]{0,1:T(8,128)(2,1)}, u32[]{:S(2)}) %copy-start) | copy-done | bytes 1024024
  2.7 1.2 %local_gram.1 = (f32[1120,128]{1,0:T(8,128)S(1)}, bf16[512,1024]{1,0:T(8,128)(2,1)S(1)}) custom-call(bf16[500,1024]{1,0:T(8,128)(2,1)S(1)} %bitcast.40, f32[8,1024]{1,0:T(8,128)S(1)} %bitcast_multiply_fusion.masked, f32[8,1024]{1,0:T(8,128)S(1)} %convert_bitcast_fusion.present), custom_call_target="tpu_custom_call" | custom-call | tf_op jit(solution)/shard_map/local_gram/pallas_call | solution.py:590
  4.0 0.5 collective-permute-start
  4.5 1.2 %collective-permute-done = f32[2,280,128]{2,1,0:T(8,128)S(1)} collective-permute-done((f32[2,280,128]{2,1,0:T(8,128)S(1)}, f32[2,280,128]{2,1,0:T(8,128)S(1)}, u32[]{:S(2)}, u32[]{:S(2)}) %collective-permute-start) | collective-permute-done | bytes 286752 | tf_op jit(solution)/shard_map/ppermute | solution.py:554
  5.7 0.1 bitcast_add_fusion
  5.8 2.9 %collective-permute-start.1 = (f32[280,128]{1,0:T(8,128)S(1)}, f32[280,128]{1,0:T(8,128)S(1)}, u32[]{:S(2)}, u32[]{:S(2)}) collective-permute-start(f32[280,128]{1,0:T(8,128)S(1)} %select_bitcast_fusion.1), channel_id=1, source_target_pairs={{0,4},{2,6},{4,0},{6,2},{8,12},{10,14},{12,8},{14,10},{16,20},{18,... | collective-permute-start | bytes 430088 | tf_op jit(solution)/shard_map/ppermute | solution.py:554
  8.7 4.1 %collective-permute-done.1 = f32[280,128]{1,0:T(8,128)S(1)} collective-permute-done((f32[280,128]{1,0:T(8,128)S(1)}, f32[280,128]{1,0:T(8,128)S(1)}, u32[]{:S(2)}, u32[]{:S(2)}) %collective-permute-start.1) | collective-permute-done | bytes 143392 | tf_op jit(solution)/shard_map/ppermute | solution.py:554
  12.8 1.9 %collective-permute-start.2 = (f32[280,128]{1,0:T(8,128)S(1)}, f32[280,128]{1,0:T(8,128)S(1)}, u32[]{:S(2)}, u32[]{:S(2)}) collective-permute-start(f32[280,128]{1,0:T(8,128)S(1)} %bitcast_add_fusion.1), channel_id=1, source_target_pairs={{0,8},{2,10},{4,12},{6,14},{8,0},{10,2},{12,4},{14,6},{16,24},{18,... | collective-permute-start | bytes 430088 | tf_op jit(solution)/shard_map/ppermute | solution.py:554
  14.7 3.5 %collective-permute-done.2 = f32[280,128]{1,0:T(8,128)S(1)} collective-permute-done((f32[280,128]{1,0:T(8,128)S(1)}, f32[280,128]{1,0:T(8,128)S(1)}, u32[]{:S(2)}, u32[]{:S(2)}) %collective-permute-start.2) | collective-permute-done | bytes 143392 | tf_op jit(solution)/shard_map/ppermute | solution.py:554
  18.2 2.7 %collective-permute-start.3 = (f32[280,128]{1,0:T(8,128)S(1)}, f32[280,128]{1,0:T(8,128)S(1)}, u32[]{:S(2)}, u32[]{:S(2)}) collective-permute-start(f32[280,128]{1,0:T(8,128)S(1)} %add.36), channel_id=1, source_target_pairs={{0,16},{2,18},{4,20},{6,22},{8,24},{10,26},{12,28},{14,30},{16,0},... | collective-permute-start | bytes 430088 | tf_op jit(solution)/shard_map/ppermute | solution.py:554
  20.9 5.7 %collective-permute-done.3 = f32[280,128]{1,0:T(8,128)S(1)} collective-permute-done((f32[280,128]{1,0:T(8,128)S(1)}, f32[280,128]{1,0:T(8,128)S(1)}, u32[]{:S(2)}, u32[]{:S(2)}) %collective-permute-start.3) | collective-permute-done | bytes 143392 | tf_op jit(solution)/shard_map/ppermute | solution.py:554
  26.7 0.1 collective-permute-start.4
  26.8 0.1 pad_add_fusion.place
  26.9 1.2 %collective-permute-done.4 = f32[280,128]{1,0:T(8,128)S(1)} collective-permute-done((f32[280,128]{1,0:T(8,128)S(1)}, f32[280,128]{1,0:T(8,128)S(1)}, u32[]{:S(2)}, u32[]{:S(2)}) %collective-permute-start.4) | collective-permute-done | bytes 143392 | tf_op jit(solution)/shard_map/ppermute | solution.py:554
  28.2 1.0 %collective-permute-start.5 = (f32[560,128]{1,0:T(8,128)S(1)}, f32[560,128]{1,0:T(8,128)S(1)}, u32[]{:S(2)}, u32[]{:S(2)}) collective-permute-start(f32[560,128]{1,0:T(8,128)S(1)} %pad_maximum_fusion.mine), channel_id=1, source_target_pairs={{0,4},{2,6},{4,0},{6,2},{8,12},{10,14},{12,8},{14,10},{16,20},{18,... | collective-permute-start | bytes 860168 | tf_op jit(solution)/shard_map/ppermute | solution.py:554
  29.2 9.1 %first_fits.1 = (f32[3,2,128,128]{3,2,1,0:T(8,128)S(1)}, f32[3,2,128,128]{3,2,1,0:T(8,128)S(1)}, f32[3,128,128]{2,1,0:T(8,128)S(1)}, f32[3,128,128]{2,1,0:T(8,128)S(1)}) custom-call(f32[3]{0:T(128)S(1)} %broadcast_select_fusion.2.penalty, s32[3]{0:T(128)S(1)} %pad_add_fusion.place, f32[560,128]{1,0:T(8,128)S(1)} %pad_maximum_fusion.mine), custom_call_target="tpu_custom_call" | custom-call | flops 4000000000 | bytes 2097152 | tf_op jit(solution)/shard_map/first_fits/pallas_call | solution.py:624
  38.4 13.1 %second_fits.1 = (f32[3,8,512]{2,1,0:T(8,128)S(1)}, f32[8,128]{1,0:T(8,128)S(1)}, f32[8,512]{1,0:T(8,128)S(1)}) custom-call(f32[3]{0:T(128)S(1)} %broadcast_select_fusion.2.penalty, s32[3]{0:T(128)S(1)} %pad_add_fusion.place, f32[560,128]{1,0:T(8,128)S(1)} %pad_maximum_fusion.mine, f32[560,128]{1,0:T(8,128)S(1)} %collective-permute-done.5.theirs, ...), custom_call_target="tpu_custom_call" | custom-call | tf_op jit(solution)/shard_map/second_fits/pallas_call | solution.py:632
  51.5 0.1 collective-permute-start.6
  51.5 1.2 %collective-permute-done.6.other = f32[3,8,512]{2,1,0:T(8,128)S(1)} collective-permute-done((f32[3,8,512]{2,1,0:T(8,128)S(1)}, f32[3,8,512]{2,1,0:T(8,128)S(1)}, u32[]{:S(2)}, u32[]{:S(2)}) %collective-permute-start.6) | collective-permute-done | bytes 49184 | tf_op jit(solution)/shard_map/ppermute | solution.py:554
  52.8 0.9 %predictions.1 = f32[2,24,1024]{2,1,0:T(8,128)S(1)} custom-call(s32[3]{0:T(128)S(1)} %pad_add_fusion.place, f32[3,8,512]{2,1,0:T(8,128)S(1)} %get-tuple-element.18.mine, f32[3,8,512]{2,1,0:T(8,128)S(1)} %collective-permute-done.6.other, f32[8,512]{1,0:T(8,128)S(1)} %get-tuple-element.19.centre, bf16[512,1024]{1,0:T(8,128)(2,1)S(1)} %get-tuple-element.20.padded), custom_call_target="tpu_custom_call" | custom-call | tf_op jit(solution)/shard_map/predictions/pallas_call | solution.py:649
  53.7 1.6 %collective-permute-start.7 = (f32[24,1024]{1,0:T(8,128)S(1)}, f32[24,1024]{1,0:T(8,128)S(1)}, u32[]{:S(2)}, u32[]{:S(2)}) collective-permute-start(f32[24,1024]{1,0:T(8,128)S(1)} %get-tuple-element.26), channel_id=1, source_target_pairs={{0,1},{1,0},{2,3},{3,2},{4,5},{5,4},{6,7},{7,6},{8,9},{9,8},{10,11... | collective-permute-start | bytes 294920 | tf_op jit(solution)/shard_map/ppermute | solution.py:554
  55.3 3.4 %collective-permute-done.7.other = f32[24,1024]{1,0:T(8,128)S(1)} collective-permute-done((f32[24,1024]{1,0:T(8,128)S(1)}, f32[24,1024]{1,0:T(8,128)S(1)}, u32[]{:S(2)}, u32[]{:S(2)}) %collective-permute-start.7) | collective-permute-done | bytes 98336 | tf_op jit(solution)/shard_map/ppermute | solution.py:554
  58.6 1.5 %stacking.1 = f32[16,256]{1,0:T(8,128)S(1)} custom-call(s32[3]{0:T(128)S(1)} %pad_add_fusion.place, f32[24,1024]{1,0:T(8,128)S(1)} %get-tuple-element.27.mine, f32[24,1024]{1,0:T(8,128)S(1)} %collective-permute-done.7.other, f32[8,128]{1,0:T(8,128)S(1)} %get-tuple-element.21.stats, f32[8,1024]{1,0:T(8,128)S(1)} %bitcast_multiply_fusion.masked, ...), custom_call_target="tpu_custom_call" | custom-call | tf_op jit(solution)/shard_map/stacking/pallas_call | solution.py:666
  60.1 1.2 %collective-permute-done.8 = f32[16,256]{1,0:T(8,128)S(1)} collective-permute-done((f32[16,256]{1,0:T(8,128)S(1)}, f32[16,256]{1,0:T(8,128)S(1)}, u32[]{:S(2)}, u32[]{:S(2)}) %collective-permute-start.8) | collective-permute-done | bytes 16416 | tf_op jit(solution)/shard_map/ppermute | solution.py:554
  61.4 1.1 %collective-permute-start.9 = (f32[16,256]{1,0:T(8,128)S(1)}, f32[16,256]{1,0:T(8,128)S(1)}, u32[]{:S(2)}, u32[]{:S(2)}) collective-permute-start(f32[16,256]{1,0:T(8,128)S(1)} %add.38), channel_id=1, source_target_pairs={{0,4},{2,6},{4,0},{6,2},{8,12},{10,14},{12,8},{14,10},{16,20},{18,... | collective-permute-start | bytes 49160 | tf_op jit(solution)/shard_map/ppermute | solution.py:554
  62.4 2.7 %collective-permute-done.9 = f32[16,256]{1,0:T(8,128)S(1)} collective-permute-done((f32[16,256]{1,0:T(8,128)S(1)}, f32[16,256]{1,0:T(8,128)S(1)}, u32[]{:S(2)}, u32[]{:S(2)}) %collective-permute-start.9) | collective-permute-done | bytes 16416 | tf_op jit(solution)/shard_map/ppermute | solution.py:554
  65.1 0.7 collective-permute-start.10
  65.8 3.1 %collective-permute-done.10 = f32[16,256]{1,0:T(8,128)S(1)} collective-permute-done((f32[16,256]{1,0:T(8,128)S(1)}, f32[16,256]{1,0:T(8,128)S(1)}, u32[]{:S(2)}, u32[]{:S(2)}) %collective-permute-start.10) | collective-permute-done | bytes 16416 | tf_op jit(solution)/shard_map/ppermute | solution.py:554
  68.9 2.0 %collective-permute-start.11 = (f32[16,256]{1,0:T(8,128)S(1)}, f32[16,256]{1,0:T(8,128)S(1)}, u32[]{:S(2)}, u32[]{:S(2)}) collective-permute-start(f32[16,256]{1,0:T(8,128)S(1)} %add.40), channel_id=1, source_target_pairs={{0,16},{2,18},{4,20},{6,22},{8,24},{10,26},{12,28},{14,30},{16,0},... | collective-permute-start | bytes 49160 | tf_op jit(solution)/shard_map/ppermute | solution.py:554
  70.9 2.6 %collective-permute-done.11 = f32[16,256]{1,0:T(8,128)S(1)} collective-permute-done((f32[16,256]{1,0:T(8,128)S(1)}, f32[16,256]{1,0:T(8,128)S(1)}, u32[]{:S(2)}, u32[]{:S(2)}) %collective-permute-start.11) | collective-permute-done | bytes 16416 | tf_op jit(solution)/shard_map/ppermute | solution.py:554
  73.5 1.2 %standardize.1 = (f32[5,10,4,10]{3,2,1,0:T(4,128)}, f32[5,4,10]{2,1,0:T(4,128)}) custom-call(f32[16,256]{1,0:T(8,128)S(1)} %add.41.total), custom_call_target="tpu_custom_call" | custom-call | tf_op jit(solution)/shard_map/standardize/pallas_call | solution.py:674
  (27 shorter events, 0.2 us)
Async XLA Ops:
  0.6 0.8 %copy-start.2 = (s32[1024,8]{0,1:T(8,128)S(1)}, s32[1024,8]{0,1:T(8,128)}, u32[]{:S(2)}) copy-start(s32[1024,8]{0,1:T(8,128)} %param.8) | copy-start | bytes 98308
  0.7 0.8 %copy-start.3 = (f32[1024,8]{0,1:T(8,128)S(1)}, f32[1024,8]{0,1:T(8,128)}, u32[]{:S(2)}) copy-start(f32[1024,8]{0,1:T(8,128)} %param.7) | copy-start | bytes 98308
  1.5 1.2 %copy-start = (bf16[1024,500]{0,1:T(8,128)(2,1)S(1)}, bf16[1024,500]{0,1:T(8,128)(2,1)}, u32[]{:S(2)}) copy-start(bf16[1024,500]{0,1:T(8,128)(2,1)} %param.6) | copy-start | bytes 3072004
  4.0 1.7 %collective-permute-start = (f32[2,280,128]{2,1,0:T(8,128)S(1)}, f32[2,280,128]{2,1,0:T(8,128)S(1)}, u32[]{:S(2)}, u32[]{:S(2)}) collective-permute-start(f32[2,280,128]{2,1,0:T(8,128)S(1)} %select_bitcast_fusion), channel_id=1, source_target_pairs={{0,2},{2,0},{4,6},{6,4},{8,10},{10,8},{12,14},{14,12},{16,18},{18,... | collective-permute-start | bytes 860168 | tf_op jit(solution)/shard_map/ppermute | solution.py:554
  5.8 7.0 %collective-permute-start.1 = (f32[280,128]{1,0:T(8,128)S(1)}, f32[280,128]{1,0:T(8,128)S(1)}, u32[]{:S(2)}, u32[]{:S(2)}) collective-permute-start(f32[280,128]{1,0:T(8,128)S(1)} %select_bitcast_fusion.1), channel_id=1, source_target_pairs={{0,4},{2,6},{4,0},{6,2},{8,12},{10,14},{12,8},{14,10},{16,20},{18,... | collective-permute-start | bytes 430088 | tf_op jit(solution)/shard_map/ppermute | solution.py:554
  12.8 5.4 %collective-permute-start.2 = (f32[280,128]{1,0:T(8,128)S(1)}, f32[280,128]{1,0:T(8,128)S(1)}, u32[]{:S(2)}, u32[]{:S(2)}) collective-permute-start(f32[280,128]{1,0:T(8,128)S(1)} %bitcast_add_fusion.1), channel_id=1, source_target_pairs={{0,8},{2,10},{4,12},{6,14},{8,0},{10,2},{12,4},{14,6},{16,24},{18,... | collective-permute-start | bytes 430088 | tf_op jit(solution)/shard_map/ppermute | solution.py:554
  18.2 8.6 %copy-start.4 = (f32[3]{0:T(128)S(1)}, f32[3]{0:T(128)}, u32[]{:S(2)}) copy-start(f32[3]{0:T(128)} %constant.42.clone) | copy-start | bytes 40
  18.2 8.6 %copy-start.5 = (f32[3]{0:T(128)S(1)}, f32[3]{0:T(128)}, u32[]{:S(2)}) copy-start(f32[3]{0:T(128)} %constant.41.clone) | copy-start | bytes 40
  18.2 8.4 %collective-permute-start.3 = (f32[280,128]{1,0:T(8,128)S(1)}, f32[280,128]{1,0:T(8,128)S(1)}, u32[]{:S(2)}, u32[]{:S(2)}) collective-permute-start(f32[280,128]{1,0:T(8,128)S(1)} %add.36), channel_id=1, source_target_pairs={{0,16},{2,18},{4,20},{6,22},{8,24},{10,26},{12,28},{14,30},{16,0},... | collective-permute-start | bytes 430088 | tf_op jit(solution)/shard_map/ppermute | solution.py:554
  26.7 1.4 %collective-permute-start.4 = (f32[280,128]{1,0:T(8,128)S(1)}, f32[280,128]{1,0:T(8,128)S(1)}, u32[]{:S(2)}, u32[]{:S(2)}) collective-permute-start(f32[280,128]{1,0:T(8,128)S(1)} %add.37), channel_id=1, source_target_pairs={{0,2},{2,0},{4,6},{6,4},{8,10},{10,8},{12,14},{14,12},{16,18},{18,... | collective-permute-start | bytes 430088 | tf_op jit(solution)/shard_map/ppermute | solution.py:554
  28.2 10.2 %collective-permute-start.5 = (f32[560,128]{1,0:T(8,128)S(1)}, f32[560,128]{1,0:T(8,128)S(1)}, u32[]{:S(2)}, u32[]{:S(2)}) collective-permute-start(f32[560,128]{1,0:T(8,128)S(1)} %pad_maximum_fusion.mine), channel_id=1, source_target_pairs={{0,4},{2,6},{4,0},{6,2},{8,12},{10,14},{12,8},{14,10},{16,20},{18,... | collective-permute-start | bytes 860168 | tf_op jit(solution)/shard_map/ppermute | solution.py:554
  51.5 1.3 %collective-permute-start.6 = (f32[3,8,512]{2,1,0:T(8,128)S(1)}, f32[3,8,512]{2,1,0:T(8,128)S(1)}, u32[]{:S(2)}, u32[]{:S(2)}) collective-permute-start(f32[3,8,512]{2,1,0:T(8,128)S(1)} %get-tuple-element.18.mine), channel_id=1, source_target_pairs={{0,2},{2,0},{4,6},{6,4},{8,10},{10,8},{12,14},{14,12},{16,18},{18,... | collective-permute-start | bytes 147464 | tf_op jit(solution)/shard_map/ppermute | solution.py:554
  53.7 5.0 %copy-start.1 = (s32[1024]{0:T(1024)S(1)}, s32[1024]{0:T(1024)}, u32[]{:S(2)}) copy-start(s32[1024]{0:T(1024)} %param.9) | copy-start | bytes 12292
  53.7 4.9 %collective-permute-start.7 = (f32[24,1024]{1,0:T(8,128)S(1)}, f32[24,1024]{1,0:T(8,128)S(1)}, u32[]{:S(2)}, u32[]{:S(2)}) collective-permute-start(f32[24,1024]{1,0:T(8,128)S(1)} %get-tuple-element.26), channel_id=1, source_target_pairs={{0,1},{1,0},{2,3},{3,2},{4,5},{5,4},{6,7},{7,6},{8,9},{9,8},{10,11... | collective-permute-start | bytes 294920 | tf_op jit(solution)/shard_map/ppermute | solution.py:554
  60.1 1.2 %collective-permute-start.8 = (f32[16,256]{1,0:T(8,128)S(1)}, f32[16,256]{1,0:T(8,128)S(1)}, u32[]{:S(2)}, u32[]{:S(2)}) collective-permute-start(f32[16,256]{1,0:T(8,128)S(1)} %stacking.1), channel_id=1, source_target_pairs={{0,2},{2,0},{4,6},{6,4},{8,10},{10,8},{12,14},{14,12},{16,18},{18,... | collective-permute-start | bytes 49160 | tf_op jit(solution)/shard_map/ppermute | solution.py:554
  61.4 3.7 %collective-permute-start.9 = (f32[16,256]{1,0:T(8,128)S(1)}, f32[16,256]{1,0:T(8,128)S(1)}, u32[]{:S(2)}, u32[]{:S(2)}) collective-permute-start(f32[16,256]{1,0:T(8,128)S(1)} %add.38), channel_id=1, source_target_pairs={{0,4},{2,6},{4,0},{6,2},{8,12},{10,14},{12,8},{14,10},{16,20},{18,... | collective-permute-start | bytes 49160 | tf_op jit(solution)/shard_map/ppermute | solution.py:554
  65.1 3.7 %collective-permute-start.10 = (f32[16,256]{1,0:T(8,128)S(1)}, f32[16,256]{1,0:T(8,128)S(1)}, u32[]{:S(2)}, u32[]{:S(2)}) collective-permute-start(f32[16,256]{1,0:T(8,128)S(1)} %add.39), channel_id=1, source_target_pairs={{0,8},{2,10},{4,12},{6,14},{8,0},{10,2},{12,4},{14,6},{16,24},{18,... | collective-permute-start | bytes 49160 | tf_op jit(solution)/shard_map/ppermute | solution.py:554
  68.9 4.6 %collective-permute-start.11 = (f32[16,256]{1,0:T(8,128)S(1)}, f32[16,256]{1,0:T(8,128)S(1)}, u32[]{:S(2)}, u32[]{:S(2)}) collective-permute-start(f32[16,256]{1,0:T(8,128)S(1)} %add.40), channel_id=1, source_target_pairs={{0,16},{2,18},{4,20},{6,22},{8,24},{10,26},{12,28},{14,30},{16,0},... | collective-permute-start | bytes 49160 | tf_op jit(solution)/shard_map/ppermute | solution.py:554
